TPU v7x, 32 devices: a whole 2x2x4 slice. The times are simulated.
32 devices in a mesh: dp: 8 (over z, y), tensor: 4 (over x, core).
Axes of the slice: x: 2, y: 2, z: 4, core: 2. Of those that a mesh axis runs over, the one named last changes fastest.
Arguments:
- tokens: bfloat16 [50176, 384], P(('dp', 'tensor')), may hold values from -6 to 6
- cotangent: bfloat16 [50176, 384], P(('dp', 'tensor')), may hold values from -6 to 6
- image_size: int32 [64, 2], P('dp'), may hold values from 15 to 28
- vectors: bfloat16 [2, 2304], P(None, ('dp', 'tensor')), may hold values from -1.5 to 1.6
- mix_weight: bfloat16 [2, 384, 3, 384], P(None, None, None, 'tensor'), may hold values from -0.3125 to 0.3125
- mix_bias: bfloat16 [2, 2, 384], P(None, None, 'tensor'), may hold values from -3 to 3
- bias_table: bfloat16 [2, 169, 12], P(None, None, 'tensor'), may hold values from -4 to 4
- out_weight: bfloat16 [2, 384, 384], P(None, 'tensor'), may hold values from -1.75 to 1.75
- up_weight: bfloat16 [2, 384, 1536], P(None, None, ('dp', 'tensor')), may hold values from -0.3125 to 0.3125
- up_bias: bfloat16 [2, 1536], P(None, ('dp', 'tensor')), may hold values from -3 to 3
- down_weight: bfloat16 [2, 1536, 384], P(None, ('dp', 'tensor')), may hold values from -0.21875 to 0.21875
Outputs:
- output: bfloat16 [50176, 384], P(('dp', 'tensor'))
- image_mean: float32 [64, 384], P(('dp', 'tensor'))
- tokens_grad: float32 [50176, 384], P(('dp', 'tensor'))
- vectors_grad: float32 [2, 2304], P(None, ('dp', 'tensor'))
- mix_weight_grad: float32 [2, 384, 3, 384], P(None, None, None, 'tensor')
- mix_bias_grad: float32 [2, 2, 384], P(None, None, 'tensor')
- bias_table_grad: float32 [2, 169, 12], P(None, None, 'tensor')
- out_weight_grad: float32 [2, 384, 384], P(None, 'tensor')
- up_weight_grad: float32 [2, 384, 1536], P(None, None, ('dp', 'tensor'))
- up_bias_grad: float32 [2, 1536], P(None, ('dp', 'tensor'))
- down_weight_grad: float32 [2, 1536, 384], P(None, ('dp', 'tensor'))
Inputs may be any that keep to these rules, and one draw needn't show every extreme that they name: `image_size`: each padded image is 28 patches on a side.
All inputs are finite; a program needn't handle non-finite values.
Results may differ from a plain program's by a relative error of at most 0.022.
Values may be sent and summed in bfloat16 or wider, within the bound.
No kernel may reach another device: no remote copies, remote signals or barrier semaphores. Data moves between devices by JAX's collectives and lax.ppermute only.
A program may use at most 256 MiB of HBM per device.

v0:
```python
import jax
import jax.numpy as jnp
from jax import lax
from jax.sharding import PartitionSpec as P

HDIM = 32
WIN = 7
SHIFT = 3
GRID = 4
LAYERS = 2


highest = lax.Precision.HIGHEST
norm_eps = 1e-05
neg_fill = -10000.0


def to_image(token_rows, images):
    extent = GRID * WIN
    cell_grid = token_rows.reshape(images, GRID, GRID, WIN, WIN, -1).transpose(0, 1, 3, 2, 4, 5)
    return cell_grid.reshape(images, extent, extent, -1)


def to_tokens(cell_grid):
    images = cell_grid.shape[0]
    grid_parts = cell_grid.reshape(images, GRID, WIN, GRID, WIN, -1).transpose(0, 1, 3, 2, 4, 5)
    return grid_parts.reshape(images * GRID * GRID * WIN * WIN, -1)


def roll_tokens(token_rows, offset):
    images = token_rows.shape[0] // (GRID * GRID * WIN * WIN)
    return to_tokens(jnp.roll(to_image(token_rows, images), (offset, offset), axis=(1, 2)))


def inside_flags(image_size):
    places = jnp.arange(GRID * WIN, dtype=jnp.int32)
    inside = (places[None, :, None] < image_size[:, 0, None, None]) & (
        places[None, None, :] < image_size[:, 1, None, None]
    )
    return inside.astype(jnp.int32)[..., None]


def window_bias(image_size, shifted):
    extent = GRID * WIN
    places = jnp.arange(extent, dtype=jnp.int32)
    inside = inside_flags(image_size)
    if shifted:
        inside = jnp.roll(inside, (-SHIFT, -SHIFT), axis=(1, 2))
        band_of = (places >= extent - WIN).astype(jnp.int32) + (places >= extent - SHIFT).astype(
            jnp.int32
        )
        region = band_of[:, None] * 3 + band_of[None, :]
    else:
        region = jnp.zeros((extent, extent), jnp.int32)
    region = jnp.broadcast_to(region[None, :, :, None], inside.shape)
    key_ok = to_tokens(inside).reshape(-1, WIN * WIN)
    labels = to_tokens(region).reshape(-1, WIN * WIN)
    allowed = (key_ok[:, None, :] == 1) & (labels[:, :, None] == labels[:, None, :])
    return jnp.where(allowed, 0.0, neg_fill).astype(jnp.float32)


def relative_index():
    cells_all = jnp.arange(WIN * WIN, dtype=jnp.int32)
    rows_of = cells_all // WIN
    cols_of = cells_all % WIN
    return (rows_of[:, None] - rows_of[None, :] + WIN - 1) * (2 * WIN - 1) + (
        cols_of[:, None] - cols_of[None, :] + WIN - 1
    )


def relative_onehot(table_count):
    return (
        relative_index().reshape(-1)[:, None] == jnp.arange(table_count, dtype=jnp.int32)[None, :]
    ).astype(jnp.float32)


def relative_bias(table_rows):
    head_count = table_rows.shape[1]
    looked = jnp.dot(
        relative_onehot(table_rows.shape[0]), table_rows.astype(jnp.float32), precision=highest
    )
    return looked.T.reshape(head_count, WIN * WIN, WIN * WIN)


def layer_norm(entries, gain_row, bias_row):
    centre = entries - jnp.mean(entries, axis=-1, keepdims=True)
    spread = jnp.mean(centre * centre, axis=-1, keepdims=True)
    return centre * lax.rsqrt(spread + norm_eps) * gain_row + bias_row


def gelu_slope(inner_pre):
    return (
        0.5 * (1.0 + lax.erf(inner_pre * 0.7071067811865476))
        + inner_pre * jnp.exp(-0.5 * inner_pre * inner_pre) * 0.3989422804014327
    )


def split_windows(token_rows):
    return token_rows.reshape(-1, WIN * WIN, token_rows.shape[1] // HDIM, HDIM)


def gather_dense(vectors, up_weight, up_bias, down_weight):
    return (
        lax.all_gather(vectors, ("dp", "tensor"), axis=1, tiled=True),
        lax.all_gather(up_weight, ("dp", "tensor"), axis=2, tiled=True),
        lax.all_gather(up_bias, ("dp", "tensor"), axis=1, tiled=True),
        lax.all_gather(down_weight, ("dp", "tensor"), axis=1, tiled=True),
    )


def layer_forward(stream, layer_at, dense_set, attn_set, group_size):
    shifted = layer_at % 2 == 1
    vectors_all, up_all, up_bias_all, down_all = dense_set
    mix_all, mix_biases, table_all, out_all = attn_set
    rows_all = vectors_all[layer_at].astype(jnp.float32).reshape(6, -1)
    normed = layer_norm(stream, rows_all[0], rows_all[2]).astype(jnp.bfloat16)
    weight_mix = mix_all[layer_at]
    piece_rows = lax.all_gather(normed, "tensor", axis=0, tiled=True)
    mixed_rows = jnp.einsum(
        "td,dce->tce", piece_rows, weight_mix, preferred_element_type=jnp.float32
    )
    bias_pair = mix_biases[layer_at].astype(jnp.float32)
    stacked = jnp.concatenate(
        [mixed_rows[:, 0] + bias_pair[0], mixed_rows[:, 1], mixed_rows[:, 2] + bias_pair[1]], axis=1
    ).astype(jnp.bfloat16)
    if shifted:
        stacked = roll_tokens(stacked, -SHIFT)
    head_width = weight_mix.shape[2]
    queries = split_windows(stacked[:, :head_width])
    key_rows = split_windows(stacked[:, head_width : 2 * head_width])
    values = split_windows(stacked[:, 2 * head_width :])
    scores = (
        HDIM ** (-0.5)
        * jnp.einsum("wqhe,wkhe->whqk", queries, key_rows, preferred_element_type=jnp.float32)
        + relative_bias(table_all[layer_at])[None]
        + window_bias(group_size, shifted)[:, None]
    )
    soft_weights = jax.nn.softmax(scores, axis=-1)
    attended = jnp.einsum(
        "whqk,wkhe->wqhe",
        soft_weights.astype(jnp.bfloat16),
        values,
        preferred_element_type=jnp.float32,
    )
    attended = attended.reshape(-1, head_width).astype(jnp.bfloat16)
    unrolled = roll_tokens(attended, SHIFT) if shifted else attended
    weight_out = out_all[layer_at]
    branch = lax.psum_scatter(
        jnp.dot(unrolled, weight_out, preferred_element_type=jnp.float32).astype(jnp.bfloat16),
        "tensor",
        scatter_dimension=0,
        tiled=True,
    ).astype(jnp.float32)
    hidden_in = stream + (branch + rows_all[4])
    normed_two = layer_norm(hidden_in, rows_all[1], rows_all[3]).astype(jnp.bfloat16)
    inner_pre = jnp.dot(
        normed_two, up_all[layer_at], preferred_element_type=jnp.float32
    ) + up_bias_all[layer_at].astype(jnp.float32)
    activated = jax.nn.gelu(inner_pre, approximate=False).astype(jnp.bfloat16)
    output = hidden_in + (
        jnp.dot(activated, down_all[layer_at], preferred_element_type=jnp.float32) + rows_all[5]
    )
    return (
        output,
        (piece_rows, stacked, soft_weights, unrolled, hidden_in, normed_two, inner_pre, activated),
    )


def layer_backward(grad_stream, stream, layer_at, dense_set, attn_set, kept_values):
    shifted = layer_at % 2 == 1
    gathered, stacked, soft_weights, unrolled, hidden_in, normed_two, inner_pre, activated = (
        kept_values
    )
    vectors_all, up_all, up_bias_all, down_all = dense_set
    mix_all, mix_biases, table_all, out_all = attn_set
    rows_all = vectors_all[layer_at].astype(jnp.float32).reshape(6, -1)
    grad_branch = grad_stream.astype(jnp.bfloat16)
    down_grad = jnp.einsum("tf,td->fd", activated, grad_branch, preferred_element_type=jnp.float32)
    down_bias_grad = jnp.sum(grad_branch.astype(jnp.float32), axis=0)
    grad_activated = jnp.einsum(
        "td,fd->tf", grad_branch, down_all[layer_at], preferred_element_type=jnp.float32
    )
    grad_inner = (grad_activated * gelu_slope(inner_pre)).astype(jnp.bfloat16)
    up_grad = jnp.einsum("td,tf->df", normed_two, grad_inner, preferred_element_type=jnp.float32)
    up_bias_grad = jnp.sum(grad_inner.astype(jnp.float32), axis=0)
    grad_normed_two = jnp.einsum(
        "tf,df->td", grad_inner, up_all[layer_at], preferred_element_type=jnp.float32
    )
    unused, norm_back = jax.vjp(layer_norm, hidden_in, rows_all[1], rows_all[3])
    grad_part, gain_two_grad, bias_two_grad = norm_back(grad_normed_two)
    grad_hidden = grad_stream + grad_part
    grad_attn = grad_hidden.astype(jnp.bfloat16)
    out_bias_grad = jnp.sum(grad_attn.astype(jnp.float32), axis=0)
    weight_out = out_all[layer_at]
    head_width = weight_out.shape[0]
    piece_rows = lax.all_gather(grad_attn, "tensor", axis=0, tiled=True)
    grad_cols = jnp.einsum("td,ed->te", piece_rows, weight_out, preferred_element_type=jnp.float32)
    weight_acc = jnp.einsum("te,td->ed", unrolled, piece_rows, preferred_element_type=jnp.float32)
    grad_unrolled = grad_cols
    if shifted:
        grad_unrolled = roll_tokens(grad_unrolled, -SHIFT)
    grad_attended = split_windows(grad_unrolled.astype(jnp.bfloat16))
    queries = split_windows(stacked[:, :head_width])
    key_rows = split_windows(stacked[:, head_width : 2 * head_width])
    values = split_windows(stacked[:, 2 * head_width :])
    grad_soft = jnp.einsum(
        "wqhe,wkhe->whqk", grad_attended, values, preferred_element_type=jnp.float32
    )
    grad_scores = (
        soft_weights * (grad_soft - jnp.sum(grad_soft * soft_weights, axis=-1, keepdims=True))
    ).astype(jnp.bfloat16)
    grad_values = jnp.einsum(
        "whqk,wqhe->wkhe",
        soft_weights.astype(jnp.bfloat16),
        grad_attended,
        preferred_element_type=jnp.float32,
    ).astype(jnp.bfloat16)
    grad_queries = (
        HDIM ** (-0.5)
        * jnp.einsum("whqk,wkhe->wqhe", grad_scores, key_rows, preferred_element_type=jnp.float32)
    ).astype(jnp.bfloat16)
    grad_keys = (
        HDIM ** (-0.5)
        * jnp.einsum("whqk,wqhe->wkhe", grad_scores, queries, preferred_element_type=jnp.float32)
    ).astype(jnp.bfloat16)
    table_rows = table_all[layer_at]
    score_sums = jnp.sum(grad_scores.astype(jnp.float32), axis=0)
    table_grad = jnp.einsum(
        "pr,hp->rh",
        relative_onehot(table_rows.shape[0]),
        score_sums.reshape(score_sums.shape[0], -1),
        precision=highest,
    )
    grad_stacked = jnp.concatenate(
        [
            grad_queries.reshape(-1, head_width),
            grad_keys.reshape(-1, head_width),
            grad_values.reshape(-1, head_width),
        ],
        axis=1,
    )
    if shifted:
        grad_stacked = roll_tokens(grad_stacked, SHIFT)
    grad_mix = grad_stacked.reshape(-1, 3, head_width)
    column_sums = jnp.sum(grad_mix.astype(jnp.float32), axis=0)
    mix_bias_grad = jnp.stack([column_sums[0], column_sums[2]])
    mix_grad = jnp.einsum("td,tce->dce", gathered, grad_mix, preferred_element_type=jnp.float32)
    weight_mix = mix_all[layer_at]
    grad_normed = lax.psum_scatter(
        jnp.einsum("tce,dce->td", grad_mix, weight_mix, preferred_element_type=jnp.float32).astype(
            jnp.bfloat16
        ),
        "tensor",
        scatter_dimension=0,
        tiled=True,
    ).astype(jnp.float32)
    unused, norm_back_one = jax.vjp(layer_norm, stream, rows_all[0], rows_all[2])
    grad_first, gain_one_grad, bias_one_grad = norm_back_one(grad_normed)
    vector_grad = jnp.concatenate(
        [gain_one_grad, gain_two_grad, bias_one_grad, bias_two_grad, out_bias_grad, down_bias_grad]
    )
    return (
        grad_hidden + grad_first,
        (vector_grad, up_grad, up_bias_grad, down_grad),
        (mix_grad, mix_bias_grad, table_grad, weight_acc),
    )


def masked_mean(stream, own_size):
    images = own_size.shape[0]
    inside_rows = to_tokens(inside_flags(own_size)).reshape(images, -1).astype(jnp.float32)
    totals = jnp.einsum(
        "ip,ipd->id",
        inside_rows,
        stream.reshape(images, inside_rows.shape[1], -1),
        precision=highest,
    )
    return totals / jnp.sum(inside_rows, axis=1, keepdims=True)


def body(
    tokens,
    cotangent,
    image_size,
    vectors,
    mix_weight,
    mix_bias,
    bias_table,
    out_weight,
    up_weight,
    up_bias,
    down_weight,
):
    local_images = tokens.shape[0] // (GRID * GRID * WIN * WIN)
    own_size = lax.dynamic_slice_in_dim(
        image_size, lax.axis_index("tensor") * local_images, local_images, 0
    )
    attn_set = (mix_weight, mix_bias, bias_table, out_weight)
    dense_set = gather_dense(vectors, up_weight, up_bias, down_weight)
    stream = tokens.astype(jnp.float32)
    layer_inputs = []
    for layer_at in range(LAYERS):
        layer_inputs.append(stream)
        stream, unused = layer_forward(stream, layer_at, dense_set, attn_set, image_size)
    image_mean = masked_mean(stream, own_size)
    dense_set = gather_dense(vectors, up_weight, up_bias, down_weight)
    grad_stream = cotangent.astype(jnp.float32)
    dense_parts = [None] * LAYERS
    attn_parts = [None] * LAYERS
    for layer_at in reversed(range(LAYERS)):
        unused, kept_values = layer_forward(
            layer_inputs[layer_at], layer_at, dense_set, attn_set, image_size
        )
        grad_stream, dense_parts[layer_at], attn_parts[layer_at] = layer_backward(
            grad_stream, layer_inputs[layer_at], layer_at, dense_set, attn_set, kept_values
        )
    dense_grads = [
        jnp.stack([dense_parts[layer_at][member] for layer_at in range(LAYERS)])
        for member in range(4)
    ]
    attn_stack = [
        jnp.stack([attn_parts[layer_at][member] for layer_at in range(LAYERS)])
        for member in range(4)
    ]
    vectors_grad, up_weight_grad, up_bias_grad, down_weight_grad = (
        lax.psum_scatter(dense_grads[0], ("dp", "tensor"), scatter_dimension=1, tiled=True),
        lax.psum_scatter(dense_grads[1], ("dp", "tensor"), scatter_dimension=2, tiled=True),
        lax.psum_scatter(dense_grads[2], ("dp", "tensor"), scatter_dimension=1, tiled=True),
        lax.psum_scatter(dense_grads[3], ("dp", "tensor"), scatter_dimension=1, tiled=True),
    )
    mix_weight_grad, mix_bias_grad, bias_table_grad, out_weight_grad = lax.psum(
        (attn_stack[0], attn_stack[1], attn_stack[2], attn_stack[3]), "dp"
    )
    return (
        stream.astype(jnp.bfloat16),
        image_mean,
        grad_stream,
        vectors_grad,
        mix_weight_grad,
        mix_bias_grad,
        bias_table_grad,
        out_weight_grad,
        up_weight_grad,
        up_bias_grad,
        down_weight_grad,
    )


def solution(mesh):
    placed = (
        P(("dp", "tensor"), None),
        P(("dp", "tensor"), None),
        P("dp", None),
        P(None, ("dp", "tensor")),
        P(None, None, None, "tensor"),
        P(None, None, "tensor"),
        P(None, None, "tensor"),
        P(None, "tensor", None),
        P(None, None, ("dp", "tensor")),
        P(None, ("dp", "tensor")),
        P(None, ("dp", "tensor"), None),
    )
    return jax.shard_map(
        body,
        mesh=mesh,
        in_specs=placed,
        out_specs=(
            P(("dp", "tensor"), None),
            P(("dp", "tensor"), None),
            P(("dp", "tensor"), None),
            P(None, ("dp", "tensor")),
            P(None, None, None, "tensor"),
            P(None, None, "tensor"),
            P(None, None, "tensor"),
            P(None, "tensor", None),
            P(None, None, ("dp", "tensor")),
            P(None, ("dp", "tensor")),
            P(None, ("dp", "tensor"), None),
        ),
        check_vma=False,
    )
```

profile of v0, /device:TPU:0, one launch (start us, length us, event | category | flops | bytes accessed | tf_op | source)
XLA Modules:
  0.0 1418.4 jit_solution(5666168176968727142)
XLA Ops:
  11.8 43.3 %all-gather = bf16[32,72,2]{1,2,0:T(2,128)(2,1)S(1)} all-gather(bf16[1,72,2]{1,2,0:T(2,128)(2,1)} %bitcast.326), channel_id=1, replica_groups=mesh['dp'=8,'tensor'=4] {'dp','tensor'}, dimensions={0}, use_global_device_ids=true | all-gather | bytes 9504 | tf_op jit(solution)/shard_map/all_gather | solution.py:104
  59.6 32.1 %all-gather.9.cloned.1.call-done = bf16[6272,384]{1,0:T(8,128)(2,1)} async-done(((bf16[1568,384]{1,0:T(8,128)(2,1)}), bf16[6272,384]{1,0:T(8,128)(2,1)}) %all-gather.9.cloned.1.call-update) | async-done | bytes 4816912 | tf_op jit(solution)/shard_map/all_gather | solution.py:118
  128.5 13.8 fusion.82
  142.2 12.0 fusion.184
  175.7 40.4 %all-gather.1 = bf16[32,48,2]{1,2,0:T(2,128)(2,1)S(1)} all-gather(bf16[1,48,2]{1,2,0:T(2,128)(2,1)S(1)} %bitcast.327), channel_id=1, replica_groups=mesh['dp'=8,'tensor'=4] {'dp','tensor'}, dimensions={0}, use_global_device_ids=true | all-gather | bytes 6336 | tf_op jit(solution)/shard_map/all_gather | solution.py:106
  226.8 25.1 %all-gather.11.cloned.1.call-done = bf16[2,384,1536]{1,2,0:T(8,128)(2,1)} async-done(((bf16[2,384,48]{1,2,0:T(8,128)(2,1)}), bf16[2,384,1536]{1,2,0:T(8,128)(2,1)}) %all-gather.11.cloned.1.call-update) | async-done | bytes 2359312 | tf_op jit(solution)/shard_map/all_gather | solution.py:105
  251.9 26.3 %fusion.6 = (bf16[1568,1536]{1,0:T(8,128)(2,1)}, f32[1568,1536]{1,0:T(8,128)}) fusion(f32[1536]{0:T(1024)S(1)} %get-tuple-element.82, bf16[2,384,1536]{1,2,0:T(8,128)(2,1)} %all-gather.11.cloned.1.call-done, f32[384]{0:T(512)S(1)} %get-tuple-element.161, f32[384]{0:T(512)S(1)} %get-tuple-element.160, f32[1568]{0:T(1024)S(1)} %fusion.156, ...), kind=kOutput, calls=%fused_computation.24 | convolution fusion | flops 2014064640 | bytes 18062080 | tf_op jit(solution)/shard_map/dot_general | solution.py:156
  278.1 33.1 %all-gather.13.cloned.1.call-done = bf16[2,1536,384]{2,1,0:T(8,128)(2,1)} async-done(((bf16[2,48,384]{2,1,0:T(8,128)(2,1)}), bf16[2,1536,384]{2,1,0:T(8,128)(2,1)}) %all-gather.13.cloned.1.call-update) | async-done | bytes 2359312 | tf_op jit(solution)/shard_map/all_gather | solution.py:107
  327.9 29.7 %all-gather.15.cloned.1.call-done = bf16[6272,384]{1,0:T(8,128)(2,1)} async-done(((bf16[1568,384]{1,0:T(8,128)(2,1)}), bf16[6272,384]{1,0:T(8,128)(2,1)}) %all-gather.15.cloned.1.call-update) | async-done | bytes 4816912 | tf_op jit(solution)/shard_map/all_gather | solution.py:118
  448.3 13.0 fusion.72
  461.2 15.1 %fusion.186 = (f32[128,3,49]{2,1,0:T(4,128)S(1)}, f32[128,3,49,49]{2,3,1,0:T(8,128)}) fusion(f32[128,3,49,49]{2,3,1,0:T(8,128)} %fusion.72, f32[128,49,49]{1,2,0:T(8,128)S(1)} %copy-done.34, f32[3,49,49]{1,2,0:T(8,128)S(1)} %copy.174), kind=kOutput, calls=%fused_computation.373 | output fusion | flops 7375920 | bytes 8709260 | tf_op jit(solution)/shard_map/sub | solution.py:138
  512.3 48.6 %reduce-scatter.12.cloned.1.call-done = bf16[1568,384]{1,0:T(8,128)(2,1)} async-done(((bf16[6272,384]{1,0:T(8,128)(2,1)}), bf16[1568,384]{1,0:T(8,128)(2,1)}) %reduce-scatter.12.cloned.1.call-update) | async-done | bytes 1204240 | tf_op jit(solution)/shard_map/reduce_scatter | solution.py:148
  563.5 24.3 %fusion.9 = (bf16[1568,1536]{1,0:T(8,128)(2,1)}, f32[1568,1536]{1,0:T(8,128)S(1)}) fusion(f32[1536]{0:T(1024)S(1)} %copy-done.83, bf16[2,384,1536]{1,2,0:T(8,128)(2,1)S(1)} %copy-done.100, f32[1568,384]{1,0:T(8,128)S(1)} %get-tuple-element.102, f32[384]{0:T(512)S(1)} %copy-done.95, f32[384]{0:T(512)S(1)} %copy-done.84, f32[1568]{0:T(1024)S(1)} %fusion.158, ...), kind=kOutput, calls=%fused_computation.27 | convolution fusion | flops 2011656192 | bytes 18067456 | tf_op jit(solution)/shard_map/dot_general | solution.py:156
  601.7 38.1 %all-gather.17.cloned.1.call-done = bf16[6272,384]{1,0:T(8,128)(2,1)} async-done(((bf16[1568,384]{1,0:T(8,128)(2,1)}), bf16[6272,384]{1,0:T(8,128)(2,1)}) %all-gather.17.cloned.1.call-update) | async-done | bytes 4816912 | tf_op jit(solution)/shard_map/all_gather | solution.py:196
  680.1 13.7 multiply_reduce_fusion.1
  801.4 15.2 %reshape_reshape.4 = bf16[6272,3,96]{2,1,0:T(4,128)(2,1)} reshape(bf16[8,4,4,7,7,288]{5,4,3,2,1,0:T(8,128)(2,1)} %copy.196) | data formatting | bytes 7225344 | tf_op jit(solution)/shard_map/reshape;reshape | solution.py:244
  834.5 48.6 %reduce-scatter.14.cloned.1.call-done = bf16[1568,384]{1,0:T(8,128)(2,1)} async-done(((bf16[6272,384]{1,0:T(8,128)(2,1)}), bf16[1568,384]{1,0:T(8,128)(2,1)}) %reduce-scatter.14.cloned.1.call-update) | async-done | bytes 1204240 | tf_op jit(solution)/shard_map/reduce_scatter | solution.py:249
  931.1 13.2 all-gather.19.cloned.1.call-done
  968.4 17.0 %multiply_reduce_fusion = (f32[128,3,49]{2,1,0:T(4,128)S(1)}, f32[128,3,49,49]{2,3,1,0:T(8,128)}) fusion(f32[128,3,49,49]{2,3,1,0:T(8,128)} %copy-done.22, f32[128,3,49]{2,1,0:T(4,128)S(1)} %copy-done.51, bf16[128,49,3,32]{1,0,3,2:T(8,128)(2,1)S(1)} %copy-done.37, bf16[128,49,3,32]{1,0,3,2:T(8,128)(2,1)} %reshape.662), kind=kOutput, calls=%fused_computation.9 | convolution fusion | flops 61754112 | bytes 9934848 | tf_op jit(solution)/shard_map/wqhe,wkhe->whqk/dot_general | solution.py:206
  1088.3 72.1 %all-reduce.7.cloned.1.call-done = f32[2,384,1536]{1,0,2:T(2,128)} async-done(((f32[2,384,1536]{1,0,2:T(2,128)}), f32[2,384,1536]{1,0,2:T(2,128)}) %all-reduce.7.cloned.1.call-update) | async-done | bytes 4718608
  1165.8 35.5 %all-reduce.2 = (f32[2,2,96]{2,1,0:T(2,128)}, f32[2,169,3]{1,2,0:T(4,128)S(1)}) all-reduce(f32[2,2,96]{2,1,0:T(2,128)S(1)} %pad_maximum_fusion.13, f32[2,169,3]{1,2,0:T(4,128)S(1)} %pad_maximum_fusion.12), channel_id=1, replica_groups=mesh['dp'=8,'tensor'=4] {'dp'}, use_global_device_ids=true, to_apply=%region_43.44 | all-reduce | flops 1398 | bytes 11184 | tf_op jit(solution)/shard_map/psum | solution.py:331
  1215.4 38.0 %all-reduce = f32[2,2304]{1,0:T(2,128)S(1)} all-reduce(f32[2,2304]{1,0:T(2,128)S(1)} %pad_maximum_fusion.10), channel_id=6, replica_groups=mesh['dp'=8,'tensor'=4] {'dp','tensor'}, use_global_device_ids=true, to_apply=%region_39.40.clone | all-reduce | flops 4608 | bytes 36864
  1259.4 64.7 %reduce-scatter.18.cloned.1.call-done = f32[2,48,384]{2,1,0:T(8,128)} async-done(((f32[2,1536,384]{2,1,0:T(8,128)}), f32[2,48,384]{2,1,0:T(8,128)}) %reduce-scatter.18.cloned.1.call-update) | async-done | bytes 147472 | tf_op jit(solution)/shard_map/reduce_scatter | solution.py:329
  1324.1 82.8 %all-reduce.9.cloned.1.call-done = (f32[2,384,3,96]{1,3,2,0:T(8,128)}, f32[2,96,384]{2,1,0:T(8,128)}) async-done(((f32[2,384,3,96]{1,3,2,0:T(8,128)}, f32[2,96,384]{2,1,0:T(8,128)}), (f32[2,384,3,96]{1,3,2,0:T(8,128)}, f32[2,96,384]{2,1,0:T(8,128)})) %all-reduce.9.cloned.1.call-update) | async-done | bytes 1179664 | tf_op jit(solution)/shard_map/psum | solution.py:331
  (477 shorter events, 605.0 us)
Async XLA Ops:
  8.0 83.7 %all-gather.9.cloned.1.call-start = ((), (), s32[]{:S(2)}) async-start(), calls=%async_computation.6 | async-start | bytes 6021120 | tf_op jit(solution)/shard_map/all_gather | solution.py:118
  55.9 196.0 %copy-start.80 = (f32[384]{0:T(512)}, f32[384]{0:T(512)S(1)}, u32[]{:S(2)}) copy-start(f32[384]{0:T(512)S(1)} %get-tuple-element.160) | copy-start | bytes 4612
  55.9 196.0 %copy-start.93 = (f32[384]{0:T(512)}, f32[384]{0:T(512)S(1)}, u32[]{:S(2)}) copy-start(f32[384]{0:T(512)S(1)} %get-tuple-element.161) | copy-start | bytes 4612
  55.9 255.4 %copy-start.72 = (f32[384]{0:T(512)}, f32[384]{0:T(512)S(1)}, u32[]{:S(2)}) copy-start(f32[384]{0:T(512)S(1)} %get-tuple-element.159) | copy-start | bytes 4612
  55.9 262.6 %copy-start.68 = (f32[384]{0:T(512)}, f32[384]{0:T(512)S(1)}, u32[]{:S(2)}) copy-start(f32[384]{0:T(512)S(1)} %get-tuple-element.74) | copy-start | bytes 4612
  57.5 166.0 %reduce-scatter.10.cloned.1.call-start = ((), (), s32[]{:S(2)}) async-start(), calls=%async_computation.7 | async-start | bytes 6021120 | tf_op jit(solution)/shard_map/reduce_scatter | solution.py:148
  57.8 263.1 %copy-start.77 = (s32[2401]{0:T(1024)}, s32[2401]{0:T(1024)S(1)}, u32[]{:S(2)}) copy-start(s32[2401]{0:T(1024)S(1)} %add.500) | copy-start | bytes 28816
  174.5 77.4 %all-gather.11.cloned.1.call-start = ((), (), s32[]{:S(2)}) async-start(), calls=%async_computation.8 | async-start | bytes 2433024 | tf_op jit(solution)/shard_map/all_gather | solution.py:105
  175.1 136.2 %all-gather.13.cloned.1.call-start = ((), (), s32[]{:S(2)}) async-start(), calls=%async_computation.9 | async-start | bytes 2433024 | tf_op jit(solution)/shard_map/all_gather | solution.py:107
  175.7 181.9 %all-gather.15.cloned.1.call-start = ((), (), s32[]{:S(2)}) async-start(), calls=%async_computation.10 | async-start | bytes 6021120 | tf_op jit(solution)/shard_map/all_gather | solution.py:118
  225.3 52.8 %copy-start.58 = (f32[1568]{0:T(1024)}, f32[1568]{0:T(1024)S(1)}, u32[]{:S(2)}) copy-start(f32[1568]{0:T(1024)S(1)} %broadcast_multiply_fusion.2) | copy-start | bytes 18820
  226.8 51.3 %copy-start.70 = (f32[1568]{0:T(1024)}, f32[1568]{0:T(1024)S(1)}, u32[]{:S(2)}) copy-start(f32[1568]{0:T(1024)S(1)} %fusion.156) | copy-start | bytes 18820
  320.6 240.4 %reduce-scatter.12.cloned.1.call-start = ((), (), s32[]{:S(2)}) async-start(), calls=%async_computation.11 | async-start | bytes 6021120 | tf_op jit(solution)/shard_map/reduce_scatter | solution.py:148
  512.3 127.6 %all-gather.17.cloned.1.call-start = ((), (), s32[]{:S(2)}) async-start(), calls=%async_computation.12 | async-start | bytes 6021120 | tf_op jit(solution)/shard_map/all_gather | solution.py:196
  601.7 281.3 %reduce-scatter.14.cloned.1.call-start = ((), (), s32[]{:S(2)}) async-start(), calls=%async_computation.13 | async-start | bytes 6021120 | tf_op jit(solution)/shard_map/reduce_scatter | solution.py:249
  834.4 51.0 %copy-start.57 = (f32[1568]{0:T(1024)S(1)}, f32[1568]{0:T(1024)}, u32[]{:S(2)}) copy-start(f32[1568]{0:T(1024)} %copy-done.56) | copy-start | bytes 18820
  834.4 110.0 %all-gather.19.cloned.1.call-start = ((), (), s32[]{:S(2)}) async-start(), calls=%async_computation.14 | async-start | bytes 6021120 | tf_op jit(solution)/shard_map/all_gather | solution.py:196
  906.2 180.6 %reduce-scatter.20.cloned.1.call-start = ((), (), s32[]{:S(2)}) async-start(), calls=%async_computation.17 | async-start | bytes 811008
  914.5 245.8 %all-reduce.7.cloned.1.call-start = ((), (), s32[]{:S(2)}) async-start(), calls=%async_computation.18 | async-start | bytes 9437184
  931.1 280.6 %reduce-scatter.16.cloned.1.call-start = ((), (), s32[]{:S(2)}) async-start(), calls=%async_computation.15 | async-start | bytes 6021120 | tf_op jit(solution)/shard_map/reduce_scatter | solution.py:249
  1049.5 274.5 %reduce-scatter.18.cloned.1.call-start = ((), (), s32[]{:S(2)}) async-start(), calls=%async_computation.16 | async-start | bytes 4866048 | tf_op jit(solution)/shard_map/reduce_scatter | solution.py:329
  1063.3 343.6 %all-reduce.9.cloned.1.call-start = ((), (), s32[]{:S(2)}) async-start(), calls=%async_computation.19 | async-start | bytes 2359296 | tf_op jit(solution)/shard_map/psum | solution.py:331
  1086.6 79.1 %copy-start.87 = (f32[1,169,3]{1,2,0:T(4,128)S(1)}, f32[1,169,3]{1,2,0:T(4,128)}, u32[]{:S(2)}) copy-start(f32[1,169,3]{1,2,0:T(4,128)} %fusion.141) | copy-start | bytes 6088
  1086.6 115.2 %copy-start.20 = (bf16[6272,96]{0,1:T(8,128)(2,1)S(1)}, bf16[6272,96]{0,1:T(8,128)(2,1)}, u32[]{:S(2)}) copy-start(bf16[6272,96]{0,1:T(8,128)(2,1)} %copy-done.19) | copy-start | bytes 3612676
  (94 other events, 1222.6 us)
Sparse Core Ops, SparseCore 0:
  57.6 34.0 all-gather.8
  174.6 48.7 reduce-scatter.9
  320.7 36.8 all-gather.14
  512.4 48.4 reduce-scatter.11
  601.8 38.0 all-gather.16
  834.5 48.4 reduce-scatter.13
  906.3 38.0 all-gather.18
Sparse Core Ops, SparseCore 1:
  177.9 73.9 all-gather.10
  255.1 56.1 all-gather.12
  914.6 95.5 reduce-scatter.19
  1016.9 143.4 all-reduce.6
  1162.9 47.2 reduce-scatter.15
  1217.1 106.9 reduce-scatter.17
  1328.0 78.8 all-reduce.8
where the time goes:
time: 1430 us; the launch traced here: 1420 us
  waiting for transfers between devices  496 us (35%)
  local copies, waits for them, and re-layouts  327 us (23%)
  matrix products  297 us (21%)
  blocking collectives  157 us (11%)
  other arithmetic  123 us (9%)
  between operations  17.8 us (1%)
    psum x1, waiting for transfers between devices, body(): lax.psum((attn_stack[0], attn_stack[1], attn_stack[2], attn_stack[3]), 'dp')  82.8 us
    unnamed x16, waiting for transfers between devices  73.4 us
    reshape x7, local copies, waits for them, and re-layouts, split_windows(): return token_rows.reshape(-1, WIN * WIN, token_rows.shape[1] // HDIM, HDIM)  69.3 us
    reduce_scatter x1, waiting for transfers between devices, body(): lax.psum_scatter(dense_grads[3], ('dp', 'tensor'), scatter_dimension=1, t...  64.7 us
    all_gather x2, waiting for transfers between devices, layer_forward(): piece_rows = lax.all_gather(normed, 'tensor', axis=0, tiled=True)  61.8 us
    reduce_scatter x2, waiting for transfers between devices, layer_forward(): lax.psum_scatter(jnp.dot(unrolled, weight_out, preferred_element_type=jnp...  55.2 us
    concatenate x7, local copies, waits for them, and re-layouts, layer_backward(): jnp.concatenate([grad_queries.reshape(-1, head_width), grad_keys.reshape(...  51.4 us
    all_gather x2, waiting for transfers between devices, layer_backward(): piece_rows = lax.all_gather(grad_attn, 'tensor', axis=0, tiled=True)  51.3 us
  transfers between devices with their start and end apart: 14, of which 12 were waited for; matrix products, arithmetic and copies ran while one was open for 16% of the time, Pallas kernels for 0%

commit v1 on v0

v1 whole, which is shorter than its diff:
```python
import jax
import jax.numpy as jnp
import numpy as np
from jax import lax
from jax.experimental import pallas as pl
from jax.experimental.pallas import tpu as pltpu
from jax.sharding import PartitionSpec as P

D = 384
HEADS = 12
HDIM = 32
FF = 1536
WIN = 7
SHIFT = 3
GRID = 4
LAYERS = 2
SIDE = GRID * WIN
CELLS = WIN * WIN
WINDOWS = GRID * GRID
IMG_ROWS = WINDOWS * CELLS
PAD = 64
PAD_ROWS = WINDOWS * PAD
PAIRS = WINDOWS // 2
TABLE = (2 * WIN - 1) ** 2
TILES = D // 128
norm_eps = 1e-05
neg_fill = -10000.0
never = -1e30
bf16 = jnp.bfloat16
f32 = jnp.float32
VMEM_LIMIT = 56 * 1024 * 1024


def nn(a, b):
    return lax.dot_general(a, b, (((1,), (0,)), ((), ())), preferred_element_type=f32)


def nt(a, b):
    return lax.dot_general(a, b, (((1,), (1,)), ((), ())), preferred_element_type=f32)


def tn(a, b):
    return lax.dot_general(a, b, (((0,), (0,)), ((), ())), preferred_element_type=f32)


def padded_source(shifted):
    source = np.full((PAD_ROWS,), -1, np.int32)
    for a in range(GRID):
        for b in range(GRID):
            for p in range(WIN):
                for c in range(WIN):
                    row, col = a * WIN + p, b * WIN + c
                    if shifted:
                        row, col = (row + SHIFT) % SIDE, (col + SHIFT) % SIDE
                    here = (a * GRID + b) * PAD + p * WIN + c
                    source[here] = ((row // WIN) * GRID + col // WIN) * CELLS + (row % WIN) * WIN + col % WIN
    return source


def token_places():
    rows = np.zeros((IMG_ROWS,), np.int32)
    cols = np.zeros((IMG_ROWS,), np.int32)
    for a in range(GRID):
        for b in range(GRID):
            for p in range(WIN):
                for c in range(WIN):
                    at = (a * GRID + b) * CELLS + p * WIN + c
                    rows[at], cols[at] = a * WIN + p, b * WIN + c
    return rows, cols


def padded_labels(shifted):
    labels = np.zeros((PAD_ROWS,), np.int32)
    if shifted:
        band = lambda at: int(at >= SIDE - WIN) + int(at >= SIDE - SHIFT)
        for a in range(GRID):
            for b in range(GRID):
                for p in range(WIN):
                    for c in range(WIN):
                        here = (a * GRID + b) * PAD + p * WIN + c
                        labels[here] = 3 * band(a * WIN + p) + band(b * WIN + c)
    return labels


def relative_rows():
    index = np.full((PAD, PAD), TABLE, np.int32)
    for j in range(CELLS):
        for i in range(CELLS):
            index[j, i] = (i // WIN - j // WIN + WIN - 1) * (2 * WIN - 1) + (i % WIN - j % WIN + WIN - 1)
    return index


def normalize(rows):
    centre = rows - jnp.mean(rows, axis=-1, keepdims=True)
    spread = jnp.mean(centre * centre, axis=-1, keepdims=True)
    scale = lax.rsqrt(spread + norm_eps)
    return centre * scale, scale


def normalize_back(grad, gain, unit, scale):
    grad_unit = grad * gain
    first = jnp.mean(grad_unit, axis=-1, keepdims=True)
    second = jnp.mean(grad_unit * unit, axis=-1, keepdims=True)
    return scale * (grad_unit - first - unit * second)


def column_sum(rows):
    return jnp.sum(rows, axis=0, keepdims=True)


def head_masks():
    lane = lax.broadcasted_iota(jnp.int32, (1, 128), 1)
    return [jnp.where(lane // HDIM == h, 1.0, 0.0).astype(bf16) for h in range(4)]


def spread_heads(tile, masks):
    return jnp.concatenate([tile * mask for mask in masks], axis=0)


def stack_heads(tile):
    return jnp.concatenate([tile[:, 128 * h : 128 * (h + 1)] for h in range(4)], axis=0)


def attn_fwd_kernel(x_ref, perm_ref, vec_ref, w_ref, mixb_ref, bias_ref, mask_ref, h_ref, a1_ref, qkv_ref, p_ref, ou_ref, o_ref):
    x = x_ref[...].astype(f32)
    unit, _ = normalize(x)
    a1 = (unit * vec_ref[0:1, :] + vec_ref[2:3, :]).astype(bf16)
    a1p = nn(perm_ref[...], a1).astype(bf16)
    a1_ref[...] = a1p
    qkv_ref[:, 0:D] = (nt(a1p, w_ref[0]) + mixb_ref[0:1, :]).astype(bf16)
    qkv_ref[:, D : 2 * D] = nt(a1p, w_ref[1]).astype(bf16)
    qkv_ref[:, 2 * D : 3 * D] = (nt(a1p, w_ref[2]) + mixb_ref[1:2, :]).astype(bf16)
    masks = head_masks()

    def one_pair(pair, carry):
        rows = pl.ds(pl.multiple_of(pair * 128, 128), 128)
        mask = mask_ref[0, pair]
        mask4 = jnp.concatenate([mask] * 4, axis=1)
        for g in range(TILES):
            q = qkv_ref[rows, 128 * g : 128 * (g + 1)]
            k = qkv_ref[rows, D + 128 * g : D + 128 * (g + 1)]
            v = qkv_ref[rows, 2 * D + 128 * g : 2 * D + 128 * (g + 1)]
            s = (HDIM**-0.5) * nt(k, spread_heads(q, masks)) + bias_ref[g] + mask4
            e = jnp.exp(s - jnp.max(s, axis=0, keepdims=True))
            p = (e * (1.0 / jnp.sum(e, axis=0, keepdims=True))).astype(bf16)
            p_ref[0, pair, g] = p
            o = tn(stack_heads(p), spread_heads(v, masks))
            o_ref[rows, 128 * g : 128 * (g + 1)] = o.astype(bf16)
        return carry

    lax.fori_loop(0, PAIRS, one_pair, 0)
    ou = tn(perm_ref[...], o_ref[...]).astype(bf16)
    ou_ref[...] = ou
    h_ref[...] = x + (nn(ou, w_ref[3]) + vec_ref[4:5, :])


def attn_bwd_kernel(gh_ref, x_ref, perm_ref, vec_ref, w_ref, a1_ref, qkv_ref, p_ref, ou_ref, g_ref, lo_ref, hi_ref, ds_ref, vg_ref, wacc_ref, do_ref, dm_ref):
    image = pl.program_id(0)
    last = image == pl.num_programs(0) - 1

    @pl.when(image == 0)
    def _():
        wacc_ref[...] = jnp.zeros_like(wacc_ref)
        ds_ref[...] = jnp.zeros_like(ds_ref)
        vg_ref[...] = jnp.zeros_like(vg_ref)

    go = gh_ref[...].astype(bf16)
    vg_ref[2:3, :] += column_sum(go.astype(f32))
    wacc_ref[3] += tn(ou_ref[...], go)
    do_ref[...] = nn(perm_ref[...], nt(go, w_ref[3]).astype(bf16)).astype(bf16)
    masks = head_masks()

    def one_pair(pair, carry):
        rows = pl.ds(pl.multiple_of(pair * 128, 128), 128)
        for g in range(TILES):
            q = qkv_ref[rows, 128 * g : 128 * (g + 1)]
            k = qkv_ref[rows, D + 128 * g : D + 128 * (g + 1)]
            v = qkv_ref[rows, 2 * D + 128 * g : 2 * D + 128 * (g + 1)]
            do4 = spread_heads(do_ref[rows, 128 * g : 128 * (g + 1)], masks)
            pb = p_ref[0, pair, g]
            p = pb.astype(f32)
            dp = nt(v, do4)
            ds = p * (dp - jnp.sum(p * dp, axis=0, keepdims=True))
            dsb = ds.astype(bf16)
            ds_ref[g] += dsb.astype(f32)
            dv = nn(pb, do4)
            dk = (HDIM**-0.5) * nn(dsb, spread_heads(q, masks))
            dq = (HDIM**-0.5) * tn(stack_heads(dsb), spread_heads(k, masks))
            dm_ref[rows, 128 * g : 128 * (g + 1)] = dq.astype(bf16)
            dm_ref[rows, D + 128 * g : D + 128 * (g + 1)] = dk.astype(bf16)
            dm_ref[rows, 2 * D + 128 * g : 2 * D + 128 * (g + 1)] = dv.astype(bf16)
        return carry

    lax.fori_loop(0, PAIRS, one_pair, 0)
    a1p = a1_ref[...]
    da = jnp.zeros((PAD_ROWS, D), f32)
    for c in range(3):
        dm = dm_ref[:, D * c : D * (c + 1)]
        wacc_ref[c] += tn(dm, a1p)
        da += nn(dm, w_ref[c])
        if c != 1:
            vg_ref[3 + c // 2 : 4 + c // 2, :] += column_sum(dm.astype(f32))
    da1 = tn(perm_ref[...], da.astype(bf16))
    unit, scale = normalize(x_ref[...].astype(f32))
    vg_ref[0:1, :] += column_sum(da1 * unit)
    vg_ref[1:2, :] += column_sum(da1)
    g_ref[...] = gh_ref[...] + normalize_back(da1, vec_ref[0:1, :], unit, scale)

    @pl.when(last)
    def _():
        lo_ref[...] = wacc_ref[:, : D // 2, :].astype(bf16)
        hi_ref[...] = wacc_ref[:, D // 2 :, :].astype(bf16)


def gelu_parts(z):
    cdf = 0.5 * (1.0 + lax.erf(z * 0.7071067811865476))
    slope = cdf + z * (jnp.exp(-0.5 * z * z) * 0.3989422804014327)
    return (z * cdf).astype(bf16), slope


CHUNK = 768


def ffn_fwd_kernel(h_ref, vec_ref, w_ref, ub_ref, x_ref):
    h = h_ref[...]
    unit, _ = normalize(h)
    a2 = (unit * vec_ref[1:2, :] + vec_ref[3:4, :]).astype(bf16)
    out = h + vec_ref[5:6, :]
    for at in range(0, FF, CHUNK):
        z = nt(a2, w_ref[0, at : at + CHUNK, :]) + ub_ref[0:1, at : at + CHUNK]
        m = (z * (0.5 * (1.0 + lax.erf(z * 0.7071067811865476)))).astype(bf16)
        out += nn(m, w_ref[1, at : at + CHUNK, :])
    x_ref[...] = out


def ffn_both_kernel(with_output, *refs):
    if with_output:
        h_ref, g_ref, vec_ref, w_ref, ub_ref, in_ref, gh_ref, lo_ref, hi_ref, vg_ref, ug_ref, x_ref, mean_ref, wacc_ref = refs
    else:
        h_ref, g_ref, vec_ref, w_ref, ub_ref, gh_ref, lo_ref, hi_ref, vg_ref, ug_ref, wacc_ref = refs
    image = pl.program_id(0)
    last = image == pl.num_programs(0) - 1

    @pl.when(image == 0)
    def _():
        wacc_ref[...] = jnp.zeros_like(wacc_ref)
        vg_ref[...] = jnp.zeros_like(vg_ref)
        ug_ref[...] = jnp.zeros_like(ug_ref)

    h = h_ref[...]
    unit, scale = normalize(h)
    a2 = (unit * vec_ref[1:2, :] + vec_ref[3:4, :]).astype(bf16)
    g = g_ref[...].astype(f32)
    gm = g.astype(bf16)
    vg_ref[2:3, :] += column_sum(gm.astype(f32))
    if with_output:
        out = h + vec_ref[5:6, :]
    da = jnp.zeros((IMG_ROWS, D), f32)
    for at in range(0, FF, CHUNK):
        up = w_ref[0, at : at + CHUNK, :]
        down = w_ref[1, at : at + CHUNK, :]
        z = nt(a2, up) + ub_ref[0:1, at : at + CHUNK]
        m, slope = gelu_parts(z)
        if with_output:
            out += nn(m, down)
        dz = (nt(gm, down) * slope).astype(bf16)
        ug_ref[0:1, at : at + CHUNK] += column_sum(dz.astype(f32))
        wacc_ref[0, at : at + CHUNK, :] += tn(dz, a2)
        wacc_ref[1, at : at + CHUNK, :] += tn(m, gm)
        da += nn(dz, up)
    vg_ref[0:1, :] += column_sum(da * unit)
    vg_ref[1:2, :] += column_sum(da)
    gh_ref[...] = g + normalize_back(da, vec_ref[1:2, :], unit, scale)
    if with_output:
        x_ref[...] = out.astype(bf16)
        flags = in_ref[...]
        mean_ref[0] = column_sum(out * flags) / jnp.sum(flags)

    @pl.when(last)
    def _():
        lo_ref[...] = wacc_ref[:, : FF // 2, :].astype(bf16)
        hi_ref[...] = wacc_ref[:, FF // 2 :, :].astype(bf16)


def whole(*shape):
    return pl.BlockSpec(shape, lambda i: (0,) * len(shape))


def by_image(*shape):
    return pl.BlockSpec(shape, lambda i: (i,) + (0,) * (len(shape) - 1))


def shape_of(shape, kind):
    return jax.ShapeDtypeStruct(shape, kind)


def call(kernel, name, images, ins, outs, scratch, flops, moved):
    return pl.pallas_call(
        kernel,
        name=name,
        grid=(images,),
        in_specs=ins,
        out_specs=[spec for spec, _ in outs],
        out_shape=[shape for _, shape in outs],
        scratch_shapes=scratch,
        compiler_params=pltpu.CompilerParams(vmem_limit_bytes=VMEM_LIMIT, dimension_semantics=("arbitrary",)),
        cost_estimate=pl.CostEstimate(flops=int(flops), bytes_accessed=int(moved), transcendentals=0),
    )


def attn_forward(x, perm, vec, weights, mix_bias, bias4, mask):
    images = x.shape[0] // IMG_ROWS
    rows = images * IMG_ROWS
    padded = images * PAD_ROWS
    return call(
        attn_fwd_kernel,
        "attn_fwd",
        images,
        [
            by_image(IMG_ROWS, D),
            whole(PAD_ROWS, IMG_ROWS),
            whole(8, D),
            whole(4, D, D),
            whole(8, D),
            whole(TILES, 128, 512),
            by_image(1, PAIRS, 128, 128),
        ],
        [
            (by_image(IMG_ROWS, D), shape_of((rows, D), f32)),
            (by_image(PAD_ROWS, D), shape_of((padded, D), bf16)),
            (by_image(PAD_ROWS, 3 * D), shape_of((padded, 3 * D), bf16)),
            (by_image(1, PAIRS, TILES, 128, 512), shape_of((images, PAIRS, TILES, 128, 512), bf16)),
            (by_image(IMG_ROWS, D), shape_of((rows, D), bf16)),
        ],
        [pltpu.VMEM((PAD_ROWS, D), bf16)],
        2e10,
        2e7,
    )(x, perm, vec, weights, mix_bias, bias4, mask)


def attn_backward(gh, x, perm, vec, weights, kept):
    a1p, qkv, p, ou = kept
    images = x.shape[0] // IMG_ROWS
    rows = images * IMG_ROWS
    return call(
        attn_bwd_kernel,
        "attn_bwd",
        images,
        [
            by_image(IMG_ROWS, D),
            by_image(IMG_ROWS, D),
            whole(PAD_ROWS, IMG_ROWS),
            whole(8, D),
            whole(4, D, D),
            by_image(PAD_ROWS, D),
            by_image(PAD_ROWS, 3 * D),
            by_image(1, PAIRS, TILES, 128, 512),
            by_image(IMG_ROWS, D),
        ],
        [
            (by_image(IMG_ROWS, D), shape_of((rows, D), f32)),
            (whole(4, D // 2, D), shape_of((4, D // 2, D), bf16)),
            (whole(4, D // 2, D), shape_of((4, D // 2, D), bf16)),
            (whole(TILES, 128, 512), shape_of((TILES, 128, 512), f32)),
            (whole(8, D), shape_of((8, D), f32)),
        ],
        [pltpu.VMEM((4, D, D), f32), pltpu.VMEM((PAD_ROWS, D), bf16), pltpu.VMEM((PAD_ROWS, 3 * D), bf16)],
        3e10,
        2e7,
    )(gh, x, perm, vec, weights, a1p, qkv, p, ou)


def ffn_forward(h, vec, weights, up_bias):
    images = h.shape[0] // IMG_ROWS
    return call(
        ffn_fwd_kernel,
        "ffn_fwd",
        images,
        [by_image(IMG_ROWS, D), whole(8, D), whole(2, FF, D), whole(8, FF)],
        [(by_image(IMG_ROWS, D), shape_of(h.shape, f32))],
        [],
        1e10,
        1e7,
    )(h, vec, weights, up_bias)[0]


def ffn_both(h, g, vec, weights, up_bias, flags=None):
    images = h.shape[0] // IMG_ROWS
    rows = images * IMG_ROWS
    with_output = flags is not None
    ins = [by_image(IMG_ROWS, D), by_image(IMG_ROWS, D), whole(8, D), whole(2, FF, D), whole(8, FF)]
    outs = [
        (by_image(IMG_ROWS, D), shape_of((rows, D), f32)),
        (whole(2, FF // 2, D), shape_of((2, FF // 2, D), bf16)),
        (whole(2, FF // 2, D), shape_of((2, FF // 2, D), bf16)),
        (whole(8, D), shape_of((8, D), f32)),
        (whole(8, FF), shape_of((8, FF), f32)),
    ]
    args = [h, g, vec, weights, up_bias]
    if with_output:
        ins.append(by_image(IMG_ROWS, 1))
        args.append(flags)
        outs.append((by_image(IMG_ROWS, D), shape_of((rows, D), bf16)))
        outs.append((by_image(1, 1, D), shape_of((images, 1, D), f32)))
    return call(
        lambda *refs: ffn_both_kernel(with_output, *refs),
        "ffn_both_out" if with_output else "ffn_both",
        images,
        ins,
        outs,
        [pltpu.VMEM((2, FF, D), f32)],
        2e10,
        2e7,
    )(*args)


def expanded_bias(tables):
    layers = tables.shape[0]
    onehot = jnp.asarray(relative_rows().reshape(1, -1)) == jnp.arange(TABLE, dtype=jnp.int32)[:, None]
    looked = nn(tables.reshape(layers * HEADS, TABLE).astype(bf16), onehot.astype(bf16))
    looked = looked.reshape(layers, TILES, 4, PAD, PAD).transpose(0, 1, 3, 2, 4)
    key_real = (jnp.arange(PAD) < CELLS)[:, None, None]
    looked = jnp.where(key_real, looked, never)
    other = jnp.full_like(looked, never)
    first = jnp.stack([looked, other], axis=4)
    second = jnp.stack([other, looked], axis=4)
    return jnp.concatenate([first, second], axis=2).reshape(layers, TILES, 128, 512)


def folded_bias(sums):
    both = sums.reshape(TILES, 2, PAD, 4, 2, PAD)
    one = both[:, 0, :, :, 0, :] + both[:, 1, :, :, 1, :]
    flat = one.transpose(0, 2, 1, 3).reshape(HEADS, PAD * PAD)
    onehot = jnp.asarray(relative_rows().reshape(-1, 1)) == jnp.arange(TABLE, dtype=jnp.int32)[None, :]
    onehot = onehot.astype(bf16)
    high = flat.astype(bf16)
    low = (flat - high.astype(f32)).astype(bf16)
    return nn(high, onehot) + nn(low, onehot)


def key_masks(own_size, shifted):
    source = padded_source(shifted)
    rows_of, cols_of = token_places()
    key_row = jnp.asarray(np.where(source < 0, SIDE, rows_of[source]))
    key_col = jnp.asarray(np.where(source < 0, SIDE, cols_of[source]))
    inside = (key_row[None] < own_size[:, 0:1]) & (key_col[None] < own_size[:, 1:2])
    inside = inside.reshape(-1, PAIRS, 128, 1)
    labels = jnp.asarray(padded_labels(shifted).reshape(PAIRS, 128))
    same = labels[None, :, :, None] == labels[None, :, None, :]
    return jnp.where(inside & same, 0.0, neg_fill).astype(f32)


def inside_column(own_size):
    rows_of, cols_of = token_places()
    inside = (jnp.asarray(rows_of)[None] < own_size[:, 0:1]) & (jnp.asarray(cols_of)[None] < own_size[:, 1:2])
    return inside.astype(f32).reshape(-1, 1)


def move_matrix(shifted):
    source = jnp.asarray(padded_source(shifted))
    return (source[:, None] == jnp.arange(IMG_ROWS, dtype=jnp.int32)[None, :]).astype(bf16)


def swap(rows, axis, bit, size):
    return lax.ppermute(rows, axis, [(i, i ^ bit) for i in range(size)])


def bits_of(axis, size):
    bit = size // 2
    stages = []
    while bit:
        stages.append((axis, bit, size))
        bit //= 2
    return stages


def spread_out(rows, stages, axis):
    for stage in stages:
        rows = jnp.concatenate([rows, swap(rows, *stage)], axis=axis)
    return rows


def fold_in(lo, hi, stages, axis):
    kept = None
    for at, stage in enumerate(reversed(stages)):
        got = swap(hi, *stage)
        kept = lo.astype(f32) + got.astype(f32)
        if at + 1 < len(stages):
            half = kept.shape[axis] // 2
            lo = lax.slice_in_dim(kept, 0, half, axis=axis)
            hi = lax.slice_in_dim(kept, half, 2 * half, axis=axis).astype(bf16)
    return kept


def fold_small(rows, stages):
    for stage in reversed(stages):
        half = rows.shape[0] // 2
        rows = rows[:half] + swap(rows[half:], *stage)
    return rows


def sum_over(rows, stages):
    for stage in stages:
        rows = rows + swap(rows.astype(bf16), *stage).astype(f32)
    return rows


def exchange_order(count):
    bits = count.bit_length() - 1
    return np.array([int(format(p, "0" + str(max(bits, 1)) + "b")[::-1], 2) if bits else 0 for p in range(count)], np.int32)


def body(n_dp, n_tensor, tokens, cotangent, image_size, vectors, mix_weight, mix_bias, bias_table, out_weight, up_weight, up_bias, down_weight):
    local_images = tokens.shape[0] // IMG_ROWS
    devices = n_dp * n_tensor
    dp_stages = bits_of("dp", n_dp)
    tensor_stages = bits_of("tensor", n_tensor)
    stages = dp_stages + tensor_stages
    own = lax.axis_index("dp") * n_tensor + lax.axis_index("tensor")
    own_size = lax.dynamic_slice_in_dim(image_size, lax.axis_index("tensor") * local_images, local_images, 0)
    vec_own = vectors.shape[1]
    ub_own = up_bias.shape[1]
    own_heads = bias_table.shape[2]
    own_cols = own_heads * HDIM

    small = jnp.concatenate([vectors, up_bias], axis=1).reshape(1, -1)
    small = spread_out(small, stages, 0).reshape(devices, LAYERS, vec_own + ub_own)
    order = jnp.asarray(exchange_order(devices))
    place = ((jnp.arange(devices, dtype=jnp.int32) ^ own)[:, None] == order[None, :])
    vec_rel = small[:, :, :vec_own].reshape(devices, -1)
    vec_abs = nn(place.astype(bf16), vec_rel).reshape(devices, LAYERS, vec_own).transpose(1, 0, 2).reshape(LAYERS, 6, D)
    vec_rows = jnp.pad(vec_abs, ((0, 0), (0, 2), (0, 0)))
    ub_all = small[:, :, vec_own:].transpose(1, 0, 2).reshape(LAYERS, 1, FF).astype(f32)
    ub_rows = jnp.pad(ub_all, ((0, 0), (0, 7), (0, 0)))

    table_rows = bias_table.transpose(2, 0, 1).reshape(own_heads, -1)
    bias_rows = mix_bias.reshape(LAYERS, 2, own_heads, HDIM).transpose(2, 0, 1, 3).reshape(own_heads, -1)
    misc = spread_out(jnp.concatenate([table_rows, bias_rows], axis=1), tensor_stages, 0)
    tables = misc[:, : LAYERS * TABLE].reshape(HEADS, LAYERS, TABLE).transpose(1, 0, 2)
    mixb = misc[:, LAYERS * TABLE :].reshape(HEADS, LAYERS, 2, HDIM).transpose(1, 2, 0, 3).reshape(LAYERS, 2, D)
    mixb_rows = jnp.pad(mixb.astype(f32), ((0, 0), (0, 6), (0, 0)))

    mix_own = mix_weight.transpose(0, 2, 3, 1)
    attn_own = jnp.concatenate([mix_own, out_weight[:, None]], axis=1)
    dense_own = jnp.stack([up_weight.transpose(0, 2, 1), down_weight], axis=1)
    attn_w = [spread_out(attn_own[l], tensor_stages, 1) for l in range(LAYERS)]
    dense_w = [spread_out(dense_own[l], stages, 1) for l in range(LAYERS)]

    bias4 = expanded_bias(tables)
    perms = [move_matrix(l % 2 == 1) for l in range(LAYERS)]
    masks = [key_masks(own_size, l % 2 == 1) for l in range(LAYERS)]
    flags = inside_column(own_size)

    x = tokens
    xs, hs, kept = [], [], []
    for l in range(LAYERS):
        xs.append(x)
        h, *saved = attn_forward(x, perms[l], vec_rows[l], attn_w[l], mixb_rows[l], bias4[l], masks[l])
        hs.append(h)
        kept.append(saved)
        if l + 1 < LAYERS:
            x = ffn_forward(h, vec_rows[l], dense_w[l], ub_rows[l])

    g = cotangent
    dense_g, attn_g, table_g, vec_g, ub_g, mixb_g = ([None] * LAYERS for _ in range(6))
    for l in reversed(range(LAYERS)):
        if l + 1 == LAYERS:
            gh, lo, hi, vg, ug, output, image_mean = ffn_both(hs[l], g, vec_rows[l], dense_w[l], ub_rows[l], flags)
        else:
            gh, lo, hi, vg, ug = ffn_both(hs[l], g, vec_rows[l], dense_w[l], ub_rows[l])
        dense_g[l] = fold_in(lo, hi, stages, 1)
        g, lo, hi, ds, va = attn_backward(gh, xs[l], perms[l], vec_rows[l], attn_w[l], kept[l])
        attn_g[l] = sum_over(fold_in(lo, hi, tensor_stages, 1), dp_stages)
        table_g[l] = folded_bias(ds)
        vec_g[l] = jnp.stack([va[0], vg[0], va[1], vg[1], va[2], vg[2]]).reshape(-1)
        ub_g[l] = ug[0]
        mixb_g[l] = va[3:5]

    vec_all = jnp.stack(vec_g).reshape(LAYERS, devices, vec_own).transpose(1, 0, 2).reshape(devices, -1)
    vec_all = jnp.dot(place.astype(f32).T, vec_all, precision=lax.Precision.HIGHEST)
    ub_all = jnp.stack(ub_g).reshape(LAYERS, devices, ub_own).transpose(1, 0, 2).reshape(devices, -1)
    small_g = fold_small(jnp.concatenate([vec_all, ub_all], axis=1), stages)
    vectors_grad = small_g[0, : LAYERS * vec_own].reshape(LAYERS, vec_own)
    up_bias_grad = small_g[0, LAYERS * vec_own :].reshape(LAYERS, ub_own)

    table_all = jnp.stack(table_g, axis=1).reshape(HEADS, -1)
    mixb_all = jnp.stack(mixb_g).reshape(LAYERS, 2, HEADS, HDIM).transpose(2, 0, 1, 3).reshape(HEADS, -1)
    misc_g = fold_small(jnp.concatenate([table_all, mixb_all], axis=1), tensor_stages)
    for stage in dp_stages:
        misc_g = misc_g + swap(misc_g, *stage)
    bias_table_grad = misc_g[:, : LAYERS * TABLE].reshape(own_heads, LAYERS, TABLE).transpose(1, 2, 0)
    mix_bias_grad = misc_g[:, LAYERS * TABLE :].reshape(own_heads, LAYERS, 2, HDIM).transpose(1, 2, 0, 3).reshape(LAYERS, 2, own_cols)

    attn_all = jnp.stack(attn_g)
    dense_all = jnp.stack(dense_g)
    return (
        output,
        image_mean.reshape(local_images, D),
        g,
        vectors_grad,
        attn_all[:, :3].transpose(0, 3, 1, 2),
        mix_bias_grad,
        bias_table_grad,
        attn_all[:, 3],
        dense_all[:, 0].transpose(0, 2, 1),
        up_bias_grad,
        dense_all[:, 1],
    )


def solution(mesh):
    n_dp, n_tensor = mesh.shape["dp"], mesh.shape["tensor"]
    both = ("dp", "tensor")
    placed = (
        P(both, None),
        P(both, None),
        P("dp", None),
        P(None, both),
        P(None, None, None, "tensor"),
        P(None, None, "tensor"),
        P(None, None, "tensor"),
        P(None, "tensor", None),
        P(None, None, both),
        P(None, both),
        P(None, both, None),
    )
    return jax.shard_map(
        lambda *args: body(n_dp, n_tensor, *args),
        mesh=mesh,
        in_specs=placed,
        out_specs=(
            P(both, None),
            P(both, None),
            P(both, None),
            P(None, both),
            P(None, None, None, "tensor"),
            P(None, None, "tensor"),
            P(None, None, "tensor"),
            P(None, "tensor", None),
            P(None, None, both),
            P(None, both),
            P(None, both, None),
        ),
        check_vma=False,
    )
```

time: 1430 us -> 408 us (0.29)
  waiting for transfers between devices: 496 us -> 82.8 us
  matrix products: 297 us -> 4.58 us
  local copies, waits for them, and re-layouts: 327 us -> 43.1 us
  Pallas kernels: 0 us -> 193 us
  blocking collectives: 157 us -> 0 us
  other arithmetic: 123 us -> 31.2 us
  starting transfers between devices: 0.77 us -> 47.5 us
  between operations: 17.8 us -> 1.72 us
    dot_general x37 -> x7, matrix products: 279 us -> 4.58 us  [the longest x6 4.31 us: nn(): lax.dot_general(a, b, (((1,), (0,)), ((), ())), preferred_element_type=f32)]
    pallas_call x0 -> x7, Pallas kernels: none -> 193 us  [the longest x2 75.9 us: attn_backward(): call(attn_bwd_kernel, 'attn_bwd', images, [by_image(IMG_ROWS, D), by_imag...]
    all_gather x6 -> x0, waiting for transfers between devices: 171 us -> none  [the longest x2 61.8 us: layer_forward(): piece_rows = lax.all_gather(normed, 'tensor', axis=0, tiled=True)]
    reduce_scatter x5 -> x0, waiting for transfers between devices: 169 us -> none  [the longest x1 64.7 us: body(): lax.psum_scatter(dense_grads[3], ('dp', 'tensor'), scatter_dimension=1, t...]
    all_gather x2 -> x0, blocking collectives: 83.7 us -> none  [the longest x1 43.3 us: gather_dense(): lax.all_gather(vectors, ('dp', 'tensor'), axis=1, tiled=True)]
    psum x1 -> x0, waiting for transfers between devices: 82.8 us -> none  [body(): lax.psum((attn_stack[0], attn_stack[1], attn_stack[2], attn_stack[3]), 'dp')]
    ppermute x0 -> x51, waiting for transfers between devices: none -> 82.8 us  [swap(): return lax.ppermute(rows, axis, [(i, i ^ bit) for i in range(size)])]
    convert_element_type x14 -> x7, local copies, waits for them, and re-layouts: 84.3 us -> 1.6 us  [the longest x1 1.23 us: inside_column(): return inside.astype(f32).reshape(-1, 1)]
  transfers between devices with their start and end apart: 14 -> 51, of which waited for: 12 -> 25; matrix products, arithmetic and copies ran while one was open for 16% -> 17% of each run, Pallas kernels for 0% -> 18%
where the time goes in v1:
time: 408 us; the launch traced here: 404 us
  Pallas kernels  193 us (47%)
  waiting for transfers between devices  82.8 us (20%)
  starting transfers between devices  47.5 us (12%)
  local copies, waits for them, and re-layouts  43.1 us (11%)
  other arithmetic  31.2 us (8%)
  matrix products  4.58 us (1%)
    ppermute x51, waiting for transfers between devices, swap(): return lax.ppermute(rows, axis, [(i, i ^ bit) for i in range(size)])  82.8 us
    pallas_call x2, Pallas kernels, attn_backward(): call(attn_bwd_kernel, 'attn_bwd', images, [by_image(IMG_ROWS, D), by_imag...  75.9 us
    pallas_call x2, Pallas kernels, attn_forward(): call(attn_fwd_kernel, 'attn_fwd', images, [by_image(IMG_ROWS, D), whole(P...  63 us
    ppermute x51, starting transfers between devices, swap(): return lax.ppermute(rows, axis, [(i, i ^ bit) for i in range(size)])  47.5 us
    pallas_call x2, Pallas kernels, ffn_both(): call(lambda *refs: ffn_both_kernel(with_output, *refs), 'ffn_both_out' if...  45.1 us
    concatenate x15, other arithmetic, spread_out(): rows = jnp.concatenate([rows, swap(rows, *stage)], axis=axis)  12.2 us
    unnamed x72, local copies, waits for them, and re-layouts  9.7 us
    pallas_call x1, Pallas kernels, ffn_forward(): call(ffn_fwd_kernel, 'ffn_fwd', images, [by_image(IMG_ROWS, D), whole(8,...  9.16 us
  transfers between devices with their start and end apart: 51, of which 25 were waited for; matrix products, arithmetic and copies ran while one was open for 17% of the time, Pallas kernels for 18%

profile of v1, /device:TPU:0, one launch (start us, length us, event | category | flops | bytes accessed | tf_op | source)
XLA Modules:
  0.0 404.0 jit_solution(4200271012520995501)
XLA Ops:
  2.5 2.9 collective-permute-start.7
  6.2 2.6 collective-permute-start
  12.0 2.9 collective-permute-start.9
  32.6 3.0 collective-permute-done.3
  64.6 7.7 %collective-permute-done.11 = bf16[2,192,384]{2,1,0:T(8,128)(2,1)S(1)} collective-permute-done((bf16[2,192,384]{2,1,0:T(8,128)(2,1)S(1)}, bf16[2,192,384]{2,1,0:T(8,128)(2,1)S(1)}, u32[]{:S(2)}, u32[]{:S(2)}) %collective-permute-start.11) | collective-permute-done | bytes 294944 | tf_op jit(solution)/shard_map/ppermute | solution.py:465
  81.3 8.3 %collective-permute-done.12 = bf16[2,384,384]{2,1,0:T(8,128)(2,1)S(1)} collective-permute-done((bf16[2,384,384]{2,1,0:T(8,128)(2,1)S(1)}, bf16[2,384,384]{2,1,0:T(8,128)(2,1)S(1)}, u32[]{:S(2)}, u32[]{:S(2)}) %collective-permute-start.12) | collective-permute-done | bytes 589856 | tf_op jit(solution)/shard_map/ppermute | solution.py:465
  91.9 31.3 %attn_fwd.2 = (f32[1568,384]{1,0:T(8,128)}, bf16[2048,384]{1,0:T(8,128)(2,1)}, bf16[2048,1152]{1,0:T(8,128)(2,1)}, bf16[2,8,3,128,512]{4,3,2,1,0:T(8,128)(2,1)}, bf16[1568,384]{1,0:T(8,128)(2,1)}) custom-call(bf16[1568,384]{1,0:T(8,128)(2,1)} %x_ref.3, bf16[1024,784]{1,0:T(8,128)(2,1)} %fusion.3.perm_ref, f32[8,384]{1,0:T(8,128)} %get-tuple-element.114.vec_ref.refs_2_, ...), custom_call_target="tpu_custom_call" | custom-call | flops 20000000000 | bytes 20000000 | tf_op jit(solution)/shard_map/attn_fwd/pallas_call | solution.py:315
  127.9 9.2 %ffn_fwd.1.x_ref = f32[1568,384]{1,0:T(8,128)} custom-call(f32[1568,384]{1,0:T(8,128)} %get-tuple-element.43.h_ref.refs_0_, f32[8,384]{1,0:T(8,128)} %get-tuple-element.114.vec_ref.refs_2_, bf16[2,1536,384]{2,1,0:T(8,128)(2,1)} %constant_dynamic-update-slice_fusion.11.w_ref.refs_3_, f32[8,1536]{1,0:T(8,128)} %get-tuple-element.106.ub_ref.refs_4_), custom_call_target="tpu_custom_call" | custom-call | flops 10000000000 | bytes 10000000 | tf_op jit(solution)/shard_map/ffn_fwd/pallas_call | solution.py:375
  137.1 31.7 %attn_fwd.3 = (f32[1568,384]{1,0:T(8,128)}, bf16[2048,384]{1,0:T(8,128)(2,1)}, bf16[2048,1152]{1,0:T(8,128)(2,1)}, bf16[2,8,3,128,512]{4,3,2,1,0:T(8,128)(2,1)}, bf16[1568,384]{1,0:T(8,128)(2,1)}) custom-call(f32[1568,384]{1,0:T(8,128)} %ffn_fwd.1.x_ref, bf16[1024,784]{1,0:T(8,128)(2,1)} %fusion.4.perm_ref, f32[8,384]{1,0:T(8,128)} %get-tuple-element.113.vec_ref.refs_2_, ...), custom_call_target="tpu_custom_call" | custom-call | flops 20000000000 | bytes 20000000 | tf_op jit(solution)/shard_map/attn_fwd/pallas_call | solution.py:315
  169.9 23.7 %ffn_both_out.1 = (f32[1568,384]{1,0:T(8,128)}, bf16[2,768,384]{2,1,0:T(8,128)(2,1)}, bf16[2,768,384]{2,1,0:T(8,128)(2,1)}, f32[8,384]{1,0:T(8,128)}, f32[8,1536...) custom-call(f32[1568,384]{1,0:T(8,128)} %get-tuple-element.44.refs_0_, bf16[1568,384]{1,0:T(8,128)(2,1)} %refs_1_.1, ...), custom_call_target="tpu_custom_call" | custom-call | flops 20000000000 | bytes 20000000 | tf_op jit(solution)/shard_map/ffn_both_out/pallas_call | solution.py:405
  193.6 38.1 %attn_bwd.2 = (f32[1568,384]{1,0:T(8,128)}, bf16[4,192,384]{2,1,0:T(8,128)(2,1)}, bf16[4,192,384]{2,1,0:T(8,128)(2,1)}, f32[3,128,512]{2,1,0:T(8,128)}, f32[8,384]{1,0:T(8,128)}) custom-call(f32[1568,384]{1,0:T(8,128)} %get-tuple-element.47.gh_ref, f32[1568,384]{1,0:T(8,128)} %ffn_fwd.1.x_ref, bf16[1024,784]{1,0:T(8,128)(2,1)} %fusion.4.perm_ref, ...), custom_call_target="tpu_custom_call" | custom-call | flops 30000001024 | bytes 20000000 | tf_op jit(solution)/shard_map/attn_bwd/pallas_call | solution.py:345
  231.7 21.4 %ffn_both.1 = (f32[1568,384]{1,0:T(8,128)}, bf16[2,768,384]{2,1,0:T(8,128)(2,1)}, bf16[2,768,384]{2,1,0:T(8,128)(2,1)}, f32[8,384]{1,0:T(8,128)}, f32[8,1536]{1,0:T(8,128)}) custom-call(f32[1568,384]{1,0:T(8,128)} %get-tuple-element.43.h_ref.refs_0_, f32[1568,384]{1,0:T(8,128)} %get-tuple-element.52.refs_1_, f32[8,384]{1,0:T(8,128)} %get-tuple-element.114.vec_ref.refs_2_, ...), custom_call_target="tpu_custom_call" | custom-call | flops 20000000000 | bytes 20000000 | tf_op jit(solution)/shard_map/ffn_both/pallas_call | solution.py:405
  253.2 37.8 %attn_bwd.3 = (f32[1568,384]{1,0:T(8,128)}, bf16[4,192,384]{2,1,0:T(8,128)(2,1)}, bf16[4,192,384]{2,1,0:T(8,128)(2,1)}, f32[3,128,512]{2,1,0:T(8,128)}, f32[8,384]{1,0:T(8,128)}) custom-call(f32[1568,384]{1,0:T(8,128)} %get-tuple-element.53.gh_ref, bf16[1568,384]{1,0:T(8,128)(2,1)} %x_ref.3, bf16[1024,784]{1,0:T(8,128)(2,1)} %fusion.3.perm_ref, ...), custom_call_target="tpu_custom_call" | custom-call | flops 30000001024 | bytes 20000000 | tf_op jit(solution)/shard_map/attn_bwd/pallas_call | solution.py:345
  318.2 2.5 collective-permute-done.25
  324.3 7.6 %collective-permute-done.27 = bf16[4,96,384]{2,1,0:T(8,128)(2,1)S(1)} collective-permute-done((bf16[4,96,384]{2,1,0:T(8,128)(2,1)S(1)}, bf16[4,96,384]{2,1,0:T(8,128)(2,1)S(1)}, u32[]{:S(2)}, u32[]{:S(2)}) %collective-permute-start.27) | collective-permute-done | bytes 294944 | tf_op jit(solution)/shard_map/ppermute | solution.py:465
  343.5 9.0 %collective-permute-done.28 = bf16[4,96,384]{2,1,0:T(8,128)(2,1)S(1)} collective-permute-done((bf16[4,96,384]{2,1,0:T(8,128)(2,1)}, bf16[4,96,384]{2,1,0:T(8,128)(2,1)S(1)}, u32[]{:S(2)}, u32[]{:S(2)}) %collective-permute-start.28) | collective-permute-done | bytes 294944 | tf_op jit(solution)/shard_map/ppermute | solution.py:465
  352.6 3.0 collective-permute-done.33
  363.7 4.4 %collective-permute-done.34 = bf16[4,96,384]{2,1,0:T(8,128)(2,1)S(1)} collective-permute-done((bf16[4,96,384]{2,1,0:T(8,128)(2,1)S(1)}, bf16[4,96,384]{2,1,0:T(8,128)(2,1)S(1)}, u32[]{:S(2)}, u32[]{:S(2)}) %collective-permute-start.34) | collective-permute-done | bytes 294944 | tf_op jit(solution)/shard_map/ppermute | solution.py:465
  368.8 5.5 %collective-permute-done.42 = bf16[2,384,384]{2,1,0:T(8,128)(2,1)S(1)} collective-permute-done((bf16[2,384,384]{2,1,0:T(8,128)(2,1)S(1)}, bf16[2,384,384]{2,1,0:T(8,128)(2,1)S(1)}, u32[]{:S(2)}, u32[]{:S(2)}) %collective-permute-start.42) | collective-permute-done | bytes 589856 | tf_op jit(solution)/shard_map/ppermute | solution.py:465
  374.8 8.9 %collective-permute-done.47 = bf16[2,384,384]{2,1,0:T(8,128)(2,1)S(1)} collective-permute-done((bf16[2,384,384]{2,1,0:T(8,128)(2,1)S(1)}, bf16[2,384,384]{2,1,0:T(8,128)(2,1)S(1)}, u32[]{:S(2)}, u32[]{:S(2)}) %collective-permute-start.47) | collective-permute-done | bytes 589856 | tf_op jit(solution)/shard_map/ppermute | solution.py:465
  386.5 4.1 %collective-permute-done.48 = bf16[2,192,384]{2,1,0:T(8,128)(2,1)S(1)} collective-permute-done((bf16[2,192,384]{2,1,0:T(8,128)(2,1)S(1)}, bf16[2,192,384]{2,1,0:T(8,128)(2,1)S(1)}, u32[]{:S(2)}, u32[]{:S(2)}) %collective-permute-start.48) | collective-permute-done | bytes 294944 | tf_op jit(solution)/shard_map/ppermute | solution.py:465
  393.1 3.2 collective-permute-start.45
  396.3 3.8 collective-permute-start.50
  400.2 2.8 collective-permute-done.50
  (329 shorter events, 126.8 us)
Async XLA Ops:
  2.5 25.8 %collective-permute-start.7 = (bf16[3,466]{1,0:T(4,128)(2,1)S(1)}, bf16[3,466]{1,0:T(4,128)(2,1)S(1)}, u32[]{:S(2)}, u32[]{:S(2)}) collective-permute-start(bf16[3,466]{1,0:T(4,128)(2,1)S(1)} %pad_maximum_fusion.24), channel_id=1, source_target_pairs={{0,2},{1,3},{2,0},{3,1},{4,6},{5,7},{6,4},{7,5},{8,10},{9,11},{10,... | collective-permute-start | bytes 8396 | tf_op jit(solution)/shard_map/ppermute | solution.py:465
  6.2 16.7 %collective-permute-start = (bf16[1,240]{1,0:T(2,128)(2,1)S(1)}, bf16[1,240]{1,0:T(2,128)(2,1)S(1)}, u32[]{:S(2)}, u32[]{:S(2)}) collective-permute-start(bf16[1,240]{1,0:T(2,128)(2,1)S(1)} %reshape.291), channel_id=1, source_target_pairs={{0,16},{4,20},{8,24},{12,28},{16,0},{20,4},{24,8},{28,12},{1,17},{... | collective-permute-start | bytes 1448 | tf_op jit(solution)/shard_map/ppermute | solution.py:465
  10.7 63.2 %collective-permute-start.14 = (bf16[4,96,384]{2,1,0:T(8,128)(2,1)S(1)}, bf16[4,96,384]{2,1,0:T(8,128)(2,1)}, u32[]{:S(2)}, u32[]{:S(2)}) collective-permute-start(bf16[4,96,384]{2,1,0:T(8,128)(2,1)S(1)} %get-tuple-element.89), channel_id=1, source_target_pairs={{0,2},{1,3},{2,0},{3,1},{4,6},{5,7},{6,4},{7,5},{8,10},{9,11},{10,... | collective-permute-start | bytes 884744 | tf_op jit(solution)/shard_map/ppermute | solution.py:465
  12.0 37.2 %collective-permute-start.16 = (bf16[2,48,384]{2,1,0:T(8,128)(2,1)S(1)}, bf16[2,48,384]{2,1,0:T(8,128)(2,1)}, u32[]{:S(2)}, u32[]{:S(2)}) collective-permute-start(bf16[2,48,384]{2,1,0:T(8,128)(2,1)S(1)} %get-tuple-element.76), channel_id=1, source_target_pairs={{0,16},{4,20},{8,24},{12,28},{16,0},{20,4},{24,8},{28,12},{1,17},{... | collective-permute-start | bytes 221192 | tf_op jit(solution)/shard_map/ppermute | solution.py:465
  12.0 39.8 %collective-permute-start.9 = (bf16[2,48,384]{2,1,0:T(8,128)(2,1)}, bf16[2,48,384]{2,1,0:T(8,128)(2,1)}, u32[]{:S(2)}, u32[]{:S(2)}) collective-permute-start(bf16[2,48,384]{2,1,0:T(8,128)(2,1)} %get-tuple-element.102), channel_id=1, source_target_pairs={{0,16},{4,20},{8,24},{12,28},{16,0},{20,4},{24,8},{28,12},{1,17},{... | collective-permute-start | bytes 221192 | tf_op jit(solution)/shard_map/ppermute | solution.py:465
  26.6 36.7 %collective-permute-start.5 = (bf16[4,96,384]{2,1,0:T(8,128)(2,1)}, bf16[4,96,384]{2,1,0:T(8,128)(2,1)}, u32[]{:S(2)}, u32[]{:S(2)}) collective-permute-start(bf16[4,96,384]{2,1,0:T(8,128)(2,1)} %get-tuple-element.90), channel_id=1, source_target_pairs={{0,2},{1,3},{2,0},{3,1},{4,6},{5,7},{6,4},{7,5},{8,10},{9,11},{10,... | collective-permute-start | bytes 884744 | tf_op jit(solution)/shard_map/ppermute | solution.py:465
  57.8 17.2 %collective-permute-start.18 = (bf16[2,192,384]{2,1,0:T(8,128)(2,1)S(1)}, bf16[2,192,384]{2,1,0:T(8,128)(2,1)S(1)}, u32[]{:S(2)}, u32[]{:S(2)}) collective-permute-start(bf16[2,192,384]{2,1,0:T(8,128)(2,1)S(1)} %pad_maximum_fusion.9), channel_id=1, source_target_pairs={{0,4},{4,0},{8,12},{12,8},{16,20},{20,16},{24,28},{28,24},{1,5},{5... | collective-permute-start | bytes 884744 | tf_op jit(solution)/shard_map/ppermute | solution.py:465
  64.5 14.6 %collective-permute-start.6 = (bf16[4,192,384]{2,1,0:T(8,128)(2,1)S(1)}, bf16[4,192,384]{2,1,0:T(8,128)(2,1)S(1)}, u32[]{:S(2)}, u32[]{:S(2)}) collective-permute-start(bf16[4,192,384]{2,1,0:T(8,128)(2,1)S(1)} %pad_maximum_fusion.2), channel_id=1, source_target_pairs={{0,1},{1,0},{2,3},{3,2},{4,5},{5,4},{6,7},{7,6},{8,9},{9,8},{10,11... | collective-permute-start | bytes 1769480 | tf_op jit(solution)/shard_map/ppermute | solution.py:465
  73.3 16.3 %collective-permute-start.12 = (bf16[2,384,384]{2,1,0:T(8,128)(2,1)S(1)}, bf16[2,384,384]{2,1,0:T(8,128)(2,1)S(1)}, u32[]{:S(2)}, u32[]{:S(2)}) collective-permute-start(bf16[2,384,384]{2,1,0:T(8,128)(2,1)S(1)} %pad_maximum_fusion.3), channel_id=1, source_target_pairs={{0,2},{1,3},{2,0},{3,1},{4,6},{5,7},{6,4},{7,5},{8,10},{9,11},{10,... | collective-permute-start | bytes 1769480 | tf_op jit(solution)/shard_map/ppermute | solution.py:465
  74.9 48.3 %collective-permute-start.15 = (bf16[4,192,384]{2,1,0:T(8,128)(2,1)S(1)}, bf16[4,192,384]{2,1,0:T(8,128)(2,1)S(1)}, u32[]{:S(2)}, u32[]{:S(2)}) collective-permute-start(bf16[4,192,384]{2,1,0:T(8,128)(2,1)S(1)} %pad_maximum_fusion.4), channel_id=1, source_target_pairs={{0,1},{1,0},{2,3},{3,2},{4,5},{5,4},{6,7},{7,6},{8,9},{9,8},{10,11... | collective-permute-start | bytes 1769480 | tf_op jit(solution)/shard_map/ppermute | solution.py:465
  76.0 49.4 %collective-permute-start.19 = (bf16[2,384,384]{2,1,0:T(8,128)(2,1)S(1)}, bf16[2,384,384]{2,1,0:T(8,128)(2,1)S(1)}, u32[]{:S(2)}, u32[]{:S(2)}) collective-permute-start(bf16[2,384,384]{2,1,0:T(8,128)(2,1)S(1)} %pad_maximum_fusion.5), channel_id=1, source_target_pairs={{0,2},{1,3},{2,0},{3,1},{4,6},{5,7},{6,4},{7,5},{8,10},{9,11},{10,... | collective-permute-start | bytes 1769480 | tf_op jit(solution)/shard_map/ppermute | solution.py:465
  90.6 36.2 %collective-permute-start.13 = (bf16[2,768,384]{2,1,0:T(8,128)(2,1)S(1)}, bf16[2,768,384]{2,1,0:T(8,128)(2,1)S(1)}, u32[]{:S(2)}, u32[]{:S(2)}) collective-permute-start(bf16[2,768,384]{2,1,0:T(8,128)(2,1)S(1)} %get-tuple-element.91), channel_id=1, source_target_pairs={{0,1},{1,0},{2,3},{3,2},{4,5},{5,4},{6,7},{7,6},{8,9},{9,8},{10,11... | collective-permute-start | bytes 3538952 | tf_op jit(solution)/shard_map/ppermute | solution.py:465
  126.3 42.5 %collective-permute-start.20 = (bf16[2,768,384]{2,1,0:T(8,128)(2,1)S(1)}, bf16[2,768,384]{2,1,0:T(8,128)(2,1)S(1)}, u32[]{:S(2)}, u32[]{:S(2)}) collective-permute-start(bf16[2,768,384]{2,1,0:T(8,128)(2,1)S(1)} %get-tuple-element.87), channel_id=1, source_target_pairs={{0,1},{1,0},{2,3},{3,2},{4,5},{5,4},{6,7},{7,6},{8,9},{9,8},{10,11... | collective-permute-start | bytes 3538952 | tf_op jit(solution)/shard_map/ppermute | solution.py:465
  297.1 24.7 %collective-permute-start.26 = (bf16[4,192,384]{2,1,0:T(8,128)(2,1)}, bf16[4,192,384]{2,1,0:T(8,128)(2,1)S(1)}, u32[]{:S(2)}, u32[]{:S(2)}) collective-permute-start(bf16[4,192,384]{2,1,0:T(8,128)(2,1)} %get-tuple-element.66), channel_id=1, source_target_pairs={{0,1},{1,0},{2,3},{3,2},{4,5},{5,4},{6,7},{7,6},{8,9},{9,8},{10,11... | collective-permute-start | bytes 1769480 | tf_op jit(solution)/shard_map/ppermute | solution.py:465
  317.2 39.2 %collective-permute-start.41 = (bf16[2,768,384]{2,1,0:T(8,128)(2,1)}, bf16[2,768,384]{2,1,0:T(8,128)(2,1)}, u32[]{:S(2)}, u32[]{:S(2)}) collective-permute-start(bf16[2,768,384]{2,1,0:T(8,128)(2,1)} %get-tuple-element.72), channel_id=1, source_target_pairs={{0,1},{1,0},{2,3},{3,2},{4,5},{5,4},{6,7},{7,6},{8,9},{9,8},{10,11... | collective-permute-start | bytes 3538952 | tf_op jit(solution)/shard_map/ppermute | solution.py:465
  318.2 40.2 %collective-permute-start.46 = (bf16[2,768,384]{2,1,0:T(8,128)(2,1)}, bf16[2,768,384]{2,1,0:T(8,128)(2,1)}, u32[]{:S(2)}, u32[]{:S(2)}) collective-permute-start(bf16[2,768,384]{2,1,0:T(8,128)(2,1)} %get-tuple-element.74), channel_id=1, source_target_pairs={{0,1},{1,0},{2,3},{3,2},{4,5},{5,4},{6,7},{7,6},{8,9},{9,8},{10,11... | collective-permute-start | bytes 3538952 | tf_op jit(solution)/shard_map/ppermute | solution.py:465
  320.7 19.3 %collective-permute-start.40 = (f32[3,466]{1,0:T(4,128)S(1)}, f32[3,466]{1,0:T(4,128)}, u32[]{:S(2)}, u32[]{:S(2)}) collective-permute-start(f32[3,466]{1,0:T(4,128)S(1)} %add.150), channel_id=1, source_target_pairs={{0,4},{4,0},{8,12},{12,8},{16,20},{20,16},{24,28},{28,24},{1,5},{5... | collective-permute-start | bytes 16784 | tf_op jit(solution)/shard_map/ppermute | solution.py:465
  332.7 19.7 %collective-permute-start.28 = (bf16[4,96,384]{2,1,0:T(8,128)(2,1)}, bf16[4,96,384]{2,1,0:T(8,128)(2,1)S(1)}, u32[]{:S(2)}, u32[]{:S(2)}) collective-permute-start(bf16[4,96,384]{2,1,0:T(8,128)(2,1)} %fusion.62), channel_id=1, source_target_pairs={{0,16},{4,20},{8,24},{12,28},{16,0},{20,4},{24,8},{28,12},{1,17},{... | collective-permute-start | bytes 884744 | tf_op jit(solution)/shard_map/ppermute | solution.py:465
  335.9 19.7 %collective-permute-start.33 = (bf16[4,96,384]{2,1,0:T(8,128)(2,1)}, bf16[4,96,384]{2,1,0:T(8,128)(2,1)S(1)}, u32[]{:S(2)}, u32[]{:S(2)}) collective-permute-start(bf16[4,96,384]{2,1,0:T(8,128)(2,1)} %fusion.63), channel_id=1, source_target_pairs={{0,16},{4,20},{8,24},{12,28},{16,0},{20,4},{24,8},{28,12},{1,17},{... | collective-permute-start | bytes 884744 | tf_op jit(solution)/shard_map/ppermute | solution.py:465
  355.7 12.4 %collective-permute-start.34 = (bf16[4,96,384]{2,1,0:T(8,128)(2,1)S(1)}, bf16[4,96,384]{2,1,0:T(8,128)(2,1)S(1)}, u32[]{:S(2)}, u32[]{:S(2)}) collective-permute-start(bf16[4,96,384]{2,1,0:T(8,128)(2,1)S(1)} %fusion.27), channel_id=1, source_target_pairs={{0,8},{4,12},{8,0},{12,4},{16,24},{20,28},{24,16},{28,20},{1,9},{5... | collective-permute-start | bytes 884744 | tf_op jit(solution)/shard_map/ppermute | solution.py:465
  358.0 16.3 %collective-permute-start.42 = (bf16[2,384,384]{2,1,0:T(8,128)(2,1)S(1)}, bf16[2,384,384]{2,1,0:T(8,128)(2,1)S(1)}, u32[]{:S(2)}, u32[]{:S(2)}) collective-permute-start(bf16[2,384,384]{2,1,0:T(8,128)(2,1)S(1)} %slice.509), channel_id=1, source_target_pairs={{0,2},{1,3},{2,0},{3,1},{4,6},{5,7},{6,4},{7,5},{8,10},{9,11},{10,... | collective-permute-start | bytes 1769480 | tf_op jit(solution)/shard_map/ppermute | solution.py:465
  360.8 22.9 %collective-permute-start.47 = (bf16[2,384,384]{2,1,0:T(8,128)(2,1)S(1)}, bf16[2,384,384]{2,1,0:T(8,128)(2,1)S(1)}, u32[]{:S(2)}, u32[]{:S(2)}) collective-permute-start(bf16[2,384,384]{2,1,0:T(8,128)(2,1)S(1)} %slice.508), channel_id=1, source_target_pairs={{0,2},{1,3},{2,0},{3,1},{4,6},{5,7},{6,4},{7,5},{8,10},{9,11},{10,... | collective-permute-start | bytes 1769480 | tf_op jit(solution)/shard_map/ppermute | solution.py:465
  362.7 21.3 %collective-permute-start.30 = (bf16[4,96,384]{2,1,0:T(8,128)(2,1)S(1)}, bf16[4,96,384]{2,1,0:T(8,128)(2,1)S(1)}, u32[]{:S(2)}, u32[]{:S(2)}) collective-permute-start(bf16[4,96,384]{2,1,0:T(8,128)(2,1)S(1)} %fusion.34), channel_id=1, source_target_pairs={{0,4},{4,0},{8,12},{12,8},{16,20},{20,16},{24,28},{28,24},{1,5},{5... | collective-permute-start | bytes 884744 | tf_op jit(solution)/shard_map/ppermute | solution.py:465
  368.3 15.9 %collective-permute-start.35 = (bf16[4,96,384]{2,1,0:T(8,128)(2,1)S(1)}, bf16[4,96,384]{2,1,0:T(8,128)(2,1)S(1)}, u32[]{:S(2)}, u32[]{:S(2)}) collective-permute-start(bf16[4,96,384]{2,1,0:T(8,128)(2,1)S(1)} %fusion.35), channel_id=1, source_target_pairs={{0,4},{4,0},{8,12},{12,8},{16,20},{20,16},{24,28},{28,24},{1,5},{5... | collective-permute-start | bytes 884744 | tf_op jit(solution)/shard_map/ppermute | solution.py:465
  (57 other events, 517.4 us)

commit v2 on v1

v2 whole, which is shorter than its diff:
```python
import jax
import jax.numpy as jnp
import numpy as np
from jax import lax
from jax.experimental import pallas as pl
from jax.experimental.pallas import tpu as pltpu
from jax.sharding import PartitionSpec as P

D = 384
HEADS = 12
HDIM = 32
FF = 1536
WIN = 7
SHIFT = 3
GRID = 4
LAYERS = 2
SIDE = GRID * WIN
CELLS = WIN * WIN
WINDOWS = GRID * GRID
IMG_ROWS = WINDOWS * CELLS
PAD = 64
PAD_ROWS = WINDOWS * PAD
PAIRS = WINDOWS // 2
TABLE = (2 * WIN - 1) ** 2
TILES = D // 128
TABLES_A_ROW = 9
CENTRE = (WIN - 1) * 2 * WIN
norm_eps = 1e-05
neg_fill = -10000.0
never = -1e30
bf16 = jnp.bfloat16
f32 = jnp.float32
VMEM_LIMIT = 56 * 1024 * 1024


def nn(a, b):
    return lax.dot_general(a, b, (((1,), (0,)), ((), ())), preferred_element_type=f32)


def nt(a, b):
    return lax.dot_general(a, b, (((1,), (1,)), ((), ())), preferred_element_type=f32)


def tn(a, b):
    return lax.dot_general(a, b, (((0,), (0,)), ((), ())), preferred_element_type=f32)


def padded_source(shifted):
    source = np.full((PAD_ROWS,), -1, np.int32)
    for a in range(GRID):
        for b in range(GRID):
            for p in range(WIN):
                for c in range(WIN):
                    row, col = a * WIN + p, b * WIN + c
                    if shifted:
                        row, col = (row + SHIFT) % SIDE, (col + SHIFT) % SIDE
                    here = (a * GRID + b) * PAD + p * WIN + c
                    source[here] = ((row // WIN) * GRID + col // WIN) * CELLS + (row % WIN) * WIN + col % WIN
    return source


def token_places():
    rows = np.zeros((IMG_ROWS,), np.int32)
    cols = np.zeros((IMG_ROWS,), np.int32)
    for a in range(GRID):
        for b in range(GRID):
            for p in range(WIN):
                for c in range(WIN):
                    at = (a * GRID + b) * CELLS + p * WIN + c
                    rows[at], cols[at] = a * WIN + p, b * WIN + c
    return rows, cols


def padded_labels(shifted):
    labels = np.zeros((PAD_ROWS,), np.int32)
    if shifted:
        band = lambda at: int(at >= SIDE - WIN) + int(at >= SIDE - SHIFT)
        for a in range(GRID):
            for b in range(GRID):
                for p in range(WIN):
                    for c in range(WIN):
                        here = (a * GRID + b) * PAD + p * WIN + c
                        labels[here] = 3 * band(a * WIN + p) + band(b * WIN + c)
    return labels


def normalize(rows):
    centre = rows - jnp.mean(rows, axis=-1, keepdims=True)
    spread = jnp.mean(centre * centre, axis=-1, keepdims=True)
    scale = lax.rsqrt(spread + norm_eps)
    return centre * scale, scale


def normalize_back(grad, gain, unit, scale):
    grad_unit = grad * gain
    first = jnp.mean(grad_unit, axis=-1, keepdims=True)
    second = jnp.mean(grad_unit * unit, axis=-1, keepdims=True)
    return scale * (grad_unit - first - unit * second)


def column_sum(rows):
    return jnp.sum(rows, axis=0, keepdims=True)


def head_masks():
    lane = lax.broadcasted_iota(jnp.int32, (1, 128), 1)
    return [jnp.where(lane // HDIM == h, 1.0, 0.0).astype(bf16) for h in range(4)]


def spread_heads(tile, masks):
    return jnp.concatenate([tile * mask for mask in masks], axis=0)


def stack_heads(tile):
    return jnp.concatenate([tile[:, 128 * h : 128 * (h + 1)] for h in range(4)], axis=0)


def vec_lanes(at):
    return slice(at * D, (at + 1) * D)


def table_spot(layer, head):
    spot = layer * HEADS + head
    return 4 + spot // TABLES_A_ROW, (spot % TABLES_A_ROW) * 256


def cell_lanes():
    lane = lax.broadcasted_iota(jnp.int32, (256, 128), 0)
    query = lax.broadcasted_iota(jnp.int32, (256, 128), 1) % PAD
    spot = (query // WIN) * (2 * WIN - 1) + query % WIN
    return jnp.where((lane == spot) & (query < CELLS), 1.0, 0.0).astype(bf16)


def turn_rows(rows, shift):
    return pltpu.roll(pltpu.roll(rows, shift % 256, axis=1), 0, axis=1, stride=1, stride_axis=0)


def spread_tables(layer, rows, bias_ref):
    lanes = cell_lanes()
    first = lax.broadcasted_iota(jnp.int32, (8, 128), 1) < PAD
    bias_ref[...] = jnp.full(bias_ref.shape, never, f32)
    for head in range(HEADS):
        row, at = table_spot(layer, head)
        table = jnp.broadcast_to(rows[row : row + 1, at : at + 256], (8, 256))
        turned = [turn_rows(table, 256 - CENTRE + (2 * WIN - 1) * p) for p in range(WIN)]
        looked = nn(jnp.concatenate(turned, axis=0).astype(bf16), lanes)
        here = slice(128 * (head % 4), 128 * (head % 4 + 1))
        for p in range(WIN):
            part = looked[8 * p : 8 * (p + 1), :]
            bias_ref[head // 4, WIN * p : WIN * (p + 1), here] = jnp.where(first, part, never)[:WIN]
            bias_ref[head // 4, PAD + WIN * p : PAD + WIN * (p + 1), here] = jnp.where(first, never, part)[:WIN]


def fold_tables(layer, sum_ref, rows_ref):
    lanes = cell_lanes()
    first = lax.broadcasted_iota(jnp.int32, (PAD, 128), 1) < PAD
    real = lax.broadcasted_iota(jnp.int32, (8, 256), 0) < WIN
    to_row = lax.broadcasted_iota(jnp.int32, (PAD, PAD), 0)
    from_row = lax.broadcasted_iota(jnp.int32, (PAD, PAD), 1)
    mirror = (to_row // WIN == from_row // WIN) & (to_row % WIN + from_row % WIN == WIN - 1)
    mirror = jnp.where(mirror, 1.0, 0.0).astype(bf16)
    for head in range(HEADS):
        row, at = table_spot(layer, head)
        here = slice(128 * (head % 4), 128 * (head % 4 + 1))
        both = jnp.where(first, sum_ref[head // 4, 0:PAD, here], sum_ref[head // 4, PAD : 2 * PAD, here])
        high = both.astype(bf16)
        low = (both - high.astype(f32)).astype(bf16)
        looked = nt(nn(mirror, high).astype(bf16), lanes) + nt(nn(mirror, low).astype(bf16), lanes)
        acc = jnp.zeros((8, 256), f32)
        for p in range(WIN):
            part = jnp.where(real, looked[WIN * p : WIN * p + 8, :], 0.0)
            acc += turn_rows(part, CENTRE - (2 * WIN - 1) * p - (WIN - 1))
        rows_ref[row : row + 1, at : at + 256] = column_sum(acc)


def attn_fwd_kernel(layer, pieces, *refs):
    x_ref, perm_ref, sm_ref, mask_ref = refs[:4]
    w_refs = refs[4 : 4 + pieces]
    if pieces > 1:
        at_ref, h_ref, a1_ref, qkv_ref, p_ref, ou_ref, w_ref, o_ref, bias_ref = refs[4 + pieces :]
    else:
        h_ref, a1_ref, qkv_ref, p_ref, ou_ref, o_ref, bias_ref = refs[4 + pieces :]
        w_ref = w_refs[0]

    @pl.when(pl.program_id(0) == 0)
    def _():
        spread_tables(layer, sm_ref[...], bias_ref)
        if pieces > 1:
            merge_pieces(at_ref, w_refs, w_ref)

    x = x_ref[...].astype(f32)
    unit, _ = normalize(x)
    a1 = (unit * sm_ref[layer : layer + 1, vec_lanes(0)] + sm_ref[layer : layer + 1, vec_lanes(2)]).astype(bf16)
    a1p = nn(perm_ref[...], a1).astype(bf16)
    a1_ref[...] = a1p
    qkv_ref[:, 0:D] = (nt(a1p, w_ref[0]) + sm_ref[2 + layer : 3 + layer, vec_lanes(4)]).astype(bf16)
    qkv_ref[:, D : 2 * D] = nt(a1p, w_ref[1]).astype(bf16)
    qkv_ref[:, 2 * D : 3 * D] = (nt(a1p, w_ref[2]) + sm_ref[2 + layer : 3 + layer, vec_lanes(5)]).astype(bf16)
    masks = head_masks()

    def one_pair(pair, carry):
        rows = pl.ds(pl.multiple_of(pair * 128, 128), 128)
        mask = mask_ref[0, pair]
        mask4 = jnp.concatenate([mask] * 4, axis=1)
        for g in range(TILES):
            q = qkv_ref[rows, 128 * g : 128 * (g + 1)]
            k = qkv_ref[rows, D + 128 * g : D + 128 * (g + 1)]
            v = qkv_ref[rows, 2 * D + 128 * g : 2 * D + 128 * (g + 1)]
            s = (HDIM**-0.5) * nt(k, spread_heads(q, masks)) + bias_ref[g] + mask4
            e = jnp.exp(s - jnp.max(s, axis=0, keepdims=True))
            p = (e * (1.0 / jnp.sum(e, axis=0, keepdims=True))).astype(bf16)
            p_ref[0, pair, g] = p
            o = tn(stack_heads(p), spread_heads(v, masks))
            o_ref[rows, 128 * g : 128 * (g + 1)] = o.astype(bf16)
        return carry

    lax.fori_loop(0, PAIRS, one_pair, 0)
    ou = tn(perm_ref[...], o_ref[...]).astype(bf16)
    ou_ref[...] = ou
    h_ref[...] = x + (nn(ou, w_ref[3]) + sm_ref[layer : layer + 1, vec_lanes(4)])


def merge_pieces(at_ref, pieces, whole_ref):
    rows = pieces[0].shape[1]
    for s, piece in enumerate(pieces):
        start = pl.multiple_of((at_ref[0] ^ s) * rows, 16)
        whole_ref[:, pl.ds(start, rows), :] = piece[...]


def attn_core_back(layer, gh_ref, perm_ref, w_ref, a1_ref, qkv_ref, p_ref, ou_ref, grad_ref, vg_ref, wacc_ref, do_ref, dm_ref, ds_ref):
    image = pl.program_id(0)

    @pl.when(image == 0)
    def _():
        wacc_ref[...] = jnp.zeros_like(wacc_ref)
        ds_ref[...] = jnp.zeros_like(ds_ref)
        vg_ref[...] = jnp.zeros_like(vg_ref)

    go = gh_ref[...].astype(bf16)
    vg_ref[layer : layer + 1, vec_lanes(4)] += column_sum(go.astype(f32))
    wacc_ref[3] += tn(ou_ref[...], go)
    do_ref[...] = nn(perm_ref[...], nt(go, w_ref[3]).astype(bf16)).astype(bf16)
    masks = head_masks()

    def one_pair(pair, carry):
        rows = pl.ds(pl.multiple_of(pair * 128, 128), 128)
        for g in range(TILES):
            q = qkv_ref[rows, 128 * g : 128 * (g + 1)]
            k = qkv_ref[rows, D + 128 * g : D + 128 * (g + 1)]
            v = qkv_ref[rows, 2 * D + 128 * g : 2 * D + 128 * (g + 1)]
            do4 = spread_heads(do_ref[rows, 128 * g : 128 * (g + 1)], masks)
            pb = p_ref[0, pair, g]
            p = pb.astype(f32)
            dp = nt(v, do4)
            ds = p * (dp - jnp.sum(p * dp, axis=0, keepdims=True))
            dsb = ds.astype(bf16)
            ds_ref[g] += dsb.astype(f32)
            dv = nn(pb, do4)
            dk = (HDIM**-0.5) * nn(dsb, spread_heads(q, masks))
            dq = (HDIM**-0.5) * tn(stack_heads(dsb), spread_heads(k, masks))
            dm_ref[rows, 128 * g : 128 * (g + 1)] = dq.astype(bf16)
            dm_ref[rows, D + 128 * g : D + 128 * (g + 1)] = dk.astype(bf16)
            dm_ref[rows, 2 * D + 128 * g : 2 * D + 128 * (g + 1)] = dv.astype(bf16)
        return carry

    lax.fori_loop(0, PAIRS, one_pair, 0)
    a1p = a1_ref[...]
    for c in range(3):
        dm = dm_ref[:, D * c : D * (c + 1)]
        wacc_ref[c] += tn(dm, a1p)
        if c != 1:
            vg_ref[2 + layer : 3 + layer, vec_lanes(4 + c // 2)] += column_sum(dm.astype(f32))

    @pl.when(image == pl.num_programs(0) - 1)
    def _():
        fold_tables(layer, ds_ref, vg_ref)
        grad_ref[...] = wacc_ref[...].astype(bf16)


def attn_norm_back(layer, gh_ref, x_ref, perm_ref, sm_ref, w_ref, dm_ref, g_ref, vg_ref):
    da = nn(dm_ref[:, 0:D], w_ref[0]) + nn(dm_ref[:, D : 2 * D], w_ref[1]) + nn(dm_ref[:, 2 * D : 3 * D], w_ref[2])
    da1 = tn(perm_ref[...], da.astype(bf16))
    unit, scale = normalize(x_ref[...].astype(f32))
    vg_ref[layer : layer + 1, vec_lanes(0)] += column_sum(da1 * unit)
    vg_ref[layer : layer + 1, vec_lanes(2)] += column_sum(da1)
    g_ref[...] = gh_ref[...] + normalize_back(da1, sm_ref[layer : layer + 1, vec_lanes(0)], unit, scale)


def attn_bwd_kernel(layer, gh_ref, x_ref, perm_ref, sm_ref, w_ref, a1_ref, qkv_ref, p_ref, ou_ref, g_ref, grad_ref, vg_ref, wacc_ref, do_ref, dm_ref, ds_ref):
    attn_core_back(layer, gh_ref, perm_ref, w_ref, a1_ref, qkv_ref, p_ref, ou_ref, grad_ref, vg_ref, wacc_ref, do_ref, dm_ref, ds_ref)
    attn_norm_back(layer, gh_ref, x_ref, perm_ref, sm_ref, w_ref, dm_ref, g_ref, vg_ref)


def attn_core_kernel(layer, gh_ref, perm_ref, w_ref, a1_ref, qkv_ref, p_ref, ou_ref, dm_ref, grad_ref, vg_ref, wacc_ref, do_ref, ds_ref):
    attn_core_back(layer, gh_ref, perm_ref, w_ref, a1_ref, qkv_ref, p_ref, ou_ref, grad_ref, vg_ref, wacc_ref, do_ref, dm_ref, ds_ref)


def attn_norm_kernel(layer, gh_ref, x_ref, perm_ref, sm_ref, w_ref, dm_ref, g_ref, vg_ref):
    @pl.when(pl.program_id(0) == 0)
    def _():
        vg_ref[...] = jnp.zeros_like(vg_ref)

    attn_norm_back(layer, gh_ref, x_ref, perm_ref, sm_ref, w_ref, dm_ref, g_ref, vg_ref)


def gelu_parts(z):
    cdf = 0.5 * (1.0 + lax.erf(z * 0.7071067811865476))
    slope = cdf + z * (jnp.exp(-0.5 * z * z) * 0.3989422804014327)
    return (z * cdf).astype(bf16), slope


CHUNK = 768


def ffn_fwd_kernel(layer, pieces, *refs):
    h_ref, sm_ref = refs[:2]
    at_ref, x_ref, w_ref = refs[2 + pieces :]

    @pl.when(pl.program_id(0) == 0)
    def _():
        merge_pieces(at_ref, refs[2 : 2 + pieces], w_ref)

    h = h_ref[...]
    unit, _ = normalize(h)
    a2 = (unit * sm_ref[layer : layer + 1, vec_lanes(1)] + sm_ref[layer : layer + 1, vec_lanes(3)]).astype(bf16)
    out = h + sm_ref[layer : layer + 1, vec_lanes(5)]
    for at in range(0, FF, CHUNK):
        z = nt(a2, w_ref[0, at : at + CHUNK, :]) + sm_ref[2 + layer : 3 + layer, at : at + CHUNK]
        m = (z * (0.5 * (1.0 + lax.erf(z * 0.7071067811865476)))).astype(bf16)
        out += nn(m, w_ref[1, at : at + CHUNK, :])
    x_ref[...] = out


def ffn_both_kernel(layer, with_output, *refs):
    if with_output:
        h_ref, g_ref, sm_ref, w_ref, in_ref, gh_ref, grad_ref, vg_ref, x_ref, mean_ref, wacc_ref = refs
    else:
        h_ref, g_ref, sm_ref, w_ref, gh_ref, grad_ref, vg_ref, wacc_ref = refs
    image = pl.program_id(0)

    @pl.when(image == 0)
    def _():
        wacc_ref[...] = jnp.zeros_like(wacc_ref)
        vg_ref[...] = jnp.zeros_like(vg_ref)

    h = h_ref[...]
    unit, scale = normalize(h)
    gain = sm_ref[layer : layer + 1, vec_lanes(1)]
    a2 = (unit * gain + sm_ref[layer : layer + 1, vec_lanes(3)]).astype(bf16)
    g = g_ref[...].astype(f32)
    gm = g.astype(bf16)
    vg_ref[layer : layer + 1, vec_lanes(5)] += column_sum(gm.astype(f32))
    if with_output:
        out = h + sm_ref[layer : layer + 1, vec_lanes(5)]
    da = jnp.zeros((IMG_ROWS, D), f32)
    for at in range(0, FF, CHUNK):
        up = w_ref[0, at : at + CHUNK, :]
        down = w_ref[1, at : at + CHUNK, :]
        z = nt(a2, up) + sm_ref[2 + layer : 3 + layer, at : at + CHUNK]
        m, slope = gelu_parts(z)
        if with_output:
            out += nn(m, down)
        dz = (nt(gm, down) * slope).astype(bf16)
        vg_ref[2 + layer : 3 + layer, at : at + CHUNK] += column_sum(dz.astype(f32))
        wacc_ref[0, at : at + CHUNK, :] += tn(dz, a2)
        wacc_ref[1, at : at + CHUNK, :] += tn(m, gm)
        da += nn(dz, up)
    vg_ref[layer : layer + 1, vec_lanes(1)] += column_sum(da * unit)
    vg_ref[layer : layer + 1, vec_lanes(3)] += column_sum(da)
    gh_ref[...] = g + normalize_back(da, gain, unit, scale)
    if with_output:
        x_ref[...] = out.astype(bf16)
        flags = in_ref[...]
        mean_ref[0] = column_sum(out * flags) / jnp.sum(flags)

    @pl.when(image == pl.num_programs(0) - 1)
    def _():
        grad_ref[...] = wacc_ref[...].astype(bf16)


def whole(*shape):
    return pl.BlockSpec(shape, lambda i: (0,) * len(shape))


def by_image(*shape):
    return pl.BlockSpec(shape, lambda i: (i,) + (0,) * (len(shape) - 1))


def scalar():
    return pl.BlockSpec(memory_space=pltpu.SMEM)


def shape_of(shape, kind):
    return jax.ShapeDtypeStruct(shape, kind)


def call(kernel, name, images, ins, outs, scratch=()):
    return pl.pallas_call(
        kernel,
        name=name,
        grid=(images,),
        in_specs=ins,
        out_specs=[spec for spec, _ in outs],
        out_shape=[shape for _, shape in outs],
        scratch_shapes=scratch,
        compiler_params=pltpu.CompilerParams(vmem_limit_bytes=VMEM_LIMIT, dimension_semantics=("arbitrary",)),
        cost_estimate=pl.CostEstimate(flops=10**8, bytes_accessed=10**5, transcendentals=0),
    )


def attn_forward(layer, x, perm, rows, mask, weights, at):
    images = x.shape[0] // IMG_ROWS
    tokens, padded, pieces = images * IMG_ROWS, images * PAD_ROWS, len(weights)
    ins = [by_image(IMG_ROWS, D), whole(PAD_ROWS, IMG_ROWS), whole(8, 6 * D), by_image(1, PAIRS, 128, 128)]
    ins += [whole(*piece.shape) for piece in weights]
    args = [x, perm, rows, mask, *weights]
    outs = [
        (by_image(IMG_ROWS, D), shape_of((tokens, D), f32)),
        (by_image(PAD_ROWS, D), shape_of((padded, D), bf16)),
        (by_image(PAD_ROWS, 3 * D), shape_of((padded, 3 * D), bf16)),
        (by_image(1, PAIRS, TILES, 128, 512), shape_of((images, PAIRS, TILES, 128, 512), bf16)),
        (by_image(IMG_ROWS, D), shape_of((tokens, D), bf16)),
    ]
    if pieces > 1:
        ins.append(scalar())
        args.append(at)
        outs.append((whole(4, D, D), shape_of((4, D, D), bf16)))
    return call(
        lambda *refs: attn_fwd_kernel(layer, pieces, *refs),
        "attn_fwd",
        images,
        ins,
        outs,
        [pltpu.VMEM((PAD_ROWS, D), bf16), pltpu.VMEM((TILES, 128, 512), f32)],
    )(*args)


def kept_specs():
    return [
        by_image(PAD_ROWS, D),
        by_image(PAD_ROWS, 3 * D),
        by_image(1, PAIRS, TILES, 128, 512),
        by_image(IMG_ROWS, D),
    ]


def attn_backward(layer, gh, x, perm, rows, weights, kept):
    images = x.shape[0] // IMG_ROWS
    return call(
        lambda *refs: attn_bwd_kernel(layer, *refs),
        "attn_bwd",
        images,
        [by_image(IMG_ROWS, D), by_image(IMG_ROWS, D), whole(PAD_ROWS, IMG_ROWS), whole(8, 6 * D), whole(4, D, D)] + kept_specs(),
        [
            (by_image(IMG_ROWS, D), shape_of((images * IMG_ROWS, D), f32)),
            (whole(4, D, D), shape_of((4, D, D), bf16)),
            (whole(8, 6 * D), shape_of((8, 6 * D), f32)),
        ],
        [
            pltpu.VMEM((4, D, D), f32),
            pltpu.VMEM((PAD_ROWS, D), bf16),
            pltpu.VMEM((PAD_ROWS, 3 * D), bf16),
            pltpu.VMEM((TILES, 128, 512), f32),
        ],
    )(gh, x, perm, rows, weights, *kept)


def attn_backward_core(layer, gh, perm, weights, kept):
    images = gh.shape[0] // IMG_ROWS
    return call(
        lambda *refs: attn_core_kernel(layer, *refs),
        "attn_core",
        images,
        [by_image(IMG_ROWS, D), whole(PAD_ROWS, IMG_ROWS), whole(4, D, D)] + kept_specs(),
        [
            (by_image(PAD_ROWS, 3 * D), shape_of((images * PAD_ROWS, 3 * D), bf16)),
            (whole(4, D, D), shape_of((4, D, D), bf16)),
            (whole(8, 6 * D), shape_of((8, 6 * D), f32)),
        ],
        [pltpu.VMEM((4, D, D), f32), pltpu.VMEM((PAD_ROWS, D), bf16), pltpu.VMEM((TILES, 128, 512), f32)],
    )(gh, perm, weights, *kept)


def attn_backward_norm(layer, gh, x, perm, rows, weights, dmix):
    images = x.shape[0] // IMG_ROWS
    return call(
        lambda *refs: attn_norm_kernel(layer, *refs),
        "attn_norm",
        images,
        [
            by_image(IMG_ROWS, D),
            by_image(IMG_ROWS, D),
            whole(PAD_ROWS, IMG_ROWS),
            whole(8, 6 * D),
            whole(4, D, D),
            by_image(PAD_ROWS, 3 * D),
        ],
        [
            (by_image(IMG_ROWS, D), shape_of((images * IMG_ROWS, D), f32)),
            (whole(8, 6 * D), shape_of((8, 6 * D), f32)),
        ],
    )(gh, x, perm, rows, weights, dmix)


def ffn_forward(layer, h, rows, weights, at):
    images = h.shape[0] // IMG_ROWS
    return call(
        lambda *refs: ffn_fwd_kernel(layer, len(weights), *refs),
        "ffn_fwd",
        images,
        [by_image(IMG_ROWS, D), whole(8, 6 * D)] + [whole(*piece.shape) for piece in weights] + [scalar()],
        [
            (by_image(IMG_ROWS, D), shape_of(h.shape, f32)),
            (whole(2, FF, D), shape_of((2, FF, D), bf16)),
        ],
    )(h, rows, *weights, at)


def ffn_both(layer, h, g, rows, weights, flags=None):
    images = h.shape[0] // IMG_ROWS
    tokens = images * IMG_ROWS
    with_output = flags is not None
    ins = [by_image(IMG_ROWS, D), by_image(IMG_ROWS, D), whole(8, 6 * D), whole(2, FF, D)]
    outs = [
        (by_image(IMG_ROWS, D), shape_of((tokens, D), f32)),
        (whole(2, FF, D), shape_of((2, FF, D), bf16)),
        (whole(8, 6 * D), shape_of((8, 6 * D), f32)),
    ]
    args = [h, g, rows, weights]
    if with_output:
        ins.append(by_image(IMG_ROWS, 1))
        args.append(flags)
        outs.append((by_image(IMG_ROWS, D), shape_of((tokens, D), bf16)))
        outs.append((by_image(1, 1, D), shape_of((images, 1, D), f32)))
    return call(
        lambda *refs: ffn_both_kernel(layer, with_output, *refs),
        "ffn_both_out" if with_output else "ffn_both",
        images,
        ins,
        outs,
        [pltpu.VMEM((2, FF, D), f32)],
    )(*args)


def key_masks(own_size, shifted):
    source = padded_source(shifted)
    rows_of, cols_of = token_places()
    key_row = jnp.asarray(np.where(source < 0, SIDE, rows_of[source]))
    key_col = jnp.asarray(np.where(source < 0, SIDE, cols_of[source]))
    inside = (key_row[None] < own_size[:, 0:1]) & (key_col[None] < own_size[:, 1:2])
    inside = inside.reshape(-1, PAIRS, 128, 1)
    labels = jnp.asarray(padded_labels(shifted).reshape(PAIRS, 128))
    same = labels[None, :, :, None] == labels[None, :, None, :]
    return jnp.where(inside & same, 0.0, neg_fill).astype(f32)


def inside_column(own_size):
    rows_of, cols_of = token_places()
    inside = (jnp.asarray(rows_of)[None] < own_size[:, 0:1]) & (jnp.asarray(cols_of)[None] < own_size[:, 1:2])
    return inside.astype(f32).reshape(-1, 1)


def move_matrix(shifted):
    source = jnp.asarray(padded_source(shifted))
    return (source[:, None] == jnp.arange(IMG_ROWS, dtype=jnp.int32)[None, :]).astype(bf16)


def swap(rows, axis, size, bit):
    return lax.ppermute(rows, axis, [(i, i ^ bit) for i in range(size)])


def bits_of(axis, size):
    stages = []
    bit = size // 2
    while bit:
        stages.append((axis, size, bit))
        bit //= 2
    return stages


def exchange(blocks, axis, size):
    return [swap(blocks(s), axis, size, s) for s in range(1, size)]


def total(first, others):
    acc = first.astype(f32)
    for other in others:
        acc = acc + other.astype(f32)
    return acc


def tied(*arrays):
    return lax.optimization_barrier(arrays)


def to_all(rows, axis, size):
    return lax.all_to_all(jnp.broadcast_to(rows[None], (size,) + rows.shape), axis, 0, 0)


def sum_parts(parts, axis):
    return jnp.sum(lax.all_to_all(parts.astype(bf16), axis, 0, 0).astype(f32), axis=0)


def own_block(rows, at, size, axis):
    return lax.dynamic_slice_in_dim(rows, at * size, size, axis)


def put(rows, part, row, lane):
    return lax.dynamic_update_slice(rows, part, (jnp.int32(row), jnp.int32(lane)))


def body(n_dp, n_tensor, tokens, cotangent, image_size, vectors, mix_weight, mix_bias, bias_table, out_weight, up_weight, up_bias, down_weight):
    local_images = tokens.shape[0] // IMG_ROWS
    devices = n_dp * n_tensor
    stages = bits_of("tensor", n_tensor)[::-1] + bits_of("dp", n_dp)[::-1]
    dp_at, tensor_at = lax.axis_index("dp"), lax.axis_index("tensor")
    own = dp_at * n_tensor + tensor_at
    own_size = lax.dynamic_slice_in_dim(image_size, tensor_at * local_images, local_images, 0)
    vec_own = vectors.shape[1]
    ub_own = up_bias.shape[1]
    own_heads = bias_table.shape[2]
    own_cols = own_heads * HDIM
    ff_part = FF // n_tensor

    once = (dp_at == 0).astype(bf16)
    part = jnp.zeros((8, 6 * D), bf16)
    part = put(part, vectors, 0, own * vec_own)
    part = put(part, up_bias[0:1], 2, tensor_at * ff_part + dp_at * ub_own)
    part = put(part, up_bias[1:2], 3, own * ub_own)
    own_bias = mix_bias * once
    part = put(part, own_bias[:, 0], 2, FF + tensor_at * own_cols)
    part = put(part, own_bias[:, 1], 2, FF + D + tensor_at * own_cols)
    own_tables = jnp.pad((bias_table * once).transpose(0, 2, 1), ((0, 0), (0, 0), (0, 256 - TABLE)))
    table_at = [(4 + (l * HEADS + tensor_at * own_heads) // TABLES_A_ROW, ((l * HEADS + tensor_at * own_heads) % TABLES_A_ROW) * 256) for l in range(LAYERS)]
    for l in range(LAYERS):
        part = put(part, own_tables[l].reshape(1, -1), *table_at[l])
    mix_own = mix_weight.transpose(0, 2, 3, 1)
    attn_own = jnp.concatenate([mix_own, out_weight[:, None]], axis=1)
    dense_own = jnp.stack([up_weight.transpose(0, 2, 1), down_weight], axis=1)
    part, attn_own, dense_own = tied(part, attn_own, dense_own)

    dense_part = to_all(dense_own[0], "dp", n_dp)
    attn_w0 = [attn_own[0]] + exchange(lambda s: attn_own[0], "tensor", n_tensor)
    attn_w1 = lax.all_gather(attn_own[1], "tensor", axis=1, tiled=True)
    dense_w1 = lax.all_gather(dense_own[1], ("dp", "tensor"), axis=1, tiled=True)
    rows = part
    for count, stage in enumerate(stages[::-1]):
        rows = rows + swap(rows, *stage)
        if count == len(stages) - 3:
            rows, attn_w0 = tied(rows, attn_w0)
    rows = rows.astype(f32)

    at = tensor_at.reshape(1).astype(jnp.int32)
    perms = [move_matrix(l % 2 == 1) for l in range(LAYERS)]
    masks = [key_masks(own_size, l % 2 == 1) for l in range(LAYERS)]
    flags = inside_column(own_size)

    rows, dense_part, flags, perms, masks = tied(rows, dense_part, flags, perms, masks)
    dense_part = dense_part.transpose(1, 0, 2, 3).reshape(2, ff_part, D)
    dense_w0 = [dense_part] + exchange(lambda s: dense_part, "tensor", n_tensor)
    h0, *kept0, attn_w0 = attn_forward(0, tokens, perms[0], rows, masks[0], attn_w0, at)
    h0, kept0, attn_w0, dense_w0 = tied(h0, kept0, attn_w0, dense_w0)
    x1, dense_w0 = ffn_forward(0, h0, rows, dense_w0, at)
    h1, *kept1 = attn_forward(1, x1, perms[1], rows, masks[1], [attn_w1], at)

    gh1, dense_g1, vf1, output, image_mean = ffn_both(1, h1, cotangent, rows, dense_w1, flags)
    dense_sum1 = lax.psum_scatter(dense_g1, ("dp", "tensor"), scatter_dimension=1, tiled=True).astype(f32)
    g1, attn_g1, va1 = attn_backward(1, gh1, x1, perms[1], rows, attn_w1, kept1)
    got = exchange(lambda s: own_block(attn_g1, tensor_at ^ s, own_cols, 1), "tensor", n_tensor)

    gh0, dense_g0, vf0 = ffn_both(0, h0, g1, rows, dense_w0)
    gh0, dense_g0, vf0, got = tied(gh0, dense_g0, vf0, got)
    attn_t1 = total(own_block(attn_g1, tensor_at, own_cols, 1), got)
    got = exchange(lambda s: own_block(dense_g0, tensor_at ^ s, ff_part, 1), "tensor", n_tensor)
    parts1 = lax.all_to_all(attn_t1.astype(bf16).reshape(n_dp, -1, D), "dp", 0, 0)
    dmix, attn_g0, va0 = attn_backward_core(0, gh0, perms[0], attn_w0, kept0)
    dmix, attn_g0, va0, got, parts1 = tied(dmix, attn_g0, va0, got, parts1)
    dense_t0 = total(own_block(dense_g0, tensor_at, ff_part, 1), got).astype(bf16)
    got = exchange(lambda s: own_block(attn_g0, tensor_at ^ s, own_cols, 1), "tensor", n_tensor)
    blocks = dense_t0.reshape(2, n_dp, ub_own, D).transpose(1, 0, 2, 3)
    blocks = lax.all_to_all(blocks, "dp", 0, 0)
    whole1 = to_all(jnp.sum(parts1.astype(f32), axis=0).astype(bf16), "dp", n_dp)
    g0, vn0 = attn_backward_norm(0, gh0, tokens, perms[0], rows, attn_w0, dmix)
    g0, vn0, got, blocks, whole1, dense_sum1 = tied(g0, vn0, got, blocks, whole1, dense_sum1)
    attn_t0 = total(own_block(attn_g0, tensor_at, own_cols, 1), got)
    dense_sum0 = jnp.sum(blocks.astype(f32), axis=0)

    small = vf0 + vf1 + va0 + va1 + vn0
    for stage in bits_of("tensor", n_tensor)[::-1]:
        small = small + swap(small, *stage)
    small_rows = -(-small.size // (D * n_dp))
    small = small.reshape(-1, D)
    small = jnp.pad(small, ((0, small_rows * n_dp - small.shape[0]), (0, 0))).reshape(n_dp, small_rows, D)
    matrices = attn_t0.reshape(n_dp, -1, D)
    matrix_rows = matrices.shape[1]
    sums = sum_parts(jnp.concatenate([matrices.astype(bf16), small.astype(bf16)], axis=1), "dp")
    whole0 = to_all(sums.astype(bf16), "dp", n_dp)
    attn_all = [
        rows.astype(f32).reshape(4, own_cols, D) for rows in (whole0[:, :matrix_rows], whole1)
    ]
    attn_all = jnp.stack(attn_all)
    small = whole0[:, matrix_rows:].astype(f32).reshape(-1, D)[: 8 * 6].reshape(8, 6 * D)
    vectors_grad = lax.dynamic_slice(small, (0, own * vec_own), (LAYERS, vec_own))
    up_bias_grad = jnp.concatenate(
        [
            lax.dynamic_slice(small, (2, tensor_at * ff_part + dp_at * ub_own), (1, ub_own)),
            lax.dynamic_slice(small, (3, own * ub_own), (1, ub_own)),
        ]
    )
    mix_bias_grad = jnp.stack(
        [lax.dynamic_slice(small, (2, FF + c * D + tensor_at * own_cols), (LAYERS, own_cols)) for c in range(2)], axis=1
    )
    bias_table_grad = jnp.stack(
        [lax.dynamic_slice(small, table_at[l], (1, own_heads * 256)).reshape(own_heads, 256)[:, :TABLE].T for l in range(LAYERS)]
    )
    return (
        output,
        image_mean.reshape(local_images, D),
        g0,
        vectors_grad,
        attn_all[:, :3].transpose(0, 3, 1, 2),
        mix_bias_grad,
        bias_table_grad,
        attn_all[:, 3],
        jnp.stack([dense_sum0[0].T, dense_sum1[0].T]),
        up_bias_grad,
        jnp.stack([dense_sum0[1], dense_sum1[1]]),
    )


def solution(mesh):
    n_dp, n_tensor = mesh.shape["dp"], mesh.shape["tensor"]
    both = ("dp", "tensor")
    placed = (
        P(both, None),
        P(both, None),
        P("dp", None),
        P(None, both),
        P(None, None, None, "tensor"),
        P(None, None, "tensor"),
        P(None, None, "tensor"),
        P(None, "tensor", None),
        P(None, None, both),
        P(None, both),
        P(None, both, None),
    )
    return jax.shard_map(
        lambda *args: body(n_dp, n_tensor, *args),
        mesh=mesh,
        in_specs=placed,
        out_specs=(
            P(both, None),
            P(both, None),
            P(both, None),
            P(None, both),
            P(None, None, None, "tensor"),
            P(None, None, "tensor"),
            P(None, None, "tensor"),
            P(None, "tensor", None),
            P(None, None, both),
            P(None, both),
            P(None, both, None),
        ),
        check_vma=False,
    )
```

time: 408 us -> 352 us (0.86)
  waiting for transfers between devices: 82.8 us -> 39.7 us
  local copies, waits for them, and re-layouts: 43.1 us -> 19.6 us
  between operations: 1.72 us -> 14.7 us
  other arithmetic: 31.2 us -> 19 us
  Pallas kernels: 193 us -> 201 us
  starting transfers between devices: 47.5 us -> 53.3 us
  matrix products: 4.58 us -> 0 us
    ppermute x51 -> x22, waiting for transfers between devices: 82.8 us -> 14.7 us  [swap(): return lax.ppermute(rows, axis, [(i, i ^ bit) for i in range(size)])]
    all_to_all x0 -> x6, starting transfers between devices: none -> 30.2 us  [the longest x3 13.5 us: to_all(): lax.all_to_all(jnp.broadcast_to(rows[None], (size,) + rows.shape), axis,...]
    ppermute x51 -> x22, starting transfers between devices: 47.5 us -> 22.5 us  [swap(): return lax.ppermute(rows, axis, [(i, i ^ bit) for i in range(size)])]
    all_to_all x0 -> x6, waiting for transfers between devices: none -> 24.9 us  [the longest x3 15.8 us: to_all(): lax.all_to_all(jnp.broadcast_to(rows[None], (size,) + rows.shape), axis,...]
    concatenate x19 -> x3, other arithmetic: 13.1 us -> 2.51 us  [the longest x1 1.17 us: body(): attn_own = jnp.concatenate([mix_own, out_weight[:, None]], axis=1)]
    pallas_call x7 -> x8, Pallas kernels: 193 us -> 201 us  [the longest x2 63.9 us: attn_forward(): call(lambda *refs: attn_fwd_kernel(layer, pieces, *refs), 'attn_fwd', ima...]
    slice x32 -> x8, local copies, waits for them, and re-layouts: 9.49 us -> 2.24 us  [the longest x1 0.77 us: body(): attn_w1 = lax.all_gather(attn_own[1], 'tensor', axis=1, tiled=True)]
    reshape x20 -> x3, local copies, waits for them, and re-layouts: 7.68 us -> 0.89 us  [the longest x1 0.87 us: body(): blocks = dense_t0.reshape(2, n_dp, ub_own, D).transpose(1, 0, 2, 3)]
  transfers between devices with their start and end apart: 51 -> 31, of which waited for: 25 -> 10; matrix products, arithmetic and copies ran while one was open for 17% -> 6% of each run, Pallas kernels for 18% -> 51%
where the time goes in v2:
time: 352 us; the launch traced here: 348 us
  Pallas kernels  201 us (57%)
  starting transfers between devices  53.3 us (15%)
  waiting for transfers between devices  39.7 us (11%)
  local copies, waits for them, and re-layouts  19.6 us (6%)
  other arithmetic  19 us (5%)
  between operations  14.7 us (4%)
    pallas_call x2, Pallas kernels, attn_forward(): call(lambda *refs: attn_fwd_kernel(layer, pieces, *refs), 'attn_fwd', ima...  63.9 us
    pallas_call x2, Pallas kernels, ffn_both(): call(lambda *refs: ffn_both_kernel(layer, with_output, *refs), 'ffn_both_...  45.7 us
    pallas_call x1, Pallas kernels, attn_backward(): call(lambda *refs: attn_bwd_kernel(layer, *refs), 'attn_bwd', images, [by...  38.9 us
    pallas_call x1, Pallas kernels, attn_backward_core(): call(lambda *refs: attn_core_kernel(layer, *refs), 'attn_core', images, [...  33.7 us
    ppermute x22, starting transfers between devices, swap(): return lax.ppermute(rows, axis, [(i, i ^ bit) for i in range(size)])  22.5 us
    all_to_all x3, waiting for transfers between devices, to_all(): lax.all_to_all(jnp.broadcast_to(rows[None], (size,) + rows.shape), axis,...  15.8 us
    ppermute x22, waiting for transfers between devices, swap(): return lax.ppermute(rows, axis, [(i, i ^ bit) for i in range(size)])  14.7 us
    all_to_all x3, starting transfers between devices, to_all(): lax.all_to_all(jnp.broadcast_to(rows[None], (size,) + rows.shape), axis,...  13.5 us
  transfers between devices with their start and end apart: 31, of which 10 were waited for; matrix products, arithmetic and copies ran while one was open for 6% of the time, Pallas kernels for 51%

profile of v2, /device:TPU:0, one launch (start us, length us, event | category | flops | bytes accessed | tf_op | source)
XLA Modules:
  0.0 347.8 jit_solution(5761951883530897651)
XLA Ops:
  17.5 2.6 collective-permute-start.4
  20.1 2.7 collective-permute-start
  23.7 3.8 %all-to-all-start = ((bf16[8,2,48,384]{3,2,1,0:T(8,128)(2,1)}), bf16[8,2,48,384]{3,2,1,0:T(8,128)(2,1)S(1)}, u32[]{:S(2)}, u32[]{:S(2)}) async-start(bf16[8,2,48,384]{3,2,1,0:T(8,128)(2,1)} %broadcast_in_dim.25), calls=%async_computation | async-start | bytes 1179648 | tf_op jit(solution)/shard_map/all_to_all | solution.py:597
  28.4 2.3 fusion
  32.9 5.3 %collective-permute-done.1 = bf16[8,2304]{1,0:T(8,128)(2,1)S(1)} collective-permute-done((bf16[8,2304]{1,0:T(8,128)(2,1)S(1)}, bf16[8,2304]{1,0:T(8,128)(2,1)S(1)}, u32[]{:S(2)}, u32[]{:S(2)}) %collective-permute-start.1) | collective-permute-done | bytes 36896 | tf_op jit(solution)/shard_map/ppermute | solution.py:569
  44.2 2.1 collective-permute-done.6
  53.1 32.0 %attn_fwd.2 = (f32[1568,384]{1,0:T(8,128)}, bf16[2048,384]{1,0:T(8,128)(2,1)}, bf16[2048,1152]{1,0:T(8,128)(2,1)}, bf16[2,8,3,128,512]{4,3,2,1,0:T(8,128)(2,1)},...) custom-call(bf16[1568,384]{1,0:T(8,128)(2,1)} %refs_1_.3, bf16[1024,784]{1,0:T(8,128)(2,1)} %get-tuple-element.90.refs_1_.refs_2_, ...), custom_call_target="tpu_custom_call" | custom-call | flops 100000000 | bytes 100000 | tf_op jit(solution)/shard_map/attn_fwd/pallas_call | solution.py:428
  86.3 9.3 %ffn_fwd.1 = (f32[1568,384]{1,0:T(8,128)}, bf16[2,1536,384]{2,1,0:T(8,128)(2,1)}) custom-call(f32[1568,384]{1,0:T(8,128)} %get-tuple-element.104.refs_0_, f32[8,2304]{1,0:T(8,128)} %add_convert_fusion.4.refs_2_.refs_1_.refs_3_, bf16[2,384,384]{2,1,0:T(8,128)(2,1)} %bitcast.78, bf16[2,384,384]{2,1,0:T(8,128)(2,1)} %copy-done.6, ...), custom_call_target="tpu_custom_call" | custom-call | flops 100000000 | bytes 100000 | tf_op jit(solution)/shard_map/ffn_fwd/pallas_call | solution.py:507
  95.6 31.8 %attn_fwd.3 = (f32[1568,384]{1,0:T(8,128)}, bf16[2048,384]{1,0:T(8,128)(2,1)}, bf16[2048,1152]{1,0:T(8,128)(2,1)}, bf16[2,8,3,128,512]{4,3,2,1,0:T(8,128)(2,1)}, bf16[1568,384]{1,0:T(8,128)(2,1)}) custom-call(f32[1568,384]{1,0:T(8,128)} %get-tuple-element.109.refs_0_.refs_1_, bf16[1024,784]{1,0:T(8,128)(2,1)} %get-tuple-element.110.refs_1_.refs_2_, ...), custom_call_target="tpu_custom_call" | custom-call | flops 100000000 | bytes 100000 | tf_op jit(solution)/shard_map/attn_fwd/pallas_call | solution.py:428
  127.5 23.9 %ffn_both_out.1 = (f32[1568,384]{1,0:T(8,128)}, bf16[2,1536,384]{2,1,0:T(8,128)(2,1)}, f32[8,2304]{1,0:T(8,128)}, bf16[1568,384]{1,0:T(8,128)(2,1)}, f32[2,1,384]{2,1,0:T(1,128)}) custom-call(f32[1568,384]{1,0:T(8,128)} %get-tuple-element.112.refs_0_, bf16[1568,384]{1,0:T(8,128)(2,1)} %refs_1_.2, f32[8,2304]{1,0:T(8,128)} %add_convert_fusion.4.refs_2_.refs_1_.refs_3_, ...), custom_call_target="tpu_custom_call" | custom-call | flops 100000000 | bytes 100000 | tf_op jit(solution)/shard_map/ffn_both_out/pallas_call | solution.py:535
  151.5 38.9 %attn_bwd.1 = (f32[1568,384]{1,0:T(8,128)}, bf16[4,384,384]{2,1,0:T(8,128)(2,1)}, f32[8,2304]{1,0:T(8,128)}) custom-call(f32[1568,384]{1,0:T(8,128)} %get-tuple-element.116.refs_0_, f32[1568,384]{1,0:T(8,128)} %get-tuple-element.109.refs_0_.refs_1_, bf16[1024,784]{1,0:T(8,128)(2,1)} %get-tuple-element.110.refs_1_.refs_2_, ...), custom_call_target="tpu_custom_call" | custom-call | flops 100000000 | bytes 100000 | tf_op jit(solution)/shard_map/attn_bwd/pallas_call | solution.py:449
  193.6 21.8 %ffn_both.1 = (f32[1568,384]{1,0:T(8,128)}, bf16[2,1536,384]{2,1,0:T(8,128)(2,1)}, f32[8,2304]{1,0:T(8,128)}) custom-call(f32[1568,384]{1,0:T(8,128)} %get-tuple-element.104.refs_0_, f32[1568,384]{1,0:T(8,128)} %get-tuple-element.121.refs_1_, f32[8,2304]{1,0:T(8,128)} %add_convert_fusion.4.refs_2_.refs_1_.refs_3_, ...), custom_call_target="tpu_custom_call" | custom-call | flops 100000000 | bytes 100000 | tf_op jit(solution)/shard_map/ffn_both/pallas_call | solution.py:535
  215.5 2.5 constant_dynamic-slice_fusion.3
  222.0 7.2 %all-to-all-start.1 = ((bf16[8,48,384]{2,1,0:T(8,128)(2,1)}), bf16[8,48,384]{2,1,0:T(8,128)(2,1)S(1)}, u32[]{:S(2)}, u32[]{:S(2)}) async-start(bf16[8,48,384]{2,1,0:T(8,128)(2,1)} %bitcast.19), calls=%async_computation.1 | async-start | bytes 589824 | tf_op jit(solution)/shard_map/all_to_all | solution.py:675
  229.2 33.7 %attn_core.1 = (bf16[2048,1152]{1,0:T(8,128)(2,1)}, bf16[4,384,384]{2,1,0:T(8,128)(2,1)}, f32[8,2304]{1,0:T(8,128)}) custom-call(f32[1568,384]{1,0:T(8,128)} %get-tuple-element.127.refs_0_, bf16[1024,784]{1,0:T(8,128)(2,1)} %get-tuple-element.90.refs_1_.refs_2_, bf16[4,384,384]{2,1,0:T(8,128)(2,1)} %get-tuple-element.128.refs_2_.refs_4_, ...), custom_call_target="tpu_custom_call" | custom-call | flops 100000000 | bytes 100000 | tf_op jit(solution)/shard_map/attn_core/pallas_call | solution.py:470
  263.7 6.0 %all-to-all-start.3 = ((bf16[8,48,384]{2,1,0:T(8,128)(2,1)}), bf16[8,48,384]{2,1,0:T(8,128)(2,1)S(1)}, u32[]{:S(2)}, u32[]{:S(2)}) async-start(bf16[8,48,384]{2,1,0:T(8,128)(2,1)} %broadcast_in_dim.28), calls=%async_computation.3 | async-start | bytes 589824 | tf_op jit(solution)/shard_map/all_to_all | solution.py:597
  272.1 7.2 %all-to-all-done.3 = bf16[8,48,384]{2,1,0:T(8,128)(2,1)S(1)} async-done(((bf16[8,48,384]{2,1,0:T(8,128)(2,1)}), bf16[8,48,384]{2,1,0:T(8,128)(2,1)S(1)}, u32[]{:S(2)}, u32[]{:S(2)}) %all-to-all-start.3) | async-done | bytes 294944 | tf_op jit(solution)/shard_map/all_to_all | solution.py:597
  279.3 3.6 %all-to-all-start.2 = ((bf16[8,2,48,384]{3,2,1,0:T(8,128)(2,1)}), bf16[8,2,48,384]{3,2,1,0:T(8,128)(2,1)S(1)}, u32[]{:S(2)}, u32[]{:S(2)}) async-start(bf16[8,2,48,384]{3,2,1,0:T(8,128)(2,1)} %bitcast.67), calls=%async_computation.2 | async-start | bytes 1179648 | tf_op jit(solution)/shard_map/all_to_all | solution.py:681
  285.1 10.0 %attn_norm.1 = (f32[1568,384]{1,0:T(8,128)}, f32[8,2304]{1,0:T(8,128)}) custom-call(f32[1568,384]{1,0:T(8,128)} %get-tuple-element.127.refs_0_, bf16[1568,384]{1,0:T(8,128)(2,1)} %refs_1_.3, bf16[1024,784]{1,0:T(8,128)(2,1)} %get-tuple-element.90.refs_1_.refs_2_, f32[8,2304]{1,0:T(8,128)} %add_convert_fusion.4.refs_2_.refs_1_.refs_3_, ...), custom_call_target="tpu_custom_call" | custom-call | flops 100000000 | bytes 100000 | tf_op jit(solution)/shard_map/attn_norm/pallas_call | solution.py:486
  296.0 2.7 collective-permute-done.19
  306.3 6.0 %all-to-all-start.4 = ((bf16[8,54,384]{2,1,0:T(8,128)(2,1)}), bf16[8,54,384]{2,1,0:T(8,128)(2,1)S(1)}, u32[]{:S(2)}, u32[]{:S(2)}) async-start(bf16[8,54,384]{2,1,0:T(8,128)(2,1)} %pad_maximum_fusion.1), calls=%async_computation.5 | async-start | bytes 688128 | tf_op jit(solution)/shard_map/all_to_all | solution.py:601
  312.9 9.1 %all-to-all-done.4 = bf16[8,54,384]{2,1,0:T(8,128)(2,1)S(1)} async-done(((bf16[8,54,384]{2,1,0:T(8,128)(2,1)}), bf16[8,54,384]{2,1,0:T(8,128)(2,1)S(1)}, u32[]{:S(2)}, u32[]{:S(2)}) %all-to-all-start.4) | async-done | bytes 331808 | tf_op jit(solution)/shard_map/all_to_all | solution.py:601
  322.9 3.6 %all-to-all-start.5 = ((bf16[8,54,384]{2,1,0:T(8,128)(2,1)}), bf16[8,54,384]{2,1,0:T(8,128)(2,1)S(1)}, u32[]{:S(2)}, u32[]{:S(2)}) async-start(bf16[8,54,384]{2,1,0:T(8,128)(2,1)} %broadcast_in_dim.29), calls=%async_computation.6 | async-start | bytes 688128 | tf_op jit(solution)/shard_map/all_to_all | solution.py:597
  327.9 8.6 %all-to-all-done.5 = bf16[8,54,384]{2,1,0:T(8,128)(2,1)S(1)} async-done(((bf16[8,54,384]{2,1,0:T(8,128)(2,1)}), bf16[8,54,384]{2,1,0:T(8,128)(2,1)S(1)}, u32[]{:S(2)}, u32[]{:S(2)}) %all-to-all-start.5) | async-done | bytes 331808 | tf_op jit(solution)/shard_map/all_to_all | solution.py:597
  (175 shorter events, 56.3 us)
Async XLA Ops:
  7.2 88.5 %all-gather.5.cloned.1.call-start = ((), (), s32[]{:S(2)}) async-start(), calls=%async_computation.8 | async-start | bytes 1474560 | tf_op jit(solution)/shard_map/all_gather | solution.py:644
  15.5 112.0 %all-gather.7.cloned.1.call-start = ((), (), s32[]{:S(2)}) async-start(), calls=%async_computation.9 | async-start | bytes 2433024 | tf_op jit(solution)/shard_map/all_gather | solution.py:645
  16.3 26.0 %collective-permute-start.3 = (bf16[4,96,384]{2,1,0:T(8,128)(2,1)S(1)}, bf16[4,96,384]{2,1,0:T(8,128)(2,1)S(1)}, u32[]{:S(2)}, u32[]{:S(2)}) collective-permute-start(bf16[4,96,384]{2,1,0:T(8,128)(2,1)S(1)} %get-tuple-element.93.refs_4_), channel_id=1, source_target_pairs={{0,1},{1,0},{2,3},{3,2},{4,5},{5,4},{6,7},{7,6},{8,9},{9,8},{10,11... | collective-permute-start | bytes 884744 | tf_op jit(solution)/shard_map/ppermute | solution.py:569
  17.5 24.8 %collective-permute-start.4 = (bf16[4,96,384]{2,1,0:T(8,128)(2,1)S(1)}, bf16[4,96,384]{2,1,0:T(8,128)(2,1)S(1)}, u32[]{:S(2)}, u32[]{:S(2)}) collective-permute-start(bf16[4,96,384]{2,1,0:T(8,128)(2,1)S(1)} %get-tuple-element.93.refs_4_), channel_id=1, source_target_pairs={{0,2},{1,3},{2,0},{3,1},{4,6},{5,7},{6,4},{7,5},{8,10},{9,11},{10,... | collective-permute-start | bytes 884744 | tf_op jit(solution)/shard_map/ppermute | solution.py:569
  20.0 22.3 %collective-permute-start.5 = (bf16[4,96,384]{2,1,0:T(8,128)(2,1)S(1)}, bf16[4,96,384]{2,1,0:T(8,128)(2,1)S(1)}, u32[]{:S(2)}, u32[]{:S(2)}) collective-permute-start(bf16[4,96,384]{2,1,0:T(8,128)(2,1)S(1)} %get-tuple-element.93.refs_4_), channel_id=1, source_target_pairs={{0,3},{1,2},{2,1},{3,0},{4,7},{5,6},{6,5},{7,4},{8,11},{9,10},{10,... | collective-permute-start | bytes 884744 | tf_op jit(solution)/shard_map/ppermute | solution.py:569
  23.7 24.6 %all-to-all-start = ((bf16[8,2,48,384]{3,2,1,0:T(8,128)(2,1)}), bf16[8,2,48,384]{3,2,1,0:T(8,128)(2,1)S(1)}, u32[]{:S(2)}, u32[]{:S(2)}) async-start(bf16[8,2,48,384]{3,2,1,0:T(8,128)(2,1)} %broadcast_in_dim.25), calls=%async_computation | async-start | bytes 1179648 | tf_op jit(solution)/shard_map/all_to_all | solution.py:597
  27.5 267.5 %reduce-scatter.2.cloned.1.call-start = ((), (), s32[]{:S(2)}) async-start(), calls=%async_computation.7 | async-start | bytes 2433024 | tf_op jit(solution)/shard_map/reduce_scatter | solution.py:667
  49.7 35.5 %collective-permute-start.10 = (bf16[2,384,384]{2,1,0:T(8,128)(2,1)S(1)}, bf16[2,384,384]{2,1,0:T(8,128)(2,1)S(1)}, u32[]{:S(2)}, u32[]{:S(2)}) collective-permute-start(bf16[2,384,384]{2,1,0:T(8,128)(2,1)S(1)} %bitcast.75), channel_id=1, source_target_pairs={{0,3},{1,2},{2,1},{3,0},{4,7},{5,6},{6,5},{7,4},{8,11},{9,10},{10,... | collective-permute-start | bytes 1769480 | tf_op jit(solution)/shard_map/ppermute | solution.py:569
  51.2 33.9 %collective-permute-start.8 = (bf16[2,384,384]{2,1,0:T(8,128)(2,1)S(1)}, bf16[2,384,384]{2,1,0:T(8,128)(2,1)S(1)}, u32[]{:S(2)}, u32[]{:S(2)}) collective-permute-start(bf16[2,384,384]{2,1,0:T(8,128)(2,1)S(1)} %bitcast.76), channel_id=1, source_target_pairs={{0,1},{1,0},{2,3},{3,2},{4,5},{5,4},{6,7},{7,6},{8,9},{9,8},{10,11... | collective-permute-start | bytes 1769480 | tf_op jit(solution)/shard_map/ppermute | solution.py:569
  51.6 33.6 %collective-permute-start.9 = (bf16[2,384,384]{2,1,0:T(8,128)(2,1)S(1)}, bf16[2,384,384]{2,1,0:T(8,128)(2,1)S(1)}, u32[]{:S(2)}, u32[]{:S(2)}) collective-permute-start(bf16[2,384,384]{2,1,0:T(8,128)(2,1)S(1)} %bitcast.77), channel_id=1, source_target_pairs={{0,2},{1,3},{2,0},{3,1},{4,6},{5,7},{6,4},{7,5},{8,10},{9,11},{10,... | collective-permute-start | bytes 1769480 | tf_op jit(solution)/shard_map/ppermute | solution.py:569
  191.7 23.7 %collective-permute-start.11 = (bf16[4,96,384]{2,1,0:T(8,128)(2,1)S(1)}, bf16[4,96,384]{2,1,0:T(8,128)(2,1)S(1)}, u32[]{:S(2)}, u32[]{:S(2)}) collective-permute-start(bf16[4,96,384]{2,1,0:T(8,128)(2,1)S(1)} %get-tuple-element.215), channel_id=1, source_target_pairs={{0,1},{1,0},{2,3},{3,2},{4,5},{5,4},{6,7},{7,6},{8,9},{9,8},{10,11... | collective-permute-start | bytes 884744 | tf_op jit(solution)/shard_map/ppermute | solution.py:569
  191.7 23.7 %collective-permute-start.12 = (bf16[4,96,384]{2,1,0:T(8,128)(2,1)S(1)}, bf16[4,96,384]{2,1,0:T(8,128)(2,1)S(1)}, u32[]{:S(2)}, u32[]{:S(2)}) collective-permute-start(bf16[4,96,384]{2,1,0:T(8,128)(2,1)S(1)} %get-tuple-element.214), channel_id=1, source_target_pairs={{0,2},{1,3},{2,0},{3,1},{4,6},{5,7},{6,4},{7,5},{8,10},{9,11},{10,... | collective-permute-start | bytes 884744 | tf_op jit(solution)/shard_map/ppermute | solution.py:569
  193.5 21.9 %collective-permute-start.13 = (bf16[4,96,384]{2,1,0:T(8,128)(2,1)S(1)}, bf16[4,96,384]{2,1,0:T(8,128)(2,1)S(1)}, u32[]{:S(2)}, u32[]{:S(2)}) collective-permute-start(bf16[4,96,384]{2,1,0:T(8,128)(2,1)S(1)} %get-tuple-element.213), channel_id=1, source_target_pairs={{0,3},{1,2},{2,1},{3,0},{4,7},{5,6},{6,5},{7,4},{8,11},{9,10},{10,... | collective-permute-start | bytes 884744 | tf_op jit(solution)/shard_map/ppermute | solution.py:569
  218.0 44.9 %collective-permute-start.14 = (bf16[2,384,384]{2,1,0:T(8,128)(2,1)}, bf16[2,384,384]{2,1,0:T(8,128)(2,1)S(1)}, u32[]{:S(2)}, u32[]{:S(2)}) collective-permute-start(bf16[2,384,384]{2,1,0:T(8,128)(2,1)} %get-tuple-element.209), channel_id=1, source_target_pairs={{0,1},{1,0},{2,3},{3,2},{4,5},{5,4},{6,7},{7,6},{8,9},{9,8},{10,11... | collective-permute-start | bytes 1769480 | tf_op jit(solution)/shard_map/ppermute | solution.py:569
  218.3 44.6 %collective-permute-start.15 = (bf16[2,384,384]{2,1,0:T(8,128)(2,1)S(1)}, bf16[2,384,384]{2,1,0:T(8,128)(2,1)S(1)}, u32[]{:S(2)}, u32[]{:S(2)}) collective-permute-start(bf16[2,384,384]{2,1,0:T(8,128)(2,1)S(1)} %get-tuple-element.208), channel_id=1, source_target_pairs={{0,2},{1,3},{2,0},{3,1},{4,6},{5,7},{6,4},{7,5},{8,10},{9,11},{10,... | collective-permute-start | bytes 1769480 | tf_op jit(solution)/shard_map/ppermute | solution.py:569
  220.1 42.9 %collective-permute-start.16 = (bf16[2,384,384]{2,1,0:T(8,128)(2,1)S(1)}, bf16[2,384,384]{2,1,0:T(8,128)(2,1)S(1)}, u32[]{:S(2)}, u32[]{:S(2)}) collective-permute-start(bf16[2,384,384]{2,1,0:T(8,128)(2,1)S(1)} %get-tuple-element.207), channel_id=1, source_target_pairs={{0,3},{1,2},{2,1},{3,0},{4,7},{5,6},{6,5},{7,4},{8,11},{9,10},{10,... | collective-permute-start | bytes 1769480 | tf_op jit(solution)/shard_map/ppermute | solution.py:569
  222.0 40.9 %all-to-all-start.1 = ((bf16[8,48,384]{2,1,0:T(8,128)(2,1)}), bf16[8,48,384]{2,1,0:T(8,128)(2,1)S(1)}, u32[]{:S(2)}, u32[]{:S(2)}) async-start(bf16[8,48,384]{2,1,0:T(8,128)(2,1)} %bitcast.19), calls=%async_computation.1 | async-start | bytes 589824 | tf_op jit(solution)/shard_map/all_to_all | solution.py:675
  263.7 15.5 %all-to-all-start.3 = ((bf16[8,48,384]{2,1,0:T(8,128)(2,1)}), bf16[8,48,384]{2,1,0:T(8,128)(2,1)S(1)}, u32[]{:S(2)}, u32[]{:S(2)}) async-start(bf16[8,48,384]{2,1,0:T(8,128)(2,1)} %broadcast_in_dim.28), calls=%async_computation.3 | async-start | bytes 589824 | tf_op jit(solution)/shard_map/all_to_all | solution.py:597
  279.3 19.5 %all-to-all-start.2 = ((bf16[8,2,48,384]{3,2,1,0:T(8,128)(2,1)}), bf16[8,2,48,384]{3,2,1,0:T(8,128)(2,1)S(1)}, u32[]{:S(2)}, u32[]{:S(2)}) async-start(bf16[8,2,48,384]{3,2,1,0:T(8,128)(2,1)} %bitcast.67), calls=%async_computation.2 | async-start | bytes 1179648 | tf_op jit(solution)/shard_map/all_to_all | solution.py:681
  283.0 13.0 %collective-permute-start.17 = (bf16[4,96,384]{2,1,0:T(8,128)(2,1)S(1)}, bf16[4,96,384]{2,1,0:T(8,128)(2,1)S(1)}, u32[]{:S(2)}, u32[]{:S(2)}) collective-permute-start(bf16[4,96,384]{2,1,0:T(8,128)(2,1)S(1)} %get-tuple-element.212), channel_id=1, source_target_pairs={{0,1},{1,0},{2,3},{3,2},{4,5},{5,4},{6,7},{7,6},{8,9},{9,8},{10,11... | collective-permute-start | bytes 884744 | tf_op jit(solution)/shard_map/ppermute | solution.py:569
  283.1 12.9 %collective-permute-start.18 = (bf16[4,96,384]{2,1,0:T(8,128)(2,1)S(1)}, bf16[4,96,384]{2,1,0:T(8,128)(2,1)}, u32[]{:S(2)}, u32[]{:S(2)}) collective-permute-start(bf16[4,96,384]{2,1,0:T(8,128)(2,1)S(1)} %get-tuple-element.211), channel_id=1, source_target_pairs={{0,2},{1,3},{2,0},{3,1},{4,6},{5,7},{6,4},{7,5},{8,10},{9,11},{10,... | collective-permute-start | bytes 884744 | tf_op jit(solution)/shard_map/ppermute | solution.py:569
  285.0 13.7 %collective-permute-start.19 = (bf16[4,96,384]{2,1,0:T(8,128)(2,1)S(1)}, bf16[4,96,384]{2,1,0:T(8,128)(2,1)}, u32[]{:S(2)}, u32[]{:S(2)}) collective-permute-start(bf16[4,96,384]{2,1,0:T(8,128)(2,1)S(1)} %get-tuple-element.210), channel_id=1, source_target_pairs={{0,3},{1,2},{2,1},{3,0},{4,7},{5,6},{6,5},{7,4},{8,11},{9,10},{10,... | collective-permute-start | bytes 884744 | tf_op jit(solution)/shard_map/ppermute | solution.py:569
  306.3 15.8 %all-to-all-start.4 = ((bf16[8,54,384]{2,1,0:T(8,128)(2,1)}), bf16[8,54,384]{2,1,0:T(8,128)(2,1)S(1)}, u32[]{:S(2)}, u32[]{:S(2)}) async-start(bf16[8,54,384]{2,1,0:T(8,128)(2,1)} %pad_maximum_fusion.1), calls=%async_computation.5 | async-start | bytes 688128 | tf_op jit(solution)/shard_map/all_to_all | solution.py:601
  322.9 13.6 %all-to-all-start.5 = ((bf16[8,54,384]{2,1,0:T(8,128)(2,1)}), bf16[8,54,384]{2,1,0:T(8,128)(2,1)S(1)}, u32[]{:S(2)}, u32[]{:S(2)}) async-start(bf16[8,54,384]{2,1,0:T(8,128)(2,1)} %broadcast_in_dim.29), calls=%async_computation.6 | async-start | bytes 688128 | tf_op jit(solution)/shard_map/all_to_all | solution.py:597
  (31 other events, 316.1 us)
Sparse Core Ops, SparseCore 0:
  15.7 26.0 all-gather.4
  45.3 60.0 all-gather.6
  151.6 106.7 reduce-scatter.1

commit v3 on v2

--- a/solution.py
+++ b/solution.py
@@ -59,6 +59,24 @@
     return source
 
 
+def moved_rows(shifted):
+    moves = []
+    for a in range(GRID):
+        for b in range(GRID):
+            wide, here = (a * GRID + b) * PAD, (a * GRID + b) * CELLS
+            if not shifted:
+                moves.append((wide, here, CELLS))
+                continue
+            for p in range(WIN):
+                row = a * WIN + p + SHIFT
+                base = ((row // WIN) % GRID) * GRID
+                left = (base + b) * CELLS + (row % WIN) * WIN
+                right = (base + (b + 1) % GRID) * CELLS + (row % WIN) * WIN
+                moves.append((wide + p * WIN, left + SHIFT, WIN - SHIFT))
+                moves.append((wide + p * WIN + WIN - SHIFT, right, SHIFT))
+    return moves
+
+
 def token_places():
     rows = np.zeros((IMG_ROWS,), np.int32)
     cols = np.zeros((IMG_ROWS,), np.int32)
@@ -173,25 +191,38 @@
         rows_ref[row : row + 1, at : at + 256] = column_sum(acc)
 
 
+def move_out(layer, dense_ref, wide_ref):
+    for wide, dense, count in moved_rows(layer % 2 == 1):
+        wide_ref[wide : wide + count, :] = dense_ref[dense : dense + count, :]
+
+
+def move_back(layer, wide_ref, dense_ref):
+    for wide, dense, count in moved_rows(layer % 2 == 1):
+        dense_ref[dense : dense + count, :] = wide_ref[wide : wide + count, :]
+
+
 def attn_fwd_kernel(layer, pieces, *refs):
-    x_ref, perm_ref, sm_ref, mask_ref = refs[:4]
-    w_refs = refs[4 : 4 + pieces]
+    x_ref, sm_ref, mask_ref = refs[:3]
+    w_refs = refs[3 : 3 + pieces]
     if pieces > 1:
-        at_ref, h_ref, a1_ref, qkv_ref, p_ref, ou_ref, w_ref, o_ref, bias_ref = refs[4 + pieces :]
+        at_ref, h_ref, a1_ref, qkv_ref, p_ref, ou_ref, w_ref, dense_ref, wide_ref, bias_ref = refs[3 + pieces :]
     else:
-        h_ref, a1_ref, qkv_ref, p_ref, ou_ref, o_ref, bias_ref = refs[4 + pieces :]
+        h_ref, a1_ref, qkv_ref, p_ref, ou_ref, dense_ref, wide_ref, bias_ref = refs[3 + pieces :]
         w_ref = w_refs[0]
 
     @pl.when(pl.program_id(0) == 0)
     def _():
         spread_tables(layer, sm_ref[...], bias_ref)
+        wide_ref[...] = jnp.zeros_like(wide_ref)
         if pieces > 1:
             merge_pieces(at_ref, w_refs, w_ref)
 
     x = x_ref[...].astype(f32)
     unit, _ = normalize(x)
-    a1 = (unit * sm_ref[layer : layer + 1, vec_lanes(0)] + sm_ref[layer : layer + 1, vec_lanes(2)]).astype(bf16)
-    a1p = nn(perm_ref[...], a1).astype(bf16)
+    a1 = unit * sm_ref[layer : layer + 1, vec_lanes(0)] + sm_ref[layer : layer + 1, vec_lanes(2)]
+    dense_ref[...] = a1
+    move_out(layer, dense_ref, wide_ref)
+    a1p = wide_ref[...].astype(bf16)
     a1_ref[...] = a1p
     qkv_ref[:, 0:D] = (nt(a1p, w_ref[0]) + sm_ref[2 + layer : 3 + layer, vec_lanes(4)]).astype(bf16)
     qkv_ref[:, D : 2 * D] = nt(a1p, w_ref[1]).astype(bf16)
@@ -201,21 +232,25 @@
     def one_pair(pair, carry):
         rows = pl.ds(pl.multiple_of(pair * 128, 128), 128)
         mask = mask_ref[0, pair]
-        mask4 = jnp.concatenate([mask] * 4, axis=1)
         for g in range(TILES):
             q = qkv_ref[rows, 128 * g : 128 * (g + 1)]
             k = qkv_ref[rows, D + 128 * g : D + 128 * (g + 1)]
             v = qkv_ref[rows, 2 * D + 128 * g : 2 * D + 128 * (g + 1)]
-            s = (HDIM**-0.5) * nt(k, spread_heads(q, masks)) + bias_ref[g] + mask4
-            e = jnp.exp(s - jnp.max(s, axis=0, keepdims=True))
-            p = (e * (1.0 / jnp.sum(e, axis=0, keepdims=True))).astype(bf16)
-            p_ref[0, pair, g] = p
-            o = tn(stack_heads(p), spread_heads(v, masks))
-            o_ref[rows, 128 * g : 128 * (g + 1)] = o.astype(bf16)
+            scores = nt(k, spread_heads(q, masks))
+            o = jnp.zeros((128, 128), f32)
+            for head in range(4):
+                here = slice(128 * head, 128 * (head + 1))
+                s = (HDIM**-0.5) * scores[:, here] + bias_ref[g, :, here] + mask
+                e = jnp.exp(s - jnp.max(s, axis=0, keepdims=True))
+                p = (e * (1.0 / jnp.sum(e, axis=0, keepdims=True))).astype(bf16)
+                p_ref[0, pair, g, :, here] = p
+                o += tn(p, v * masks[head])
+            wide_ref[rows, 128 * g : 128 * (g + 1)] = o
         return carry
 
-    lax.fori_loop(0, PAIRS, one_pair, 0)
-    ou = tn(perm_ref[...], o_ref[...]).astype(bf16)
+    lax.fori_loop(0, PAIRS, one_pair, 0, unroll=True)
+    move_back(layer, wide_ref, dense_ref)
+    ou = dense_ref[...].astype(bf16)
     ou_ref[...] = ou
     h_ref[...] = x + (nn(ou, w_ref[3]) + sm_ref[layer : layer + 1, vec_lanes(4)])
 
@@ -227,7 +262,7 @@
         whole_ref[:, pl.ds(start, rows), :] = piece[...]
 
 
-def attn_core_back(layer, gh_ref, perm_ref, w_ref, a1_ref, qkv_ref, p_ref, ou_ref, grad_ref, vg_ref, wacc_ref, do_ref, dm_ref, ds_ref):
+def attn_core_back(layer, gh_ref, w_ref, a1_ref, qkv_ref, p_ref, ou_ref, grad_ref, vg_ref, wacc_ref, dm_ref, ds_ref, dense_ref, wide_ref, do_ref):
     image = pl.program_id(0)
 
     @pl.when(image == 0)
@@ -235,11 +270,14 @@
         wacc_ref[...] = jnp.zeros_like(wacc_ref)
         ds_ref[...] = jnp.zeros_like(ds_ref)
         vg_ref[...] = jnp.zeros_like(vg_ref)
+        wide_ref[...] = jnp.zeros_like(wide_ref)
 
     go = gh_ref[...].astype(bf16)
     vg_ref[layer : layer + 1, vec_lanes(4)] += column_sum(go.astype(f32))
     wacc_ref[3] += tn(ou_ref[...], go)
-    do_ref[...] = nn(perm_ref[...], nt(go, w_ref[3]).astype(bf16)).astype(bf16)
+    dense_ref[...] = nt(go, w_ref[3])
+    move_out(layer, dense_ref, wide_ref)
+    do_ref[...] = wide_ref[...].astype(bf16)
     masks = head_masks()
 
     def one_pair(pair, carry):
@@ -248,22 +286,29 @@
             q = qkv_ref[rows, 128 * g : 128 * (g + 1)]
             k = qkv_ref[rows, D + 128 * g : D + 128 * (g + 1)]
             v = qkv_ref[rows, 2 * D + 128 * g : 2 * D + 128 * (g + 1)]
-            do4 = spread_heads(do_ref[rows, 128 * g : 128 * (g + 1)], masks)
-            pb = p_ref[0, pair, g]
-            p = pb.astype(f32)
-            dp = nt(v, do4)
-            ds = p * (dp - jnp.sum(p * dp, axis=0, keepdims=True))
-            dsb = ds.astype(bf16)
-            ds_ref[g] += dsb.astype(f32)
-            dv = nn(pb, do4)
-            dk = (HDIM**-0.5) * nn(dsb, spread_heads(q, masks))
-            dq = (HDIM**-0.5) * tn(stack_heads(dsb), spread_heads(k, masks))
-            dm_ref[rows, 128 * g : 128 * (g + 1)] = dq.astype(bf16)
+            do = do_ref[rows, 128 * g : 128 * (g + 1)]
+            dq = jnp.zeros((128, 128), f32)
+            parts = []
+            for two in range(2):
+                do2 = spread_heads(do, masks[2 * two : 2 * two + 2])
+                dp2 = nt(v, do2)
+                for one in range(2):
+                    head = 2 * two + one
+                    here = slice(128 * head, 128 * (head + 1))
+                    p = p_ref[0, pair, g, :, here].astype(f32)
+                    dp = dp2[:, 128 * one : 128 * (one + 1)]
+                    ds = (p * (dp - jnp.sum(p * dp, axis=0, keepdims=True))).astype(bf16)
+                    ds_ref[g, :, here] += ds.astype(f32)
+                    dq += tn(ds, k * masks[head])
+                    parts.append(ds)
+            dv = nn(p_ref[0, pair, g], spread_heads(do, masks))
+            dk = (HDIM**-0.5) * nn(jnp.concatenate(parts, axis=1), spread_heads(q, masks))
+            dm_ref[rows, 128 * g : 128 * (g + 1)] = ((HDIM**-0.5) * dq).astype(bf16)
             dm_ref[rows, D + 128 * g : D + 128 * (g + 1)] = dk.astype(bf16)
             dm_ref[rows, 2 * D + 128 * g : 2 * D + 128 * (g + 1)] = dv.astype(bf16)
         return carry
 
-    lax.fori_loop(0, PAIRS, one_pair, 0)
+    lax.fori_loop(0, PAIRS, one_pair, 0, unroll=True)
     a1p = a1_ref[...]
     for c in range(3):
         dm = dm_ref[:, D * c : D * (c + 1)]
@@ -277,30 +322,31 @@
         grad_ref[...] = wacc_ref[...].astype(bf16)
 
 
-def attn_norm_back(layer, gh_ref, x_ref, perm_ref, sm_ref, w_ref, dm_ref, g_ref, vg_ref):
-    da = nn(dm_ref[:, 0:D], w_ref[0]) + nn(dm_ref[:, D : 2 * D], w_ref[1]) + nn(dm_ref[:, 2 * D : 3 * D], w_ref[2])
-    da1 = tn(perm_ref[...], da.astype(bf16))
+def attn_norm_back(layer, gh_ref, x_ref, sm_ref, w_ref, dm_ref, g_ref, vg_ref, dense_ref, wide_ref):
+    wide_ref[...] = nn(dm_ref[:, 0:D], w_ref[0]) + nn(dm_ref[:, D : 2 * D], w_ref[1]) + nn(dm_ref[:, 2 * D : 3 * D], w_ref[2])
+    move_back(layer, wide_ref, dense_ref)
+    da1 = dense_ref[...]
     unit, scale = normalize(x_ref[...].astype(f32))
     vg_ref[layer : layer + 1, vec_lanes(0)] += column_sum(da1 * unit)
     vg_ref[layer : layer + 1, vec_lanes(2)] += column_sum(da1)
     g_ref[...] = gh_ref[...] + normalize_back(da1, sm_ref[layer : layer + 1, vec_lanes(0)], unit, scale)
 
 
-def attn_bwd_kernel(layer, gh_ref, x_ref, perm_ref, sm_ref, w_ref, a1_ref, qkv_ref, p_ref, ou_ref, g_ref, grad_ref, vg_ref, wacc_ref, do_ref, dm_ref, ds_ref):
-    attn_core_back(layer, gh_ref, perm_ref, w_ref, a1_ref, qkv_ref, p_ref, ou_ref, grad_ref, vg_ref, wacc_ref, do_ref, dm_ref, ds_ref)
-    attn_norm_back(layer, gh_ref, x_ref, perm_ref, sm_ref, w_ref, dm_ref, g_ref, vg_ref)
-
-
-def attn_core_kernel(layer, gh_ref, perm_ref, w_ref, a1_ref, qkv_ref, p_ref, ou_ref, dm_ref, grad_ref, vg_ref, wacc_ref, do_ref, ds_ref):
-    attn_core_back(layer, gh_ref, perm_ref, w_ref, a1_ref, qkv_ref, p_ref, ou_ref, grad_ref, vg_ref, wacc_ref, do_ref, dm_ref, ds_ref)
-
-
-def attn_norm_kernel(layer, gh_ref, x_ref, perm_ref, sm_ref, w_ref, dm_ref, g_ref, vg_ref):
+def attn_bwd_kernel(layer, gh_ref, x_ref, sm_ref, w_ref, a1_ref, qkv_ref, p_ref, ou_ref, g_ref, grad_ref, vg_ref, wacc_ref, dm_ref, ds_ref, dense_ref, wide_ref, do_ref, out_ref):
+    attn_core_back(layer, gh_ref, w_ref, a1_ref, qkv_ref, p_ref, ou_ref, grad_ref, vg_ref, wacc_ref, dm_ref, ds_ref, dense_ref, wide_ref, do_ref)
+    attn_norm_back(layer, gh_ref, x_ref, sm_ref, w_ref, dm_ref, g_ref, vg_ref, dense_ref, out_ref)
+
+
+def attn_core_kernel(layer, gh_ref, w_ref, a1_ref, qkv_ref, p_ref, ou_ref, dm_ref, grad_ref, vg_ref, wacc_ref, ds_ref, dense_ref, wide_ref, do_ref):
+    attn_core_back(layer, gh_ref, w_ref, a1_ref, qkv_ref, p_ref, ou_ref, grad_ref, vg_ref, wacc_ref, dm_ref, ds_ref, dense_ref, wide_ref, do_ref)
+
+
+def attn_norm_kernel(layer, gh_ref, x_ref, sm_ref, w_ref, dm_ref, g_ref, vg_ref, dense_ref, wide_ref):
     @pl.when(pl.program_id(0) == 0)
     def _():
         vg_ref[...] = jnp.zeros_like(vg_ref)
 
-    attn_norm_back(layer, gh_ref, x_ref, perm_ref, sm_ref, w_ref, dm_ref, g_ref, vg_ref)
+    attn_norm_back(layer, gh_ref, x_ref, sm_ref, w_ref, dm_ref, g_ref, vg_ref, dense_ref, wide_ref)
 
 
 def gelu_parts(z):
@@ -333,14 +379,14 @@
 
 def ffn_both_kernel(layer, with_output, *refs):
     if with_output:
-        h_ref, g_ref, sm_ref, w_ref, in_ref, gh_ref, grad_ref, vg_ref, x_ref, mean_ref, wacc_ref = refs
+        h_ref, g_ref, sm_ref, w_ref, in_ref, gh_ref, grad_ref, vg_ref, x_ref, mean_ref, a2_ref, gm_ref, m_ref, dz_ref = refs
     else:
-        h_ref, g_ref, sm_ref, w_ref, gh_ref, grad_ref, vg_ref, wacc_ref = refs
+        h_ref, g_ref, sm_ref, w_ref, gh_ref, grad_ref, vg_ref, a2_ref, gm_ref, m_ref, dz_ref = refs
     image = pl.program_id(0)
+    here = pl.ds(pl.multiple_of(image * IMG_ROWS, 16), IMG_ROWS)
 
     @pl.when(image == 0)
     def _():
-        wacc_ref[...] = jnp.zeros_like(wacc_ref)
         vg_ref[...] = jnp.zeros_like(vg_ref)
 
     h = h_ref[...]
@@ -349,6 +395,8 @@
     a2 = (unit * gain + sm_ref[layer : layer + 1, vec_lanes(3)]).astype(bf16)
     g = g_ref[...].astype(f32)
     gm = g.astype(bf16)
+    a2_ref[here, :] = a2
+    gm_ref[here, :] = gm
     vg_ref[layer : layer + 1, vec_lanes(5)] += column_sum(gm.astype(f32))
     if with_output:
         out = h + sm_ref[layer : layer + 1, vec_lanes(5)]
@@ -358,12 +406,12 @@
         down = w_ref[1, at : at + CHUNK, :]
         z = nt(a2, up) + sm_ref[2 + layer : 3 + layer, at : at + CHUNK]
         m, slope = gelu_parts(z)
+        m_ref[here, at : at + CHUNK] = m
         if with_output:
             out += nn(m, down)
         dz = (nt(gm, down) * slope).astype(bf16)
+        dz_ref[here, at : at + CHUNK] = dz
         vg_ref[2 + layer : 3 + layer, at : at + CHUNK] += column_sum(dz.astype(f32))
-        wacc_ref[0, at : at + CHUNK, :] += tn(dz, a2)
-        wacc_ref[1, at : at + CHUNK, :] += tn(m, gm)
         da += nn(dz, up)
     vg_ref[layer : layer + 1, vec_lanes(1)] += column_sum(da * unit)
     vg_ref[layer : layer + 1, vec_lanes(3)] += column_sum(da)
@@ -375,7 +423,9 @@
 
     @pl.when(image == pl.num_programs(0) - 1)
     def _():
-        grad_ref[...] = wacc_ref[...].astype(bf16)
+        for at in range(0, FF, CHUNK):
+            grad_ref[0, at : at + CHUNK, :] = tn(dz_ref[:, at : at + CHUNK], a2_ref[...]).astype(bf16)
+            grad_ref[1, at : at + CHUNK, :] = tn(m_ref[:, at : at + CHUNK], gm_ref[...]).astype(bf16)
 
 
 def whole(*shape):
@@ -408,12 +458,12 @@
     )
 
 
-def attn_forward(layer, x, perm, rows, mask, weights, at):
+def attn_forward(layer, x, rows, mask, weights, at):
     images = x.shape[0] // IMG_ROWS
     tokens, padded, pieces = images * IMG_ROWS, images * PAD_ROWS, len(weights)
-    ins = [by_image(IMG_ROWS, D), whole(PAD_ROWS, IMG_ROWS), whole(8, 6 * D), by_image(1, PAIRS, 128, 128)]
+    ins = [by_image(IMG_ROWS, D), whole(8, 6 * D), by_image(1, PAIRS, 128, 128)]
     ins += [whole(*piece.shape) for piece in weights]
-    args = [x, perm, rows, mask, *weights]
+    args = [x, rows, mask, *weights]
     outs = [
         (by_image(IMG_ROWS, D), shape_of((tokens, D), f32)),
         (by_image(PAD_ROWS, D), shape_of((padded, D), bf16)),
@@ -431,8 +481,12 @@
         images,
         ins,
         outs,
-        [pltpu.VMEM((PAD_ROWS, D), bf16), pltpu.VMEM((TILES, 128, 512), f32)],
+        [*move_scratch(), pltpu.VMEM((TILES, 128, 512), f32)],
     )(*args)
+
+
+def move_scratch():
+    return [pltpu.VMEM((IMG_ROWS, D), f32), pltpu.VMEM((PAD_ROWS, D), f32)]
 
 
 def kept_specs():
@@ -444,13 +498,13 @@
     ]
 
 
-def attn_backward(layer, gh, x, perm, rows, weights, kept):
+def attn_backward(layer, gh, x, rows, weights, kept):
     images = x.shape[0] // IMG_ROWS
     return call(
         lambda *refs: attn_bwd_kernel(layer, *refs),
         "attn_bwd",
         images,
-        [by_image(IMG_ROWS, D), by_image(IMG_ROWS, D), whole(PAD_ROWS, IMG_ROWS), whole(8, 6 * D), whole(4, D, D)] + kept_specs(),
+        [by_image(IMG_ROWS, D), by_image(IMG_ROWS, D), whole(8, 6 * D), whole(4, D, D)] + kept_specs(),
         [
             (by_image(IMG_ROWS, D), shape_of((images * IMG_ROWS, D), f32)),
             (whole(4, D, D), shape_of((4, D, D), bf16)),
@@ -458,30 +512,32 @@
         ],
         [
             pltpu.VMEM((4, D, D), f32),
-            pltpu.VMEM((PAD_ROWS, D), bf16),
             pltpu.VMEM((PAD_ROWS, 3 * D), bf16),
             pltpu.VMEM((TILES, 128, 512), f32),
+            *move_scratch(),
+            pltpu.VMEM((PAD_ROWS, D), bf16),
+            pltpu.VMEM((PAD_ROWS, D), f32),
         ],
-    )(gh, x, perm, rows, weights, *kept)
-
-
-def attn_backward_core(layer, gh, perm, weights, kept):
+    )(gh, x, rows, weights, *kept)
+
+
+def attn_backward_core(layer, gh, weights, kept):
     images = gh.shape[0] // IMG_ROWS
     return call(
         lambda *refs: attn_core_kernel(layer, *refs),
         "attn_core",
         images,
-        [by_image(IMG_ROWS, D), whole(PAD_ROWS, IMG_ROWS), whole(4, D, D)] + kept_specs(),
+        [by_image(IMG_ROWS, D), whole(4, D, D)] + kept_specs(),
         [
             (by_image(PAD_ROWS, 3 * D), shape_of((images * PAD_ROWS, 3 * D), bf16)),
             (whole(4, D, D), shape_of((4, D, D), bf16)),
             (whole(8, 6 * D), shape_of((8, 6 * D), f32)),
         ],
-        [pltpu.VMEM((4, D, D), f32), pltpu.VMEM((PAD_ROWS, D), bf16), pltpu.VMEM((TILES, 128, 512), f32)],
-    )(gh, perm, weights, *kept)
-
-
-def attn_backward_norm(layer, gh, x, perm, rows, weights, dmix):
+        [pltpu.VMEM((4, D, D), f32), pltpu.VMEM((TILES, 128, 512), f32), *move_scratch(), pltpu.VMEM((PAD_ROWS, D), bf16)],
+    )(gh, weights, *kept)
+
+
+def attn_backward_norm(layer, gh, x, rows, weights, dmix):
     images = x.shape[0] // IMG_ROWS
     return call(
         lambda *refs: attn_norm_kernel(layer, *refs),
@@ -490,7 +546,6 @@
         [
             by_image(IMG_ROWS, D),
             by_image(IMG_ROWS, D),
-            whole(PAD_ROWS, IMG_ROWS),
             whole(8, 6 * D),
             whole(4, D, D),
             by_image(PAD_ROWS, 3 * D),
@@ -499,7 +554,8 @@
             (by_image(IMG_ROWS, D), shape_of((images * IMG_ROWS, D), f32)),
             (whole(8, 6 * D), shape_of((8, 6 * D), f32)),
         ],
-    )(gh, x, perm, rows, weights, dmix)
+        move_scratch(),
+    )(gh, x, rows, weights, dmix)
 
 
 def ffn_forward(layer, h, rows, weights, at):
@@ -538,7 +594,7 @@
         images,
         ins,
         outs,
-        [pltpu.VMEM((2, FF, D), f32)],
+        [pltpu.VMEM((tokens, width), bf16) for width in (D, D, FF, FF)],
     )(*args)
 
 
@@ -558,11 +614,6 @@
     rows_of, cols_of = token_places()
     inside = (jnp.asarray(rows_of)[None] < own_size[:, 0:1]) & (jnp.asarray(cols_of)[None] < own_size[:, 1:2])
     return inside.astype(f32).reshape(-1, 1)
-
-
-def move_matrix(shifted):
-    source = jnp.asarray(padded_source(shifted))
-    return (source[:, None] == jnp.arange(IMG_ROWS, dtype=jnp.int32)[None, :]).astype(bf16)
 
 
 def swap(rows, axis, size, bit):
@@ -651,21 +702,20 @@
     rows = rows.astype(f32)
 
     at = tensor_at.reshape(1).astype(jnp.int32)
-    perms = [move_matrix(l % 2 == 1) for l in range(LAYERS)]
     masks = [key_masks(own_size, l % 2 == 1) for l in range(LAYERS)]
     flags = inside_column(own_size)
 
-    rows, dense_part, flags, perms, masks = tied(rows, dense_part, flags, perms, masks)
+    rows, dense_part, flags, masks = tied(rows, dense_part, flags, masks)
     dense_part = dense_part.transpose(1, 0, 2, 3).reshape(2, ff_part, D)
     dense_w0 = [dense_part] + exchange(lambda s: dense_part, "tensor", n_tensor)
-    h0, *kept0, attn_w0 = attn_forward(0, tokens, perms[0], rows, masks[0], attn_w0, at)
+    h0, *kept0, attn_w0 = attn_forward(0, tokens, rows, masks[0], attn_w0, at)
     h0, kept0, attn_w0, dense_w0 = tied(h0, kept0, attn_w0, dense_w0)
     x1, dense_w0 = ffn_forward(0, h0, rows, dense_w0, at)
-    h1, *kept1 = attn_forward(1, x1, perms[1], rows, masks[1], [attn_w1], at)
+    h1, *kept1 = attn_forward(1, x1, rows, masks[1], [attn_w1], at)
 
     gh1, dense_g1, vf1, output, image_mean = ffn_both(1, h1, cotangent, rows, dense_w1, flags)
     dense_sum1 = lax.psum_scatter(dense_g1, ("dp", "tensor"), scatter_dimension=1, tiled=True).astype(f32)
-    g1, attn_g1, va1 = attn_backward(1, gh1, x1, perms[1], rows, attn_w1, kept1)
+    g1, attn_g1, va1 = attn_backward(1, gh1, x1, rows, attn_w1, kept1)
     got = exchange(lambda s: own_block(attn_g1, tensor_at ^ s, own_cols, 1), "tensor", n_tensor)
 
     gh0, dense_g0, vf0 = ffn_both(0, h0, g1, rows, dense_w0)
@@ -673,14 +723,14 @@
     attn_t1 = total(own_block(attn_g1, tensor_at, own_cols, 1), got)
     got = exchange(lambda s: own_block(dense_g0, tensor_at ^ s, ff_part, 1), "tensor", n_tensor)
     parts1 = lax.all_to_all(attn_t1.astype(bf16).reshape(n_dp, -1, D), "dp", 0, 0)
-    dmix, attn_g0, va0 = attn_backward_core(0, gh0, perms[0], attn_w0, kept0)
+    dmix, attn_g0, va0 = attn_backward_core(0, gh0, attn_w0, kept0)
     dmix, attn_g0, va0, got, parts1 = tied(dmix, attn_g0, va0, got, parts1)
     dense_t0 = total(own_block(dense_g0, tensor_at, ff_part, 1), got).astype(bf16)
     got = exchange(lambda s: own_block(attn_g0, tensor_at ^ s, own_cols, 1), "tensor", n_tensor)
     blocks = dense_t0.reshape(2, n_dp, ub_own, D).transpose(1, 0, 2, 3)
     blocks = lax.all_to_all(blocks, "dp", 0, 0)
     whole1 = to_all(jnp.sum(parts1.astype(f32), axis=0).astype(bf16), "dp", n_dp)
-    g0, vn0 = attn_backward_norm(0, gh0, tokens, perms[0], rows, attn_w0, dmix)
+    g0, vn0 = attn_backward_norm(0, gh0, tokens, rows, attn_w0, dmix)
     g0, vn0, got, blocks, whole1, dense_sum1 = tied(g0, vn0, got, blocks, whole1, dense_sum1)
     attn_t0 = total(own_block(attn_g0, tensor_at, own_cols, 1), got)
     dense_sum0 = jnp.sum(blocks.astype(f32), axis=0)

time: 352 us -> 311 us (0.88)
  Pallas kernels: 201 us -> 150 us
  waiting for transfers between devices: 39.7 us -> 54.5 us
    pallas_call x2, Pallas kernels: 63.9 us -> 36 us  [attn_forward(): call(lambda *refs: attn_fwd_kernel(layer, pieces, *refs), 'attn_fwd', ima...]
    ppermute x22, waiting for transfers between devices: 14.7 us -> 28.5 us  [swap(): return lax.ppermute(rows, axis, [(i, i ^ bit) for i in range(size)])]
    pallas_call x1, Pallas kernels: 38.9 us -> 28.6 us  [attn_backward(): call(lambda *refs: attn_bwd_kernel(layer, *refs), 'attn_bwd', images, [by...]
    pallas_call x1, Pallas kernels: 33.7 us -> 24.1 us  [attn_backward_core(): call(lambda *refs: attn_core_kernel(layer, *refs), 'attn_core', images, [...]
  transfers between devices with their start and end apart: 31 -> 31, of which waited for: 10 -> 11; matrix products, arithmetic and copies ran while one was open for 6% -> 6% of each run, Pallas kernels for 51% -> 41%
where the time goes in v3:
time: 311 us; the launch traced here: 307 us
  Pallas kernels  150 us (48%)
  waiting for transfers between devices  54.5 us (18%)
  starting transfers between devices  53.7 us (17%)
  local copies, waits for them, and re-layouts  18.1 us (6%)
  other arithmetic  15.8 us (5%)
  between operations  15 us (5%)
    pallas_call x2, Pallas kernels, ffn_both(): call(lambda *refs: ffn_both_kernel(layer, with_output, *refs), 'ffn_both_...  43.8 us
    pallas_call x2, Pallas kernels, attn_forward(): call(lambda *refs: attn_fwd_kernel(layer, pieces, *refs), 'attn_fwd', ima...  36 us
    pallas_call x1, Pallas kernels, attn_backward(): call(lambda *refs: attn_bwd_kernel(layer, *refs), 'attn_bwd', images, [by...  28.6 us
    ppermute x22, waiting for transfers between devices, swap(): return lax.ppermute(rows, axis, [(i, i ^ bit) for i in range(size)])  28.5 us
    pallas_call x1, Pallas kernels, attn_backward_core(): call(lambda *refs: attn_core_kernel(layer, *refs), 'attn_core', images, [...  24.1 us
    ppermute x22, starting transfers between devices, swap(): return lax.ppermute(rows, axis, [(i, i ^ bit) for i in range(size)])  22.8 us
    all_to_all x3, waiting for transfers between devices, to_all(): lax.all_to_all(jnp.broadcast_to(rows[None], (size,) + rows.shape), axis,...  16.2 us
    all_to_all x3, starting transfers between devices, to_all(): lax.all_to_all(jnp.broadcast_to(rows[None], (size,) + rows.shape), axis,...  13.6 us
  transfers between devices with their start and end apart: 31, of which 11 were waited for; matrix products, arithmetic and copies ran while one was open for 6% of the time, Pallas kernels for 41%

profile of v3, /device:TPU:0, one launch (start us, length us, event | category | flops | bytes accessed | tf_op | source)
XLA Modules:
  0.0 307.0 jit_solution(11089798662128659955)
XLA Ops:
  15.5 2.6 collective-permute-start.4
  18.1 2.7 collective-permute-start
  21.7 4.0 %all-to-all-start = ((bf16[8,2,48,384]{3,2,1,0:T(8,128)(2,1)}), bf16[8,2,48,384]{3,2,1,0:T(8,128)(2,1)S(1)}, u32[]{:S(2)}, u32[]{:S(2)}) async-start(bf16[8,2,48,384]{3,2,1,0:T(8,128)(2,1)} %broadcast_in_dim.25), calls=%async_computation | async-start | bytes 1179648 | tf_op jit(solution)/shard_map/all_to_all | solution.py:648
  28.4 7.9 %collective-permute-done.1 = bf16[8,2304]{1,0:T(8,128)(2,1)S(1)} collective-permute-done((bf16[8,2304]{1,0:T(8,128)(2,1)S(1)}, bf16[8,2304]{1,0:T(8,128)(2,1)S(1)}, u32[]{:S(2)}, u32[]{:S(2)}) %collective-permute-start.1) | collective-permute-done | bytes 36896 | tf_op jit(solution)/shard_map/ppermute | solution.py:620
  42.4 2.1 collective-permute-done.6
  51.3 17.8 %attn_fwd.2 = (f32[1568,384]{1,0:T(8,128)}, bf16[2048,384]{1,0:T(8,128)(2,1)}, bf16[2048,1152]{1,0:T(8,128)(2,1)}, bf16[2,8,3,128,512]{4,3,2,1,0:T(8,128)(2,1)},...) custom-call(bf16[1568,384]{1,0:T(8,128)(2,1)} %refs_1_.3, f32[8,2304]{1,0:T(8,128)} %add_convert_fusion.4.refs_1_.refs_2_, ...), custom_call_target="tpu_custom_call" | custom-call | flops 100000000 | bytes 100000 | tf_op jit(solution)/shard_map/attn_fwd/pallas_call | solution.py:478
  69.1 9.7 %collective-permute-done.9.refs_4_ = bf16[2,384,384]{2,1,0:T(8,128)(2,1)S(1)} collective-permute-done((bf16[2,384,384]{2,1,0:T(8,128)(2,1)S(1)}, bf16[2,384,384]{2,1,0:T(8,128)(2,1)S(1)}, u32[]{:S(2)}, u32[]{:S(2)}) %collective-permute-start.9) | collective-permute-done | bytes 589856 | tf_op jit(solution)/shard_map/ppermute | solution.py:620
  79.6 9.3 %ffn_fwd.1 = (f32[1568,384]{1,0:T(8,128)}, bf16[2,1536,384]{2,1,0:T(8,128)(2,1)}) custom-call(f32[1568,384]{1,0:T(8,128)} %get-tuple-element.101.refs_0_, f32[8,2304]{1,0:T(8,128)} %add_convert_fusion.4.refs_1_.refs_2_, bf16[2,384,384]{2,1,0:T(8,128)(2,1)} %bitcast.78, bf16[2,384,384]{2,1,0:T(8,128)(2,1)} %copy-done.6, bf16[2,384,384]{2,1,0:T(8,128)(2,1)} %copy-done.7, ...), custom_call_target="tpu_custom_call" | custom-call | flops 100000000 | bytes 100000 | tf_op jit(solution)/shard_map/ffn_fwd/pallas_call | solution.py:563
  89.0 18.2 %attn_fwd.3 = (f32[1568,384]{1,0:T(8,128)}, bf16[2048,384]{1,0:T(8,128)(2,1)}, bf16[2048,1152]{1,0:T(8,128)(2,1)}, bf16[2,8,3,128,512]{4,3,2,1,0:T(8,128)(2,1)}, bf16[1568,384]{1,0:T(8,128)(2,1)}) custom-call(f32[1568,384]{1,0:T(8,128)} %get-tuple-element.106.refs_0_.refs_1_, f32[8,2304]{1,0:T(8,128)} %add_convert_fusion.4.refs_1_.refs_2_, ...), custom_call_target="tpu_custom_call" | custom-call | flops 100000000 | bytes 100000 | tf_op jit(solution)/shard_map/attn_fwd/pallas_call | solution.py:478
  107.2 23.3 %ffn_both_out.1 = (f32[1568,384]{1,0:T(8,128)}, bf16[2,1536,384]{2,1,0:T(8,128)(2,1)}, f32[8,2304]{1,0:T(8,128)}, bf16[1568,384]{1,0:T(8,128)(2,1)}, f32[2,1,384]{2,1,0:T(1,128)}) custom-call(f32[1568,384]{1,0:T(8,128)} %get-tuple-element.108.refs_0_, bf16[1568,384]{1,0:T(8,128)(2,1)} %refs_1_.2, f32[8,2304]{1,0:T(8,128)} %add_convert_fusion.4.refs_1_.refs_2_, ...), custom_call_target="tpu_custom_call" | custom-call | flops 100000000 | bytes 100000 | tf_op jit(solution)/shard_map/ffn_both_out/pallas_call | solution.py:591
  130.5 28.6 %attn_bwd.1 = (f32[1568,384]{1,0:T(8,128)}, bf16[4,384,384]{2,1,0:T(8,128)(2,1)}, f32[8,2304]{1,0:T(8,128)}) custom-call(f32[1568,384]{1,0:T(8,128)} %get-tuple-element.112.refs_0_, f32[1568,384]{1,0:T(8,128)} %get-tuple-element.106.refs_0_.refs_1_, f32[8,2304]{1,0:T(8,128)} %add_convert_fusion.4.refs_1_.refs_2_, bf16[4,384,384]{2,1,0:T(8,128)(2,1)} %bitcast.70, ...), custom_call_target="tpu_custom_call" | custom-call | flops 100000000 | bytes 100000 | tf_op jit(solution)/shard_map/attn_bwd/pallas_call | solution.py:503
  162.3 20.5 %ffn_both.1 = (f32[1568,384]{1,0:T(8,128)}, bf16[2,1536,384]{2,1,0:T(8,128)(2,1)}, f32[8,2304]{1,0:T(8,128)}) custom-call(f32[1568,384]{1,0:T(8,128)} %get-tuple-element.101.refs_0_, f32[1568,384]{1,0:T(8,128)} %get-tuple-element.117.refs_1_, f32[8,2304]{1,0:T(8,128)} %add_convert_fusion.4.refs_1_.refs_2_, bf16[2,1536,384]{2,1,0:T(8,128)(2,1)} %get-tuple-element.118.refs_3_), custom_call_target="tpu_custom_call" | custom-call | flops 100000000 | bytes 100000 | tf_op jit(solution)/shard_map/ffn_both/pallas_call | solution.py:591
  182.9 2.5 constant_dynamic-slice_fusion.3
  189.4 7.0 %all-to-all-start.1 = ((bf16[8,48,384]{2,1,0:T(8,128)(2,1)}), bf16[8,48,384]{2,1,0:T(8,128)(2,1)S(1)}, u32[]{:S(2)}, u32[]{:S(2)}) async-start(bf16[8,48,384]{2,1,0:T(8,128)(2,1)} %bitcast.19), calls=%async_computation.1 | async-start | bytes 589824 | tf_op jit(solution)/shard_map/all_to_all | solution.py:725
  196.4 24.1 %attn_core.1 = (bf16[2048,1152]{1,0:T(8,128)(2,1)}, bf16[4,384,384]{2,1,0:T(8,128)(2,1)}, f32[8,2304]{1,0:T(8,128)}) custom-call(f32[1568,384]{1,0:T(8,128)} %get-tuple-element.123.refs_0_, bf16[4,384,384]{2,1,0:T(8,128)(2,1)} %get-tuple-element.124.refs_1_.refs_3_, bf16[2048,384]{1,0:T(8,128)(2,1)} %get-tuple-element.125.refs_2_, ...), custom_call_target="tpu_custom_call" | custom-call | flops 100000000 | bytes 100000 | tf_op jit(solution)/shard_map/attn_core/pallas_call | solution.py:526
  221.3 6.0 %all-to-all-start.3 = ((bf16[8,48,384]{2,1,0:T(8,128)(2,1)}), bf16[8,48,384]{2,1,0:T(8,128)(2,1)S(1)}, u32[]{:S(2)}, u32[]{:S(2)}) async-start(bf16[8,48,384]{2,1,0:T(8,128)(2,1)} %broadcast_in_dim.51), calls=%async_computation.3 | async-start | bytes 589824 | tf_op jit(solution)/shard_map/all_to_all | solution.py:648
  229.7 7.5 %all-to-all-done.3 = bf16[8,48,384]{2,1,0:T(8,128)(2,1)S(1)} async-done(((bf16[8,48,384]{2,1,0:T(8,128)(2,1)}), bf16[8,48,384]{2,1,0:T(8,128)(2,1)S(1)}, u32[]{:S(2)}, u32[]{:S(2)}) %all-to-all-start.3) | async-done | bytes 294944 | tf_op jit(solution)/shard_map/all_to_all | solution.py:648
  237.1 4.0 %all-to-all-start.2 = ((bf16[8,2,48,384]{3,2,1,0:T(8,128)(2,1)}), bf16[8,2,48,384]{3,2,1,0:T(8,128)(2,1)S(1)}, u32[]{:S(2)}, u32[]{:S(2)}) async-start(bf16[8,2,48,384]{3,2,1,0:T(8,128)(2,1)} %bitcast.67), calls=%async_computation.2 | async-start | bytes 1179648 | tf_op jit(solution)/shard_map/all_to_all | solution.py:731
  243.2 8.1 %attn_norm.1 = (f32[1568,384]{1,0:T(8,128)}, f32[8,2304]{1,0:T(8,128)}) custom-call(f32[1568,384]{1,0:T(8,128)} %get-tuple-element.123.refs_0_, bf16[1568,384]{1,0:T(8,128)(2,1)} %refs_1_.3, f32[8,2304]{1,0:T(8,128)} %add_convert_fusion.4.refs_1_.refs_2_, bf16[4,384,384]{2,1,0:T(8,128)(2,1)} %get-tuple-element.124.refs_1_.refs_3_, ...), custom_call_target="tpu_custom_call" | custom-call | flops 100000000 | bytes 100000 | tf_op jit(solution)/shard_map/attn_norm/pallas_call | solution.py:542
  252.3 4.5 %collective-permute-done.19 = bf16[4,96,384]{2,1,0:T(8,128)(2,1)} collective-permute-done((bf16[4,96,384]{2,1,0:T(8,128)(2,1)S(1)}, bf16[4,96,384]{2,1,0:T(8,128)(2,1)}, u32[]{:S(2)}, u32[]{:S(2)}) %collective-permute-start.19) | collective-permute-done | bytes 294944 | tf_op jit(solution)/shard_map/ppermute | solution.py:620
  264.5 5.9 %all-to-all-start.4 = ((bf16[8,54,384]{2,1,0:T(8,128)(2,1)}), bf16[8,54,384]{2,1,0:T(8,128)(2,1)S(1)}, u32[]{:S(2)}, u32[]{:S(2)}) async-start(bf16[8,54,384]{2,1,0:T(8,128)(2,1)} %pad_maximum_fusion.1), calls=%async_computation.5 | async-start | bytes 688128 | tf_op jit(solution)/shard_map/all_to_all | solution.py:652
  271.1 9.6 %all-to-all-done.4 = bf16[8,54,384]{2,1,0:T(8,128)(2,1)S(1)} async-done(((bf16[8,54,384]{2,1,0:T(8,128)(2,1)}), bf16[8,54,384]{2,1,0:T(8,128)(2,1)S(1)}, u32[]{:S(2)}, u32[]{:S(2)}) %all-to-all-start.4) | async-done | bytes 331808 | tf_op jit(solution)/shard_map/all_to_all | solution.py:652
  281.5 3.6 %all-to-all-start.5 = ((bf16[8,54,384]{2,1,0:T(8,128)(2,1)}), bf16[8,54,384]{2,1,0:T(8,128)(2,1)S(1)}, u32[]{:S(2)}, u32[]{:S(2)}) async-start(bf16[8,54,384]{2,1,0:T(8,128)(2,1)} %broadcast_in_dim.52), calls=%async_computation.6 | async-start | bytes 688128 | tf_op jit(solution)/shard_map/all_to_all | solution.py:648
  286.5 8.8 %all-to-all-done.5 = bf16[8,54,384]{2,1,0:T(8,128)(2,1)S(1)} async-done(((bf16[8,54,384]{2,1,0:T(8,128)(2,1)}), bf16[8,54,384]{2,1,0:T(8,128)(2,1)S(1)}, u32[]{:S(2)}, u32[]{:S(2)}) %all-to-all-start.5) | async-done | bytes 331808 | tf_op jit(solution)/shard_map/all_to_all | solution.py:648
  (175 shorter events, 53.6 us)
Async XLA Ops:
  7.2 81.7 %all-gather.5.cloned.1.call-start = ((), (), s32[]{:S(2)}) async-start(), calls=%async_computation.8 | async-start | bytes 1474560 | tf_op jit(solution)/shard_map/all_gather | solution.py:695
  13.5 93.7 %all-gather.7.cloned.1.call-start = ((), (), s32[]{:S(2)}) async-start(), calls=%async_computation.9 | async-start | bytes 2433024 | tf_op jit(solution)/shard_map/all_gather | solution.py:696
  14.2 26.2 %collective-permute-start.3 = (bf16[4,96,384]{2,1,0:T(8,128)(2,1)S(1)}, bf16[4,96,384]{2,1,0:T(8,128)(2,1)S(1)}, u32[]{:S(2)}, u32[]{:S(2)}) collective-permute-start(bf16[4,96,384]{2,1,0:T(8,128)(2,1)S(1)} %get-tuple-element.90.refs_3_), channel_id=1, source_target_pairs={{0,1},{1,0},{2,3},{3,2},{4,5},{5,4},{6,7},{7,6},{8,9},{9,8},{10,11... | collective-permute-start | bytes 884744 | tf_op jit(solution)/shard_map/ppermute | solution.py:620
  15.5 25.0 %collective-permute-start.4 = (bf16[4,96,384]{2,1,0:T(8,128)(2,1)S(1)}, bf16[4,96,384]{2,1,0:T(8,128)(2,1)S(1)}, u32[]{:S(2)}, u32[]{:S(2)}) collective-permute-start(bf16[4,96,384]{2,1,0:T(8,128)(2,1)S(1)} %get-tuple-element.90.refs_3_), channel_id=1, source_target_pairs={{0,2},{1,3},{2,0},{3,1},{4,6},{5,7},{6,4},{7,5},{8,10},{9,11},{10,... | collective-permute-start | bytes 884744 | tf_op jit(solution)/shard_map/ppermute | solution.py:620
  18.0 22.4 %collective-permute-start.5 = (bf16[4,96,384]{2,1,0:T(8,128)(2,1)S(1)}, bf16[4,96,384]{2,1,0:T(8,128)(2,1)S(1)}, u32[]{:S(2)}, u32[]{:S(2)}) collective-permute-start(bf16[4,96,384]{2,1,0:T(8,128)(2,1)S(1)} %get-tuple-element.90.refs_3_), channel_id=1, source_target_pairs={{0,3},{1,2},{2,1},{3,0},{4,7},{5,6},{6,5},{7,4},{8,11},{9,10},{10,... | collective-permute-start | bytes 884744 | tf_op jit(solution)/shard_map/ppermute | solution.py:620
  21.7 24.7 %all-to-all-start = ((bf16[8,2,48,384]{3,2,1,0:T(8,128)(2,1)}), bf16[8,2,48,384]{3,2,1,0:T(8,128)(2,1)S(1)}, u32[]{:S(2)}, u32[]{:S(2)}) async-start(bf16[8,2,48,384]{3,2,1,0:T(8,128)(2,1)} %broadcast_in_dim.25), calls=%async_computation | async-start | bytes 1179648 | tf_op jit(solution)/shard_map/all_to_all | solution.py:648
  25.7 225.7 %reduce-scatter.2.cloned.1.call-start = ((), (), s32[]{:S(2)}) async-start(), calls=%async_computation.7 | async-start | bytes 2433024 | tf_op jit(solution)/shard_map/reduce_scatter | solution.py:717
  47.9 21.2 %collective-permute-start.10 = (bf16[2,384,384]{2,1,0:T(8,128)(2,1)S(1)}, bf16[2,384,384]{2,1,0:T(8,128)(2,1)S(1)}, u32[]{:S(2)}, u32[]{:S(2)}) collective-permute-start(bf16[2,384,384]{2,1,0:T(8,128)(2,1)S(1)} %bitcast.75), channel_id=1, source_target_pairs={{0,3},{1,2},{2,1},{3,0},{4,7},{5,6},{6,5},{7,4},{8,11},{9,10},{10,... | collective-permute-start | bytes 1769480 | tf_op jit(solution)/shard_map/ppermute | solution.py:620
  49.4 19.7 %collective-permute-start.8 = (bf16[2,384,384]{2,1,0:T(8,128)(2,1)S(1)}, bf16[2,384,384]{2,1,0:T(8,128)(2,1)S(1)}, u32[]{:S(2)}, u32[]{:S(2)}) collective-permute-start(bf16[2,384,384]{2,1,0:T(8,128)(2,1)S(1)} %bitcast.76), channel_id=1, source_target_pairs={{0,1},{1,0},{2,3},{3,2},{4,5},{5,4},{6,7},{7,6},{8,9},{9,8},{10,11... | collective-permute-start | bytes 1769480 | tf_op jit(solution)/shard_map/ppermute | solution.py:620
  49.8 29.1 %collective-permute-start.9 = (bf16[2,384,384]{2,1,0:T(8,128)(2,1)S(1)}, bf16[2,384,384]{2,1,0:T(8,128)(2,1)S(1)}, u32[]{:S(2)}, u32[]{:S(2)}) collective-permute-start(bf16[2,384,384]{2,1,0:T(8,128)(2,1)S(1)} %bitcast.77), channel_id=1, source_target_pairs={{0,2},{1,3},{2,0},{3,1},{4,6},{5,7},{6,4},{7,5},{8,10},{9,11},{10,... | collective-permute-start | bytes 1769480 | tf_op jit(solution)/shard_map/ppermute | solution.py:620
  160.4 22.5 %collective-permute-start.11 = (bf16[4,96,384]{2,1,0:T(8,128)(2,1)S(1)}, bf16[4,96,384]{2,1,0:T(8,128)(2,1)S(1)}, u32[]{:S(2)}, u32[]{:S(2)}) collective-permute-start(bf16[4,96,384]{2,1,0:T(8,128)(2,1)S(1)} %get-tuple-element.211), channel_id=1, source_target_pairs={{0,1},{1,0},{2,3},{3,2},{4,5},{5,4},{6,7},{7,6},{8,9},{9,8},{10,11... | collective-permute-start | bytes 884744 | tf_op jit(solution)/shard_map/ppermute | solution.py:620
  160.4 22.4 %collective-permute-start.12 = (bf16[4,96,384]{2,1,0:T(8,128)(2,1)S(1)}, bf16[4,96,384]{2,1,0:T(8,128)(2,1)S(1)}, u32[]{:S(2)}, u32[]{:S(2)}) collective-permute-start(bf16[4,96,384]{2,1,0:T(8,128)(2,1)S(1)} %get-tuple-element.210), channel_id=1, source_target_pairs={{0,2},{1,3},{2,0},{3,1},{4,6},{5,7},{6,4},{7,5},{8,10},{9,11},{10,... | collective-permute-start | bytes 884744 | tf_op jit(solution)/shard_map/ppermute | solution.py:620
  162.2 20.6 %collective-permute-start.13 = (bf16[4,96,384]{2,1,0:T(8,128)(2,1)S(1)}, bf16[4,96,384]{2,1,0:T(8,128)(2,1)S(1)}, u32[]{:S(2)}, u32[]{:S(2)}) collective-permute-start(bf16[4,96,384]{2,1,0:T(8,128)(2,1)S(1)} %get-tuple-element.209), channel_id=1, source_target_pairs={{0,3},{1,2},{2,1},{3,0},{4,7},{5,6},{6,5},{7,4},{8,11},{9,10},{10,... | collective-permute-start | bytes 884744 | tf_op jit(solution)/shard_map/ppermute | solution.py:620
  185.4 35.1 %collective-permute-start.14 = (bf16[2,384,384]{2,1,0:T(8,128)(2,1)}, bf16[2,384,384]{2,1,0:T(8,128)(2,1)S(1)}, u32[]{:S(2)}, u32[]{:S(2)}) collective-permute-start(bf16[2,384,384]{2,1,0:T(8,128)(2,1)} %get-tuple-element.205), channel_id=1, source_target_pairs={{0,1},{1,0},{2,3},{3,2},{4,5},{5,4},{6,7},{7,6},{8,9},{9,8},{10,11... | collective-permute-start | bytes 1769480 | tf_op jit(solution)/shard_map/ppermute | solution.py:620
  185.7 34.8 %collective-permute-start.15 = (bf16[2,384,384]{2,1,0:T(8,128)(2,1)S(1)}, bf16[2,384,384]{2,1,0:T(8,128)(2,1)S(1)}, u32[]{:S(2)}, u32[]{:S(2)}) collective-permute-start(bf16[2,384,384]{2,1,0:T(8,128)(2,1)S(1)} %get-tuple-element.204), channel_id=1, source_target_pairs={{0,2},{1,3},{2,0},{3,1},{4,6},{5,7},{6,4},{7,5},{8,10},{9,11},{10,... | collective-permute-start | bytes 1769480 | tf_op jit(solution)/shard_map/ppermute | solution.py:620
  187.4 33.1 %collective-permute-start.16 = (bf16[2,384,384]{2,1,0:T(8,128)(2,1)S(1)}, bf16[2,384,384]{2,1,0:T(8,128)(2,1)S(1)}, u32[]{:S(2)}, u32[]{:S(2)}) collective-permute-start(bf16[2,384,384]{2,1,0:T(8,128)(2,1)S(1)} %get-tuple-element.203), channel_id=1, source_target_pairs={{0,3},{1,2},{2,1},{3,0},{4,7},{5,6},{6,5},{7,4},{8,11},{9,10},{10,... | collective-permute-start | bytes 1769480 | tf_op jit(solution)/shard_map/ppermute | solution.py:620
  189.4 31.1 %all-to-all-start.1 = ((bf16[8,48,384]{2,1,0:T(8,128)(2,1)}), bf16[8,48,384]{2,1,0:T(8,128)(2,1)S(1)}, u32[]{:S(2)}, u32[]{:S(2)}) async-start(bf16[8,48,384]{2,1,0:T(8,128)(2,1)} %bitcast.19), calls=%async_computation.1 | async-start | bytes 589824 | tf_op jit(solution)/shard_map/all_to_all | solution.py:725
  221.3 15.8 %all-to-all-start.3 = ((bf16[8,48,384]{2,1,0:T(8,128)(2,1)}), bf16[8,48,384]{2,1,0:T(8,128)(2,1)S(1)}, u32[]{:S(2)}, u32[]{:S(2)}) async-start(bf16[8,48,384]{2,1,0:T(8,128)(2,1)} %broadcast_in_dim.51), calls=%async_computation.3 | async-start | bytes 589824 | tf_op jit(solution)/shard_map/all_to_all | solution.py:648
  237.1 19.6 %all-to-all-start.2 = ((bf16[8,2,48,384]{3,2,1,0:T(8,128)(2,1)}), bf16[8,2,48,384]{3,2,1,0:T(8,128)(2,1)S(1)}, u32[]{:S(2)}, u32[]{:S(2)}) async-start(bf16[8,2,48,384]{3,2,1,0:T(8,128)(2,1)} %bitcast.67), calls=%async_computation.2 | async-start | bytes 1179648 | tf_op jit(solution)/shard_map/all_to_all | solution.py:731
  241.3 10.9 %collective-permute-start.17 = (bf16[4,96,384]{2,1,0:T(8,128)(2,1)S(1)}, bf16[4,96,384]{2,1,0:T(8,128)(2,1)S(1)}, u32[]{:S(2)}, u32[]{:S(2)}) collective-permute-start(bf16[4,96,384]{2,1,0:T(8,128)(2,1)S(1)} %get-tuple-element.208), channel_id=1, source_target_pairs={{0,1},{1,0},{2,3},{3,2},{4,5},{5,4},{6,7},{7,6},{8,9},{9,8},{10,11... | collective-permute-start | bytes 884744 | tf_op jit(solution)/shard_map/ppermute | solution.py:620
  241.4 10.9 %collective-permute-start.18 = (bf16[4,96,384]{2,1,0:T(8,128)(2,1)S(1)}, bf16[4,96,384]{2,1,0:T(8,128)(2,1)}, u32[]{:S(2)}, u32[]{:S(2)}) collective-permute-start(bf16[4,96,384]{2,1,0:T(8,128)(2,1)S(1)} %get-tuple-element.207), channel_id=1, source_target_pairs={{0,2},{1,3},{2,0},{3,1},{4,6},{5,7},{6,4},{7,5},{8,10},{9,11},{10,... | collective-permute-start | bytes 884744 | tf_op jit(solution)/shard_map/ppermute | solution.py:620
  243.1 13.6 %collective-permute-start.19 = (bf16[4,96,384]{2,1,0:T(8,128)(2,1)S(1)}, bf16[4,96,384]{2,1,0:T(8,128)(2,1)}, u32[]{:S(2)}, u32[]{:S(2)}) collective-permute-start(bf16[4,96,384]{2,1,0:T(8,128)(2,1)S(1)} %get-tuple-element.206), channel_id=1, source_target_pairs={{0,3},{1,2},{2,1},{3,0},{4,7},{5,6},{6,5},{7,4},{8,11},{9,10},{10,... | collective-permute-start | bytes 884744 | tf_op jit(solution)/shard_map/ppermute | solution.py:620
  264.5 16.2 %all-to-all-start.4 = ((bf16[8,54,384]{2,1,0:T(8,128)(2,1)}), bf16[8,54,384]{2,1,0:T(8,128)(2,1)S(1)}, u32[]{:S(2)}, u32[]{:S(2)}) async-start(bf16[8,54,384]{2,1,0:T(8,128)(2,1)} %pad_maximum_fusion.1), calls=%async_computation.5 | async-start | bytes 688128 | tf_op jit(solution)/shard_map/all_to_all | solution.py:652
  281.5 13.8 %all-to-all-start.5 = ((bf16[8,54,384]{2,1,0:T(8,128)(2,1)}), bf16[8,54,384]{2,1,0:T(8,128)(2,1)S(1)}, u32[]{:S(2)}, u32[]{:S(2)}) async-start(bf16[8,54,384]{2,1,0:T(8,128)(2,1)} %broadcast_in_dim.52), calls=%async_computation.6 | async-start | bytes 688128 | tf_op jit(solution)/shard_map/all_to_all | solution.py:648
  (32 other events, 319.7 us)
Sparse Core Ops, SparseCore 0:
  13.6 26.1 all-gather.4
  43.3 59.9 all-gather.6
  130.6 102.7 reduce-scatter.1

commit v4 on v3

--- a/solution.py
+++ b/solution.py
@@ -256,13 +256,19 @@
 
 
 def merge_pieces(at_ref, pieces, whole_ref):
-    rows = pieces[0].shape[1]
+    rows = whole_ref.shape[1] // len(pieces)
     for s, piece in enumerate(pieces):
-        start = pl.multiple_of((at_ref[0] ^ s) * rows, 16)
-        whole_ref[:, pl.ds(start, rows), :] = piece[...]
-
-
-def attn_core_back(layer, gh_ref, w_ref, a1_ref, qkv_ref, p_ref, ou_ref, grad_ref, vg_ref, wacc_ref, dm_ref, ds_ref, dense_ref, wide_ref, do_ref):
+        start = (at_ref[0] ^ s) * rows
+        if len(piece.shape) == 3:
+            whole_ref[:, pl.ds(pl.multiple_of(start, 16), rows), :] = piece[...]
+            continue
+        parts, matrices, count, _ = piece.shape
+        for part in range(parts):
+            for m in range(matrices):
+                whole_ref[m, pl.ds(pl.multiple_of(start + part * count, 16), count), :] = piece[part, m]
+
+
+def attn_core_back(layer, gh_ref, w_ref, a1_ref, qkv_ref, p_ref, ou_ref, at_ref, grad_refs, vg_ref, wacc_ref, dm_ref, ds_ref, dense_ref, wide_ref, do_ref):
     image = pl.program_id(0)
 
     @pl.when(image == 0)
@@ -319,7 +325,10 @@
     @pl.when(image == pl.num_programs(0) - 1)
     def _():
         fold_tables(layer, ds_ref, vg_ref)
-        grad_ref[...] = wacc_ref[...].astype(bf16)
+        for s, grad_ref in enumerate(grad_refs):
+            count = grad_ref.shape[1]
+            start = pl.multiple_of((at_ref[0] ^ s) * count, 16)
+            grad_ref[...] = wacc_ref[:, pl.ds(start, count), :].astype(bf16)
 
 
 def attn_norm_back(layer, gh_ref, x_ref, sm_ref, w_ref, dm_ref, g_ref, vg_ref, dense_ref, wide_ref):
@@ -332,13 +341,15 @@
     g_ref[...] = gh_ref[...] + normalize_back(da1, sm_ref[layer : layer + 1, vec_lanes(0)], unit, scale)
 
 
-def attn_bwd_kernel(layer, gh_ref, x_ref, sm_ref, w_ref, a1_ref, qkv_ref, p_ref, ou_ref, g_ref, grad_ref, vg_ref, wacc_ref, dm_ref, ds_ref, dense_ref, wide_ref, do_ref, out_ref):
-    attn_core_back(layer, gh_ref, w_ref, a1_ref, qkv_ref, p_ref, ou_ref, grad_ref, vg_ref, wacc_ref, dm_ref, ds_ref, dense_ref, wide_ref, do_ref)
+def attn_bwd_kernel(layer, gh_ref, x_ref, sm_ref, w_ref, a1_ref, qkv_ref, p_ref, ou_ref, at_ref, g_ref, *refs):
+    *grad_refs, vg_ref, wacc_ref, dm_ref, ds_ref, dense_ref, wide_ref, do_ref, out_ref = refs
+    attn_core_back(layer, gh_ref, w_ref, a1_ref, qkv_ref, p_ref, ou_ref, at_ref, grad_refs, vg_ref, wacc_ref, dm_ref, ds_ref, dense_ref, wide_ref, do_ref)
     attn_norm_back(layer, gh_ref, x_ref, sm_ref, w_ref, dm_ref, g_ref, vg_ref, dense_ref, out_ref)
 
 
-def attn_core_kernel(layer, gh_ref, w_ref, a1_ref, qkv_ref, p_ref, ou_ref, dm_ref, grad_ref, vg_ref, wacc_ref, ds_ref, dense_ref, wide_ref, do_ref):
-    attn_core_back(layer, gh_ref, w_ref, a1_ref, qkv_ref, p_ref, ou_ref, grad_ref, vg_ref, wacc_ref, dm_ref, ds_ref, dense_ref, wide_ref, do_ref)
+def attn_core_kernel(layer, gh_ref, w_ref, a1_ref, qkv_ref, p_ref, ou_ref, at_ref, dm_ref, *refs):
+    *grad_refs, vg_ref, wacc_ref, ds_ref, dense_ref, wide_ref, do_ref = refs
+    attn_core_back(layer, gh_ref, w_ref, a1_ref, qkv_ref, p_ref, ou_ref, at_ref, grad_refs, vg_ref, wacc_ref, dm_ref, ds_ref, dense_ref, wide_ref, do_ref)
 
 
 def attn_norm_kernel(layer, gh_ref, x_ref, sm_ref, w_ref, dm_ref, g_ref, vg_ref, dense_ref, wide_ref):
@@ -377,11 +388,11 @@
     x_ref[...] = out
 
 
-def ffn_both_kernel(layer, with_output, *refs):
+def ffn_both_kernel(layer, with_output, pieces, *refs):
     if with_output:
-        h_ref, g_ref, sm_ref, w_ref, in_ref, gh_ref, grad_ref, vg_ref, x_ref, mean_ref, a2_ref, gm_ref, m_ref, dz_ref = refs
+        h_ref, g_ref, sm_ref, w_ref, at_ref, in_ref, gh_ref, near_ref, far_ref, vg_ref, x_ref, mean_ref, a2_ref, gm_ref, m_ref, dz_ref = refs
     else:
-        h_ref, g_ref, sm_ref, w_ref, gh_ref, grad_ref, vg_ref, a2_ref, gm_ref, m_ref, dz_ref = refs
+        h_ref, g_ref, sm_ref, w_ref, at_ref, gh_ref, near_ref, far_ref, vg_ref, a2_ref, gm_ref, m_ref, dz_ref = refs
     image = pl.program_id(0)
     here = pl.ds(pl.multiple_of(image * IMG_ROWS, 16), IMG_ROWS)
 
@@ -418,14 +429,22 @@
     gh_ref[...] = g + normalize_back(da, gain, unit, scale)
     if with_output:
         x_ref[...] = out.astype(bf16)
-        flags = in_ref[...]
-        mean_ref[0] = column_sum(out * flags) / jnp.sum(flags)
+        flags = in_ref[0]
+        high = out.astype(bf16)
+        rest = out - high.astype(f32)
+        low = rest.astype(bf16)
+        lower = (rest - low.astype(f32)).astype(bf16)
+        sums = nn(flags, high) + (nn(flags, low) + nn(flags, lower))
+        mean_ref[0] = sums[0:1, :] / jnp.sum(flags[0:1, :].astype(f32))
 
     @pl.when(image == pl.num_programs(0) - 1)
     def _():
-        for at in range(0, FF, CHUNK):
-            grad_ref[0, at : at + CHUNK, :] = tn(dz_ref[:, at : at + CHUNK], a2_ref[...]).astype(bf16)
-            grad_ref[1, at : at + CHUNK, :] = tn(m_ref[:, at : at + CHUNK], gm_ref[...]).astype(bf16)
+        count = FF // pieces
+        for s in range(pieces):
+            grad_ref, at = (near_ref, far_ref)[s % 2], s // 2 * count
+            cols = pl.ds(pl.multiple_of((at_ref[0] ^ s) * count, 128), count)
+            grad_ref[0, at : at + count, :] = tn(dz_ref[:, cols], a2_ref[...]).astype(bf16)
+            grad_ref[1, at : at + count, :] = tn(m_ref[:, cols], gm_ref[...]).astype(bf16)
 
 
 def whole(*shape):
@@ -498,16 +517,16 @@
     ]
 
 
-def attn_backward(layer, gh, x, rows, weights, kept):
+def attn_backward(layer, gh, x, rows, weights, kept, at, pieces):
     images = x.shape[0] // IMG_ROWS
     return call(
         lambda *refs: attn_bwd_kernel(layer, *refs),
         "attn_bwd",
         images,
-        [by_image(IMG_ROWS, D), by_image(IMG_ROWS, D), whole(8, 6 * D), whole(4, D, D)] + kept_specs(),
+        [by_image(IMG_ROWS, D), by_image(IMG_ROWS, D), whole(8, 6 * D), whole(4, D, D)] + kept_specs() + [scalar()],
         [
             (by_image(IMG_ROWS, D), shape_of((images * IMG_ROWS, D), f32)),
-            (whole(4, D, D), shape_of((4, D, D), bf16)),
+            *[(whole(4, D // pieces, D), shape_of((4, D // pieces, D), bf16))] * pieces,
             (whole(8, 6 * D), shape_of((8, 6 * D), f32)),
         ],
         [
@@ -518,23 +537,23 @@
             pltpu.VMEM((PAD_ROWS, D), bf16),
             pltpu.VMEM((PAD_ROWS, D), f32),
         ],
-    )(gh, x, rows, weights, *kept)
-
-
-def attn_backward_core(layer, gh, weights, kept):
+    )(gh, x, rows, weights, *kept, at)
+
+
+def attn_backward_core(layer, gh, weights, kept, at, pieces):
     images = gh.shape[0] // IMG_ROWS
     return call(
         lambda *refs: attn_core_kernel(layer, *refs),
         "attn_core",
         images,
-        [by_image(IMG_ROWS, D), whole(4, D, D)] + kept_specs(),
+        [by_image(IMG_ROWS, D), whole(4, D, D)] + kept_specs() + [scalar()],
         [
             (by_image(PAD_ROWS, 3 * D), shape_of((images * PAD_ROWS, 3 * D), bf16)),
-            (whole(4, D, D), shape_of((4, D, D), bf16)),
+            *[(whole(4, D // pieces, D), shape_of((4, D // pieces, D), bf16))] * pieces,
             (whole(8, 6 * D), shape_of((8, 6 * D), f32)),
         ],
         [pltpu.VMEM((4, D, D), f32), pltpu.VMEM((TILES, 128, 512), f32), *move_scratch(), pltpu.VMEM((PAD_ROWS, D), bf16)],
-    )(gh, weights, *kept)
+    )(gh, weights, *kept, at)
 
 
 def attn_backward_norm(layer, gh, x, rows, weights, dmix):
@@ -572,24 +591,25 @@
     )(h, rows, *weights, at)
 
 
-def ffn_both(layer, h, g, rows, weights, flags=None):
+def ffn_both(layer, h, g, rows, weights, at, pieces, flags=None):
     images = h.shape[0] // IMG_ROWS
     tokens = images * IMG_ROWS
     with_output = flags is not None
     ins = [by_image(IMG_ROWS, D), by_image(IMG_ROWS, D), whole(8, 6 * D), whole(2, FF, D)]
     outs = [
         (by_image(IMG_ROWS, D), shape_of((tokens, D), f32)),
-        (whole(2, FF, D), shape_of((2, FF, D), bf16)),
+        *[(whole(2, FF // 2, D), shape_of((2, FF // 2, D), bf16))] * 2,
         (whole(8, 6 * D), shape_of((8, 6 * D), f32)),
     ]
-    args = [h, g, rows, weights]
+    ins.append(scalar())
+    args = [h, g, rows, weights, at]
     if with_output:
-        ins.append(by_image(IMG_ROWS, 1))
+        ins.append(by_image(1, 16, IMG_ROWS))
         args.append(flags)
         outs.append((by_image(IMG_ROWS, D), shape_of((tokens, D), bf16)))
         outs.append((by_image(1, 1, D), shape_of((images, 1, D), f32)))
     return call(
-        lambda *refs: ffn_both_kernel(layer, with_output, *refs),
+        lambda *refs: ffn_both_kernel(layer, with_output, pieces, *refs),
         "ffn_both_out" if with_output else "ffn_both",
         images,
         ins,
@@ -610,10 +630,10 @@
     return jnp.where(inside & same, 0.0, neg_fill).astype(f32)
 
 
-def inside_column(own_size):
+def inside_rows(own_size):
     rows_of, cols_of = token_places()
     inside = (jnp.asarray(rows_of)[None] < own_size[:, 0:1]) & (jnp.asarray(cols_of)[None] < own_size[:, 1:2])
-    return inside.astype(f32).reshape(-1, 1)
+    return jnp.broadcast_to(inside.astype(bf16)[:, None], (own_size.shape[0], 16, IMG_ROWS))
 
 
 def swap(rows, axis, size, bit):
@@ -652,6 +672,16 @@
     return jnp.sum(lax.all_to_all(parts.astype(bf16), axis, 0, 0).astype(f32), axis=0)
 
 
+def fold_far(near, far, rows, size):
+    kept = near.astype(f32) + swap(far, "tensor", size, 1).astype(f32)
+    bit = 2
+    while bit < size // 2:
+        parts = kept.reshape(2, -1, 2, rows, D)
+        kept = (parts[:, :, 0] + swap(parts[:, :, 1].astype(bf16), "tensor", size, bit).astype(f32)).reshape(2, -1, D)
+        bit *= 2
+    return kept[:, :rows], kept[:, rows:].astype(bf16)
+
+
 def own_block(rows, at, size, axis):
     return lax.dynamic_slice_in_dim(rows, at * size, size, axis)
 
@@ -663,7 +693,7 @@
 def body(n_dp, n_tensor, tokens, cotangent, image_size, vectors, mix_weight, mix_bias, bias_table, out_weight, up_weight, up_bias, down_weight):
     local_images = tokens.shape[0] // IMG_ROWS
     devices = n_dp * n_tensor
-    stages = bits_of("tensor", n_tensor)[::-1] + bits_of("dp", n_dp)[::-1]
+    stages = bits_of("dp", n_dp) + bits_of("tensor", n_tensor)[::-1]
     dp_at, tensor_at = lax.axis_index("dp"), lax.axis_index("tensor")
     own = dp_at * n_tensor + tensor_at
     own_size = lax.dynamic_slice_in_dim(image_size, tensor_at * local_images, local_images, 0)
@@ -676,8 +706,7 @@
     once = (dp_at == 0).astype(bf16)
     part = jnp.zeros((8, 6 * D), bf16)
     part = put(part, vectors, 0, own * vec_own)
-    part = put(part, up_bias[0:1], 2, tensor_at * ff_part + dp_at * ub_own)
-    part = put(part, up_bias[1:2], 3, own * ub_own)
+    part = put(part, up_bias, 2, tensor_at * ff_part + dp_at * ub_own)
     own_bias = mix_bias * once
     part = put(part, own_bias[:, 0], 2, FF + tensor_at * own_cols)
     part = put(part, own_bias[:, 1], 2, FF + D + tensor_at * own_cols)
@@ -688,75 +717,76 @@
     mix_own = mix_weight.transpose(0, 2, 3, 1)
     attn_own = jnp.concatenate([mix_own, out_weight[:, None]], axis=1)
     dense_own = jnp.stack([up_weight.transpose(0, 2, 1), down_weight], axis=1)
-    part, attn_own, dense_own = tied(part, attn_own, dense_own)
 
     dense_part = to_all(dense_own[0], "dp", n_dp)
     attn_w0 = [attn_own[0]] + exchange(lambda s: attn_own[0], "tensor", n_tensor)
     attn_w1 = lax.all_gather(attn_own[1], "tensor", axis=1, tiled=True)
-    dense_w1 = lax.all_gather(dense_own[1], ("dp", "tensor"), axis=1, tiled=True)
+    dense_w1 = lax.all_gather(dense_own[1], ("tensor", "dp"), axis=1, tiled=True)
+
+    at = tensor_at.reshape(1).astype(jnp.int32)
+    masks = [key_masks(own_size, l % 2 == 1) for l in range(LAYERS)]
+    flags = inside_rows(own_size)
     rows = part
-    for count, stage in enumerate(stages[::-1]):
+    for count, stage in enumerate(stages):
         rows = rows + swap(rows, *stage)
-        if count == len(stages) - 3:
+        if count == 0:
+            rows, flags, masks = tied(rows, flags, masks)
+        if count == len(stages) - 2:
             rows, attn_w0 = tied(rows, attn_w0)
     rows = rows.astype(f32)
 
-    at = tensor_at.reshape(1).astype(jnp.int32)
-    masks = [key_masks(own_size, l % 2 == 1) for l in range(LAYERS)]
-    flags = inside_column(own_size)
-
-    rows, dense_part, flags, masks = tied(rows, dense_part, flags, masks)
-    dense_part = dense_part.transpose(1, 0, 2, 3).reshape(2, ff_part, D)
-    dense_w0 = [dense_part] + exchange(lambda s: dense_part, "tensor", n_tensor)
+    rows, dense_part = tied(rows, dense_part)
+    if ub_own % 16:
+        dense_part = dense_part.transpose(1, 0, 2, 3).reshape(2, ff_part, D)
+    dense_w0 = {0: dense_part}
+    for bit in range(n_tensor.bit_length() - 1):
+        dense_w0[1 << bit] = swap(dense_part, "tensor", n_tensor, 1 << bit)
     h0, *kept0, attn_w0 = attn_forward(0, tokens, rows, masks[0], attn_w0, at)
     h0, kept0, attn_w0, dense_w0 = tied(h0, kept0, attn_w0, dense_w0)
-    x1, dense_w0 = ffn_forward(0, h0, rows, dense_w0, at)
+    for s in range(1, n_tensor):
+        if s not in dense_w0:
+            dense_w0[s] = swap(dense_w0[s & (s - 1)], "tensor", n_tensor, s & -s)
+    x1, dense_w0 = ffn_forward(0, h0, rows, [dense_w0[s] for s in range(n_tensor)], at)
     h1, *kept1 = attn_forward(1, x1, rows, masks[1], [attn_w1], at)
 
-    gh1, dense_g1, vf1, output, image_mean = ffn_both(1, h1, cotangent, rows, dense_w1, flags)
-    dense_sum1 = lax.psum_scatter(dense_g1, ("dp", "tensor"), scatter_dimension=1, tiled=True).astype(f32)
-    g1, attn_g1, va1 = attn_backward(1, gh1, x1, rows, attn_w1, kept1)
-    got = exchange(lambda s: own_block(attn_g1, tensor_at ^ s, own_cols, 1), "tensor", n_tensor)
-
-    gh0, dense_g0, vf0 = ffn_both(0, h0, g1, rows, dense_w0)
-    gh0, dense_g0, vf0, got = tied(gh0, dense_g0, vf0, got)
-    attn_t1 = total(own_block(attn_g1, tensor_at, own_cols, 1), got)
-    got = exchange(lambda s: own_block(dense_g0, tensor_at ^ s, ff_part, 1), "tensor", n_tensor)
-    parts1 = lax.all_to_all(attn_t1.astype(bf16).reshape(n_dp, -1, D), "dp", 0, 0)
-    dmix, attn_g0, va0 = attn_backward_core(0, gh0, attn_w0, kept0)
-    dmix, attn_g0, va0, got, parts1 = tied(dmix, attn_g0, va0, got, parts1)
-    dense_t0 = total(own_block(dense_g0, tensor_at, ff_part, 1), got).astype(bf16)
-    got = exchange(lambda s: own_block(attn_g0, tensor_at ^ s, own_cols, 1), "tensor", n_tensor)
-    blocks = dense_t0.reshape(2, n_dp, ub_own, D).transpose(1, 0, 2, 3)
-    blocks = lax.all_to_all(blocks, "dp", 0, 0)
-    whole1 = to_all(jnp.sum(parts1.astype(f32), axis=0).astype(bf16), "dp", n_dp)
+    gh1, near, far, vf1, output, image_mean = ffn_both(1, h1, cotangent, rows, dense_w1, at, n_tensor, flags)
+    gh1, near, far = tied(gh1, near, far)
+    kept, far = fold_far(near, far, ff_part, n_tensor)
+    gh1, far = tied(gh1, far)
+    got = swap(far, "tensor", n_tensor, n_tensor // 2)
+    g1, *attn_g1, va1 = attn_backward(1, gh1, x1, rows, attn_w1, kept1, at, n_tensor)
+    g1, attn_g1, va1, got = tied(g1, attn_g1, va1, got)
+    got1 = exchange(lambda s: attn_g1[s], "tensor", n_tensor)
+    blocks1 = (kept + got.astype(f32)).astype(bf16).reshape(2, n_dp, ub_own, D).transpose(1, 0, 2, 3)
+    blocks1 = lax.all_to_all(blocks1, "dp", 0, 0)
+
+    gh0, near, far, vf0 = ffn_both(0, h0, g1, rows, dense_w0, at, n_tensor)
+    gh0, near, far, vf0, got1, blocks1 = tied(gh0, near, far, vf0, got1, blocks1)
+    kept, far = fold_far(near, far, ff_part, n_tensor)
+    gh0, far = tied(gh0, far)
+    got0 = swap(far, "tensor", n_tensor, n_tensor // 2)
+    dmix, *attn_g0, va0 = attn_backward_core(0, gh0, attn_w0, kept0, at, n_tensor)
+    dmix, attn_g0, va0, got0, got1 = tied(dmix, attn_g0, va0, got0, got1)
+    got = exchange(lambda s: attn_g0[s], "tensor", n_tensor)
+    blocks0 = (kept + got0.astype(f32)).astype(bf16).reshape(2, n_dp, ub_own, D).transpose(1, 0, 2, 3)
+    blocks0 = lax.all_to_all(blocks0, "dp", 0, 0)
     g0, vn0 = attn_backward_norm(0, gh0, tokens, rows, attn_w0, dmix)
-    g0, vn0, got, blocks, whole1, dense_sum1 = tied(g0, vn0, got, blocks, whole1, dense_sum1)
-    attn_t0 = total(own_block(attn_g0, tensor_at, own_cols, 1), got)
-    dense_sum0 = jnp.sum(blocks.astype(f32), axis=0)
-
+    g0, vn0, got = tied(g0, vn0, got)
+    dense_sum1 = jnp.sum(blocks1.astype(f32), axis=0)
+    dense_sum0 = jnp.sum(blocks0.astype(f32), axis=0)
+
+    attn_sums = [total(attn_g0[0], got), total(attn_g1[0], got1)]
+    matrices = jnp.concatenate(attn_sums).astype(bf16).reshape(n_dp, -1, D)
+    sums = sum_parts(matrices, "dp")
     small = vf0 + vf1 + va0 + va1 + vn0
-    for stage in bits_of("tensor", n_tensor)[::-1]:
+    stages = bits_of("tensor", n_tensor)[::-1] + bits_of("dp", n_dp)[::-1]
+    for count, stage in enumerate(stages):
         small = small + swap(small, *stage)
-    small_rows = -(-small.size // (D * n_dp))
-    small = small.reshape(-1, D)
-    small = jnp.pad(small, ((0, small_rows * n_dp - small.shape[0]), (0, 0))).reshape(n_dp, small_rows, D)
-    matrices = attn_t0.reshape(n_dp, -1, D)
-    matrix_rows = matrices.shape[1]
-    sums = sum_parts(jnp.concatenate([matrices.astype(bf16), small.astype(bf16)], axis=1), "dp")
-    whole0 = to_all(sums.astype(bf16), "dp", n_dp)
-    attn_all = [
-        rows.astype(f32).reshape(4, own_cols, D) for rows in (whole0[:, :matrix_rows], whole1)
-    ]
-    attn_all = jnp.stack(attn_all)
-    small = whole0[:, matrix_rows:].astype(f32).reshape(-1, D)[: 8 * 6].reshape(8, 6 * D)
+        if count == n_tensor.bit_length():
+            small, sums = tied(small, sums)
+    attn_all = to_all(sums.astype(bf16), "dp", n_dp).astype(f32).reshape(LAYERS, 4, own_cols, D)
     vectors_grad = lax.dynamic_slice(small, (0, own * vec_own), (LAYERS, vec_own))
-    up_bias_grad = jnp.concatenate(
-        [
-            lax.dynamic_slice(small, (2, tensor_at * ff_part + dp_at * ub_own), (1, ub_own)),
-            lax.dynamic_slice(small, (3, own * ub_own), (1, ub_own)),
-        ]
-    )
+    up_bias_grad = lax.dynamic_slice(small, (2, tensor_at * ff_part + dp_at * ub_own), (LAYERS, ub_own))
     mix_bias_grad = jnp.stack(
         [lax.dynamic_slice(small, (2, FF + c * D + tensor_at * own_cols), (LAYERS, own_cols)) for c in range(2)], axis=1
     )

time: 311 us -> 300 us (0.965)
  local copies, waits for them, and re-layouts: 18.1 us -> 12.8 us
  other arithmetic: 15.8 us -> 11.9 us
    ppermute x22 -> x26, waiting for transfers between devices: 28.5 us -> 49.1 us  [swap(): return lax.ppermute(rows, axis, [(i, i ^ bit) for i in range(size)])]
    all_to_all x3 -> x2, waiting for transfers between devices: 16.2 us -> 0.01 us  [to_all(): lax.all_to_all(jnp.broadcast_to(rows[None], (size,) + rows.shape), axis,...]
    all_to_all x1, waiting for transfers between devices: 9.63 us -> 0.01 us  [sum_parts(): lax.all_to_all(parts.astype(bf16), axis, 0, 0).astype(f32)]
    ppermute x22 -> x26, starting transfers between devices: 22.8 us -> 30.7 us  [swap(): return lax.ppermute(rows, axis, [(i, i ^ bit) for i in range(size)])]
    all_to_all x3 -> x2, starting transfers between devices: 13.6 us -> 7.95 us  [to_all(): lax.all_to_all(jnp.broadcast_to(rows[None], (size,) + rows.shape), axis,...]
    convert_element_type x6 -> x3, other arithmetic: 5.61 us -> 0.31 us  [the longest x1 0.12 us: body(): (kept + got.astype(f32)).astype(bf16).reshape(2, n_dp, ub_own, D)]
    dynamic_slice x4 -> x1, local copies, waits for them, and re-layouts: 3.99 us -> 0.63 us  [body(): lax.dynamic_slice(small, (2, tensor_at * ff_part + dp_at * ub_own), (LAYE...]
  transfers between devices with their start and end apart: 31 -> 33, of which waited for: 11 -> 14; matrix products, arithmetic and copies ran while one was open for 6% -> 5% of each run, Pallas kernels for 41% -> 43%
where the time goes in v4:
time: 300 us; the launch traced here: 297 us
  Pallas kernels  150 us (50%)
  starting transfers between devices  54.6 us (18%)
  waiting for transfers between devices  51.6 us (17%)
  between operations  15.3 us (5%)
  local copies, waits for them, and re-layouts  12.8 us (4%)
  other arithmetic  11.9 us (4%)
    ppermute x26, waiting for transfers between devices, swap(): return lax.ppermute(rows, axis, [(i, i ^ bit) for i in range(size)])  49.1 us
    pallas_call x2, Pallas kernels, ffn_both(): call(lambda *refs: ffn_both_kernel(layer, with_output, pieces, *refs), 'f...  43.5 us
    pallas_call x2, Pallas kernels, attn_forward(): call(lambda *refs: attn_fwd_kernel(layer, pieces, *refs), 'attn_fwd', ima...  36.2 us
    ppermute x26, starting transfers between devices, swap(): return lax.ppermute(rows, axis, [(i, i ^ bit) for i in range(size)])  30.7 us
    pallas_call x1, Pallas kernels, attn_backward(): call(lambda *refs: attn_bwd_kernel(layer, *refs), 'attn_bwd', images, [by...  28.9 us
    pallas_call x1, Pallas kernels, attn_backward_core(): call(lambda *refs: attn_core_kernel(layer, *refs), 'attn_core', images, [...  24.2 us
    pallas_call x1, Pallas kernels, ffn_forward(): call(lambda *refs: ffn_fwd_kernel(layer, len(weights), *refs), 'ffn_fwd',...  9.35 us
    pallas_call x1, Pallas kernels, attn_backward_norm(): call(lambda *refs: attn_norm_kernel(layer, *refs), 'attn_norm', images, [...  8.09 us
  transfers between devices with their start and end apart: 33, of which 14 were waited for; matrix products, arithmetic and copies ran while one was open for 5% of the time, Pallas kernels for 43%

profile of v4, /device:TPU:0, one launch (start us, length us, event | category | flops | bytes accessed | tf_op | source)
XLA Modules:
  0.0 296.5 jit_solution(6563792952341875299)
XLA Ops:
  10.1 2.4 collective-permute-start.6
  15.1 3.1 %collective-permute-start = (bf16[8,2304]{1,0:T(8,128)(2,1)S(1)}, bf16[8,2304]{1,0:T(8,128)(2,1)S(1)}, u32[]{:S(2)}, u32[]{:S(2)}) collective-permute-start(bf16[8,2304]{1,0:T(8,128)(2,1)S(1)} %dynamic_update_slice.23), channel_id=1, source_target_pairs={{0,16},{4,20},{8,24},{12,28},{16,0},{20,4},{24,8},{28,12},{1,17},{... | collective-permute-start | bytes 110600 | tf_op jit(solution)/shard_map/ppermute | solution.py:640
  19.1 4.4 %all-to-all-start = ((bf16[8,2,48,384]{3,2,1,0:T(8,128)(2,1)}), bf16[8,2,48,384]{3,2,1,0:T(8,128)(2,1)S(1)}, u32[]{:S(2)}, u32[]{:S(2)}) async-start(bf16[8,2,48,384]{3,2,1,0:T(8,128)(2,1)} %broadcast_in_dim.51), calls=%async_computation | async-start | bytes 1179648 | tf_op jit(solution)/shard_map/all_to_all | solution.py:668
  29.4 5.0 %collective-permute-done.1 = bf16[8,2304]{1,0:T(8,128)(2,1)S(1)} collective-permute-done((bf16[8,2304]{1,0:T(8,128)(2,1)S(1)}, bf16[8,2304]{1,0:T(8,128)(2,1)S(1)}, u32[]{:S(2)}, u32[]{:S(2)}) %collective-permute-start.1) | collective-permute-done | bytes 36896 | tf_op jit(solution)/shard_map/ppermute | solution.py:640
  46.1 17.9 %attn_fwd.2 = (f32[1568,384]{1,0:T(8,128)}, bf16[2048,384]{1,0:T(8,128)(2,1)}, bf16[2048,1152]{1,0:T(8,128)(2,1)}, bf16[2,8,3,128,512]{4,3,2,1,0:T(8,128)(2,1)},...) custom-call(bf16[1568,384]{1,0:T(8,128)(2,1)} %refs_1_.3, f32[8,2304]{1,0:T(8,128)} %add_convert_fusion.2.refs_1_.refs_2_, ...), custom_call_target="tpu_custom_call" | custom-call | flops 100000000 | bytes 100000 | tf_op jit(solution)/shard_map/attn_fwd/pallas_call | solution.py:497
  67.0 9.3 %ffn_fwd.1 = (f32[1568,384]{1,0:T(8,128)}, bf16[2,1536,384]{2,1,0:T(8,128)(2,1)}) custom-call(f32[1568,384]{1,0:T(8,128)} %get-tuple-element.122.refs_0_, f32[8,2304]{1,0:T(8,128)} %add_convert_fusion.2.refs_1_.refs_2_, bf16[8,2,48,384]{3,2,1,0:T(8,128)(2,1)} %copy-done.2, bf16[8,2,48,384]{3,2,1,0:T(8,128)(2,1)} %copy-done.5, ...), custom_call_target="tpu_custom_call" | custom-call | flops 100000000 | bytes 100000 | tf_op jit(solution)/shard_map/ffn_fwd/pallas_call | solution.py:582
  76.4 18.4 %attn_fwd.3 = (f32[1568,384]{1,0:T(8,128)}, bf16[2048,384]{1,0:T(8,128)(2,1)}, bf16[2048,1152]{1,0:T(8,128)(2,1)}, bf16[2,8,3,128,512]{4,3,2,1,0:T(8,128)(2,1)}, bf16[1568,384]{1,0:T(8,128)(2,1)}) custom-call(f32[1568,384]{1,0:T(8,128)} %get-tuple-element.126.refs_0_.refs_1_, f32[8,2304]{1,0:T(8,128)} %add_convert_fusion.2.refs_1_.refs_2_, ...), custom_call_target="tpu_custom_call" | custom-call | flops 100000000 | bytes 100000 | tf_op jit(solution)/shard_map/attn_fwd/pallas_call | solution.py:497
  97.2 23.2 %ffn_both_out.1 = (f32[1568,384]{1,0:T(8,128)}, bf16[2,768,384]{2,1,0:T(8,128)(2,1)}, bf16[2,768,384]{2,1,0:T(8,128)(2,1)}, f32[8,2304]{1,0:T(8,128)}, bf16[1568,384]{1,0:T(8,128)(2,1)}, /*index=5*/f32[2,1,384]{2,1,0:T(1,128)}) custom-call(f32[1568,384]{1,0:T(8,128)} %get-tuple-element.128.refs_0_, bf16[1568,384]{1,0:T(8,128)(2,1)} %refs_1_.2, ...), custom_call_target="tpu_custom_call" | custom-call | flops 100000000 | bytes 100000 | tf_op jit(solution)/shard_map/ffn_both_out/pallas_call | solution.py:611
  120.8 2.8 collective-permute-done.11
  126.7 28.9 %attn_bwd.1 = (f32[1568,384]{1,0:T(8,128)}, bf16[4,96,384]{2,1,0:T(8,128)(2,1)}, bf16[4,96,384]{2,1,0:T(8,128)(2,1)}, bf16[4,96,384]{2,1,0:T(8,128)(2,1)}, bf16[...) custom-call(f32[1568,384]{1,0:T(8,128)} %get-tuple-element.138.refs_0_, f32[1568,384]{1,0:T(8,128)} %get-tuple-element.126.refs_0_.refs_1_, ...), custom_call_target="tpu_custom_call" | custom-call | flops 100000000 | bytes 100000 | tf_op jit(solution)/shard_map/attn_bwd/pallas_call | solution.py:522
  156.6 3.8 %all-to-all-start.1 = ((bf16[8,2,48,384]{3,2,1,0:T(8,128)(2,1)}), bf16[8,2,48,384]{3,2,1,0:T(8,128)(2,1)S(1)}, u32[]{:S(2)}, u32[]{:S(2)}) async-start(bf16[8,2,48,384]{3,2,1,0:T(8,128)(2,1)} %bitcast.62), calls=%async_computation.1 | async-start | bytes 1179648 | tf_op jit(solution)/shard_map/all_to_all | solution.py:761
  162.4 20.3 %ffn_both.1 = (f32[1568,384]{1,0:T(8,128)}, bf16[2,768,384]{2,1,0:T(8,128)(2,1)}, bf16[2,768,384]{2,1,0:T(8,128)(2,1)}, f32[8,2304]{1,0:T(8,128)}) custom-call(f32[1568,384]{1,0:T(8,128)} %get-tuple-element.122.refs_0_, f32[1568,384]{1,0:T(8,128)} %get-tuple-element.150.refs_1_, f32[8,2304]{1,0:T(8,128)} %add_convert_fusion.2.refs_1_.refs_2_, ...), custom_call_target="tpu_custom_call" | custom-call | flops 100000000 | bytes 100000 | tf_op jit(solution)/shard_map/ffn_both/pallas_call | solution.py:611
  183.1 2.7 collective-permute-done.16
  189.0 24.2 %attn_core.1 = (bf16[2048,1152]{1,0:T(8,128)(2,1)}, bf16[4,96,384]{2,1,0:T(8,128)(2,1)}, bf16[4,96,384]{2,1,0:T(8,128)(2,1)}, bf16[4,96,384]{2,1,0:T(8,128)(2,1)...) custom-call(f32[1568,384]{1,0:T(8,128)} %get-tuple-element.163.refs_0_, ...), custom_call_target="tpu_custom_call" | custom-call | flops 100000000 | bytes 100000 | tf_op jit(solution)/shard_map/attn_core/pallas_call | solution.py:545
  214.2 6.0 %all-to-all-start.4 = ((bf16[8,2,48,384]{3,2,1,0:T(8,128)(2,1)}), bf16[8,2,48,384]{3,2,1,0:T(8,128)(2,1)S(1)}, u32[]{:S(2)}, u32[]{:S(2)}) async-start(bf16[8,2,48,384]{3,2,1,0:T(8,128)(2,1)} %bitcast.61), calls=%async_computation.4 | async-start | bytes 1179648 | tf_op jit(solution)/shard_map/all_to_all | solution.py:772
  222.2 8.1 %attn_norm.1 = (f32[1568,384]{1,0:T(8,128)}, f32[8,2304]{1,0:T(8,128)}) custom-call(f32[1568,384]{1,0:T(8,128)} %get-tuple-element.163.refs_0_, bf16[1568,384]{1,0:T(8,128)(2,1)} %refs_1_.3, f32[8,2304]{1,0:T(8,128)} %add_convert_fusion.2.refs_1_.refs_2_, bf16[4,384,384]{2,1,0:T(8,128)(2,1)} %get-tuple-element.164.refs_1_.refs_3_, ...), custom_call_target="tpu_custom_call" | custom-call | flops 100000000 | bytes 100000 | tf_op jit(solution)/shard_map/attn_norm/pallas_call | solution.py:561
  230.5 5.1 %collective-permute-done.20 = bf16[4,96,384]{2,1,0:T(8,128)(2,1)S(1)} collective-permute-done((bf16[4,96,384]{2,1,0:T(8,128)(2,1)S(1)}, bf16[4,96,384]{2,1,0:T(8,128)(2,1)S(1)}, u32[]{:S(2)}, u32[]{:S(2)}) %collective-permute-start.20) | collective-permute-done | bytes 294944 | tf_op jit(solution)/shard_map/ppermute | solution.py:640
  236.7 6.1 %all-to-all-start.2 = ((bf16[8,96,384]{2,1,0:T(8,128)(2,1)}), bf16[8,96,384]{2,1,0:T(8,128)(2,1)S(1)}, u32[]{:S(2)}, u32[]{:S(2)}) async-start(bf16[8,96,384]{2,1,0:T(8,128)(2,1)} %pad_maximum_fusion), calls=%async_computation.2 | async-start | bytes 1179648 | tf_op jit(solution)/shard_map/all_to_all | solution.py:672
  245.4 3.2 %collective-permute-done.22 = f32[8,2304]{1,0:T(8,128)S(1)} collective-permute-done((f32[8,2304]{1,0:T(8,128)S(1)}, f32[8,2304]{1,0:T(8,128)S(1)}, u32[]{:S(2)}, u32[]{:S(2)}) %collective-permute-start.22) | collective-permute-done | bytes 73760 | tf_op jit(solution)/shard_map/ppermute | solution.py:640
  253.1 3.4 %collective-permute-start.24 = (f32[8,2304]{1,0:T(8,128)S(1)}, f32[8,2304]{1,0:T(8,128)S(1)}, u32[]{:S(2)}, u32[]{:S(2)}) collective-permute-start(f32[8,2304]{1,0:T(8,128)S(1)} %add.183), channel_id=1, source_target_pairs={{0,8},{4,12},{8,0},{12,4},{16,24},{20,28},{24,16},{28,20},{1,9},{5... | collective-permute-start | bytes 221192 | tf_op jit(solution)/shard_map/ppermute | solution.py:640
  256.5 4.2 %collective-permute-done.24 = f32[8,2304]{1,0:T(8,128)S(1)} collective-permute-done((f32[8,2304]{1,0:T(8,128)S(1)}, f32[8,2304]{1,0:T(8,128)S(1)}, u32[]{:S(2)}, u32[]{:S(2)}) %collective-permute-start.24) | collective-permute-done | bytes 73760 | tf_op jit(solution)/shard_map/ppermute | solution.py:640
  261.8 3.5 %all-to-all-start.3 = ((bf16[8,96,384]{2,1,0:T(8,128)(2,1)}), bf16[8,96,384]{2,1,0:T(8,128)(2,1)S(1)}, u32[]{:S(2)}, u32[]{:S(2)}) async-start(bf16[8,96,384]{2,1,0:T(8,128)(2,1)} %broadcast_in_dim.52), calls=%async_computation.3 | async-start | bytes 1179648 | tf_op jit(solution)/shard_map/all_to_all | solution.py:668
  266.0 2.8 collective-permute-start.25
  269.5 15.2 %collective-permute-done.25 = f32[8,2304]{1,0:T(8,128)S(1)} collective-permute-done((f32[8,2304]{1,0:T(8,128)S(1)}, f32[8,2304]{1,0:T(8,128)S(1)}, u32[]{:S(2)}, u32[]{:S(2)}) %collective-permute-start.25) | collective-permute-done | bytes 73760 | tf_op jit(solution)/shard_map/ppermute | solution.py:640
  (193 shorter events, 57.1 us)
Async XLA Ops:
  7.3 69.1 %all-gather.5.cloned.1.call-start = ((), (), s32[]{:S(2)}) async-start(), calls=%async_computation.5 | async-start | bytes 1474560 | tf_op jit(solution)/shard_map/all_gather | solution.py:723
  9.3 87.9 %all-gather.7.cloned.1.call-start = ((), (), s32[]{:S(2)}) async-start(), calls=%async_computation.6 | async-start | bytes 2433024 | tf_op jit(solution)/shard_map/all_gather | solution.py:724
  10.1 29.7 %collective-permute-start.6 = (bf16[4,96,384]{2,1,0:T(8,128)(2,1)S(1)}, bf16[4,96,384]{2,1,0:T(8,128)(2,1)S(1)}, u32[]{:S(2)}, u32[]{:S(2)}) collective-permute-start(bf16[4,96,384]{2,1,0:T(8,128)(2,1)S(1)} %get-tuple-element.111.refs_3_), channel_id=1, source_target_pairs={{0,3},{1,2},{2,1},{3,0},{4,7},{5,6},{6,5},{7,4},{8,11},{9,10},{10,... | collective-permute-start | bytes 884744 | tf_op jit(solution)/shard_map/ppermute | solution.py:640
  12.5 27.3 %collective-permute-start.5 = (bf16[4,96,384]{2,1,0:T(8,128)(2,1)S(1)}, bf16[4,96,384]{2,1,0:T(8,128)(2,1)S(1)}, u32[]{:S(2)}, u32[]{:S(2)}) collective-permute-start(bf16[4,96,384]{2,1,0:T(8,128)(2,1)S(1)} %get-tuple-element.111.refs_3_), channel_id=1, source_target_pairs={{0,2},{1,3},{2,0},{3,1},{4,6},{5,7},{6,4},{7,5},{8,10},{9,11},{10,... | collective-permute-start | bytes 884744 | tf_op jit(solution)/shard_map/ppermute | solution.py:640
  13.2 26.7 %collective-permute-start.4 = (bf16[4,96,384]{2,1,0:T(8,128)(2,1)S(1)}, bf16[4,96,384]{2,1,0:T(8,128)(2,1)S(1)}, u32[]{:S(2)}, u32[]{:S(2)}) collective-permute-start(bf16[4,96,384]{2,1,0:T(8,128)(2,1)S(1)} %get-tuple-element.111.refs_3_), channel_id=1, source_target_pairs={{0,1},{1,0},{2,3},{3,2},{4,5},{5,4},{6,7},{7,6},{8,9},{9,8},{10,11... | collective-permute-start | bytes 884744 | tf_op jit(solution)/shard_map/ppermute | solution.py:640
  15.1 10.3 %collective-permute-start = (bf16[8,2304]{1,0:T(8,128)(2,1)S(1)}, bf16[8,2304]{1,0:T(8,128)(2,1)S(1)}, u32[]{:S(2)}, u32[]{:S(2)}) collective-permute-start(bf16[8,2304]{1,0:T(8,128)(2,1)S(1)} %dynamic_update_slice.23), channel_id=1, source_target_pairs={{0,16},{4,20},{8,24},{12,28},{16,0},{20,4},{24,8},{28,12},{1,17},{... | collective-permute-start | bytes 110600 | tf_op jit(solution)/shard_map/ppermute | solution.py:640
  19.1 25.4 %all-to-all-start = ((bf16[8,2,48,384]{3,2,1,0:T(8,128)(2,1)}), bf16[8,2,48,384]{3,2,1,0:T(8,128)(2,1)S(1)}, u32[]{:S(2)}, u32[]{:S(2)}) async-start(bf16[8,2,48,384]{3,2,1,0:T(8,128)(2,1)} %broadcast_in_dim.51), calls=%async_computation | async-start | bytes 1179648 | tf_op jit(solution)/shard_map/all_to_all | solution.py:668
  27.4 7.0 %collective-permute-start.1 = (bf16[8,2304]{1,0:T(8,128)(2,1)S(1)}, bf16[8,2304]{1,0:T(8,128)(2,1)S(1)}, u32[]{:S(2)}, u32[]{:S(2)}) collective-permute-start(bf16[8,2304]{1,0:T(8,128)(2,1)S(1)} %add.168), channel_id=1, source_target_pairs={{0,8},{4,12},{8,0},{12,4},{16,24},{20,28},{24,16},{28,20},{1,9},{5... | collective-permute-start | bytes 110600 | tf_op jit(solution)/shard_map/ppermute | solution.py:640
  44.5 19.5 %collective-permute-start.9 = (bf16[8,2,48,384]{3,2,1,0:T(8,128)(2,1)S(1)}, bf16[8,2,48,384]{3,2,1,0:T(8,128)(2,1)S(1)}, u32[]{:S(2)}, u32[]{:S(2)}) collective-permute-start(bf16[8,2,48,384]{3,2,1,0:T(8,128)(2,1)S(1)} %all-to-all-done.refs_2_), channel_id=1, source_target_pairs={{0,2},{1,3},{2,0},{3,1},{4,6},{5,7},{6,4},{7,5},{8,10},{9,11},{10,... | collective-permute-start | bytes 1769480 | tf_op jit(solution)/shard_map/ppermute | solution.py:640
  46.1 17.9 %collective-permute-start.8 = (bf16[8,2,48,384]{3,2,1,0:T(8,128)(2,1)S(1)}, bf16[8,2,48,384]{3,2,1,0:T(8,128)(2,1)S(1)}, u32[]{:S(2)}, u32[]{:S(2)}) collective-permute-start(bf16[8,2,48,384]{3,2,1,0:T(8,128)(2,1)S(1)} %all-to-all-done.refs_2_), channel_id=1, source_target_pairs={{0,1},{1,0},{2,3},{3,2},{4,5},{5,4},{6,7},{7,6},{8,9},{9,8},{10,11... | collective-permute-start | bytes 1769480 | tf_op jit(solution)/shard_map/ppermute | solution.py:640
  125.2 30.4 %collective-permute-start.12 = (bf16[2,384,384]{2,1,0:T(8,128)(2,1)S(1)}, bf16[2,384,384]{2,1,0:T(8,128)(2,1)S(1)}, u32[]{:S(2)}, u32[]{:S(2)}) collective-permute-start(bf16[2,384,384]{2,1,0:T(8,128)(2,1)S(1)} %slice.152), channel_id=1, source_target_pairs={{0,2},{1,3},{2,0},{3,1},{4,6},{5,7},{6,4},{7,5},{8,10},{9,11},{10,... | collective-permute-start | bytes 1769480 | tf_op jit(solution)/shard_map/ppermute | solution.py:640
  156.6 26.1 %all-to-all-start.1 = ((bf16[8,2,48,384]{3,2,1,0:T(8,128)(2,1)}), bf16[8,2,48,384]{3,2,1,0:T(8,128)(2,1)S(1)}, u32[]{:S(2)}, u32[]{:S(2)}) async-start(bf16[8,2,48,384]{3,2,1,0:T(8,128)(2,1)} %bitcast.62), calls=%async_computation.1 | async-start | bytes 1179648 | tf_op jit(solution)/shard_map/all_to_all | solution.py:761
  160.4 22.3 %collective-permute-start.13 = (bf16[4,96,384]{2,1,0:T(8,128)(2,1)S(1)}, bf16[4,96,384]{2,1,0:T(8,128)(2,1)S(1)}, u32[]{:S(2)}, u32[]{:S(2)}) collective-permute-start(bf16[4,96,384]{2,1,0:T(8,128)(2,1)S(1)} %copy-done.36), channel_id=1, source_target_pairs={{0,1},{1,0},{2,3},{3,2},{4,5},{5,4},{6,7},{7,6},{8,9},{9,8},{10,11... | collective-permute-start | bytes 884744 | tf_op jit(solution)/shard_map/ppermute | solution.py:640
  160.5 22.2 %collective-permute-start.14 = (bf16[4,96,384]{2,1,0:T(8,128)(2,1)S(1)}, bf16[4,96,384]{2,1,0:T(8,128)(2,1)S(1)}, u32[]{:S(2)}, u32[]{:S(2)}) collective-permute-start(bf16[4,96,384]{2,1,0:T(8,128)(2,1)S(1)} %copy-done.34), channel_id=1, source_target_pairs={{0,2},{1,3},{2,0},{3,1},{4,6},{5,7},{6,4},{7,5},{8,10},{9,11},{10,... | collective-permute-start | bytes 884744 | tf_op jit(solution)/shard_map/ppermute | solution.py:640
  162.0 20.7 %collective-permute-start.15 = (bf16[4,96,384]{2,1,0:T(8,128)(2,1)S(1)}, bf16[4,96,384]{2,1,0:T(8,128)(2,1)S(1)}, u32[]{:S(2)}, u32[]{:S(2)}) collective-permute-start(bf16[4,96,384]{2,1,0:T(8,128)(2,1)S(1)} %copy-done.32), channel_id=1, source_target_pairs={{0,3},{1,2},{2,1},{3,0},{4,7},{5,6},{6,5},{7,4},{8,11},{9,10},{10,... | collective-permute-start | bytes 884744 | tf_op jit(solution)/shard_map/ppermute | solution.py:640
  187.4 25.7 %collective-permute-start.17 = (bf16[2,384,384]{2,1,0:T(8,128)(2,1)S(1)}, bf16[2,384,384]{2,1,0:T(8,128)(2,1)S(1)}, u32[]{:S(2)}, u32[]{:S(2)}) collective-permute-start(bf16[2,384,384]{2,1,0:T(8,128)(2,1)S(1)} %slice.151), channel_id=1, source_target_pairs={{0,2},{1,3},{2,0},{3,1},{4,6},{5,7},{6,4},{7,5},{8,10},{9,11},{10,... | collective-permute-start | bytes 1769480 | tf_op jit(solution)/shard_map/ppermute | solution.py:640
  214.2 22.5 %all-to-all-start.4 = ((bf16[8,2,48,384]{3,2,1,0:T(8,128)(2,1)}), bf16[8,2,48,384]{3,2,1,0:T(8,128)(2,1)S(1)}, u32[]{:S(2)}, u32[]{:S(2)}) async-start(bf16[8,2,48,384]{3,2,1,0:T(8,128)(2,1)} %bitcast.61), calls=%async_computation.4 | async-start | bytes 1179648 | tf_op jit(solution)/shard_map/all_to_all | solution.py:772
  220.2 10.2 %collective-permute-start.18 = (bf16[4,96,384]{2,1,0:T(8,128)(2,1)S(1)}, bf16[4,96,384]{2,1,0:T(8,128)(2,1)S(1)}, u32[]{:S(2)}, u32[]{:S(2)}) collective-permute-start(bf16[4,96,384]{2,1,0:T(8,128)(2,1)S(1)} %copy-done.35), channel_id=1, source_target_pairs={{0,1},{1,0},{2,3},{3,2},{4,5},{5,4},{6,7},{7,6},{8,9},{9,8},{10,11... | collective-permute-start | bytes 884744 | tf_op jit(solution)/shard_map/ppermute | solution.py:640
  220.3 10.1 %collective-permute-start.19 = (bf16[4,96,384]{2,1,0:T(8,128)(2,1)S(1)}, bf16[4,96,384]{2,1,0:T(8,128)(2,1)S(1)}, u32[]{:S(2)}, u32[]{:S(2)}) collective-permute-start(bf16[4,96,384]{2,1,0:T(8,128)(2,1)S(1)} %copy-done.33), channel_id=1, source_target_pairs={{0,2},{1,3},{2,0},{3,1},{4,6},{5,7},{6,4},{7,5},{8,10},{9,11},{10,... | collective-permute-start | bytes 884744 | tf_op jit(solution)/shard_map/ppermute | solution.py:640
  221.0 14.6 %collective-permute-start.20 = (bf16[4,96,384]{2,1,0:T(8,128)(2,1)S(1)}, bf16[4,96,384]{2,1,0:T(8,128)(2,1)S(1)}, u32[]{:S(2)}, u32[]{:S(2)}) collective-permute-start(bf16[4,96,384]{2,1,0:T(8,128)(2,1)S(1)} %copy-done.31), channel_id=1, source_target_pairs={{0,3},{1,2},{2,1},{3,0},{4,7},{5,6},{6,5},{7,4},{8,11},{9,10},{10,... | collective-permute-start | bytes 884744 | tf_op jit(solution)/shard_map/ppermute | solution.py:640
  236.7 24.1 %all-to-all-start.2 = ((bf16[8,96,384]{2,1,0:T(8,128)(2,1)}), bf16[8,96,384]{2,1,0:T(8,128)(2,1)S(1)}, u32[]{:S(2)}, u32[]{:S(2)}) async-start(bf16[8,96,384]{2,1,0:T(8,128)(2,1)} %pad_maximum_fusion), calls=%async_computation.2 | async-start | bytes 1179648 | tf_op jit(solution)/shard_map/all_to_all | solution.py:672
  253.1 7.6 %collective-permute-start.24 = (f32[8,2304]{1,0:T(8,128)S(1)}, f32[8,2304]{1,0:T(8,128)S(1)}, u32[]{:S(2)}, u32[]{:S(2)}) collective-permute-start(f32[8,2304]{1,0:T(8,128)S(1)} %add.183), channel_id=1, source_target_pairs={{0,8},{4,12},{8,0},{12,4},{16,24},{20,28},{24,16},{28,20},{1,9},{5... | collective-permute-start | bytes 221192 | tf_op jit(solution)/shard_map/ppermute | solution.py:640
  261.8 25.7 %all-to-all-start.3 = ((bf16[8,96,384]{2,1,0:T(8,128)(2,1)}), bf16[8,96,384]{2,1,0:T(8,128)(2,1)S(1)}, u32[]{:S(2)}, u32[]{:S(2)}) async-start(bf16[8,96,384]{2,1,0:T(8,128)(2,1)} %broadcast_in_dim.52), calls=%async_computation.3 | async-start | bytes 1179648 | tf_op jit(solution)/shard_map/all_to_all | solution.py:668
  266.0 18.7 %collective-permute-start.25 = (f32[8,2304]{1,0:T(8,128)S(1)}, f32[8,2304]{1,0:T(8,128)S(1)}, u32[]{:S(2)}, u32[]{:S(2)}) collective-permute-start(f32[8,2304]{1,0:T(8,128)S(1)} %add.184), channel_id=1, source_target_pairs={{0,16},{4,20},{8,24},{12,28},{16,0},{20,4},{24,8},{28,12},{1,17},{... | collective-permute-start | bytes 221192 | tf_op jit(solution)/shard_map/ppermute | solution.py:640
  (46 other events, 310.4 us)
Sparse Core Ops, SparseCore 0:
  10.2 23.9 all-gather.4
  37.7 59.5 all-gather.6

commit v5 on v4

--- a/solution.py
+++ b/solution.py
@@ -388,17 +388,25 @@
     x_ref[...] = out
 
 
-def ffn_both_kernel(layer, with_output, pieces, *refs):
+def ffn_both_kernel(layer, with_output, pieces, parts, *refs):
     if with_output:
-        h_ref, g_ref, sm_ref, w_ref, at_ref, in_ref, gh_ref, near_ref, far_ref, vg_ref, x_ref, mean_ref, a2_ref, gm_ref, m_ref, dz_ref = refs
+        h_ref, g_ref, sm_ref, at_ref, in_ref, *refs = refs
     else:
-        h_ref, g_ref, sm_ref, w_ref, at_ref, gh_ref, near_ref, far_ref, vg_ref, a2_ref, gm_ref, m_ref, dz_ref = refs
+        h_ref, g_ref, sm_ref, at_ref, *refs = refs
+    w_refs, refs = refs[:parts], refs[parts:]
+    gh_ref, near_ref, far_ref, vg_ref, *refs = refs
+    if with_output:
+        x_ref, mean_ref, *refs = refs
+    a2_ref, gm_ref, m_ref, dz_ref, *merged = refs
+    w_ref = merged[0] if merged else w_refs[0]
     image = pl.program_id(0)
     here = pl.ds(pl.multiple_of(image * IMG_ROWS, 16), IMG_ROWS)
 
     @pl.when(image == 0)
     def _():
         vg_ref[...] = jnp.zeros_like(vg_ref)
+        if merged:
+            merge_pieces(at_ref, w_refs, w_ref)
 
     h = h_ref[...]
     unit, scale = normalize(h)
@@ -481,7 +489,7 @@
     images = x.shape[0] // IMG_ROWS
     tokens, padded, pieces = images * IMG_ROWS, images * PAD_ROWS, len(weights)
     ins = [by_image(IMG_ROWS, D), whole(8, 6 * D), by_image(1, PAIRS, 128, 128)]
-    ins += [whole(*piece.shape) for piece in weights]
+    ins += [pl.BlockSpec((None,) + piece.shape[1:], lambda i: (layer, 0, 0, 0)) for piece in weights]
     args = [x, rows, mask, *weights]
     outs = [
         (by_image(IMG_ROWS, D), shape_of((tokens, D), f32)),
@@ -595,26 +603,30 @@
     images = h.shape[0] // IMG_ROWS
     tokens = images * IMG_ROWS
     with_output = flags is not None
-    ins = [by_image(IMG_ROWS, D), by_image(IMG_ROWS, D), whole(8, 6 * D), whole(2, FF, D)]
+    ins = [by_image(IMG_ROWS, D), by_image(IMG_ROWS, D), whole(8, 6 * D), scalar()]
     outs = [
         (by_image(IMG_ROWS, D), shape_of((tokens, D), f32)),
         *[(whole(2, FF // 2, D), shape_of((2, FF // 2, D), bf16))] * 2,
         (whole(8, 6 * D), shape_of((8, 6 * D), f32)),
     ]
-    ins.append(scalar())
-    args = [h, g, rows, weights, at]
+    args = [h, g, rows, at]
+    scratch = [pltpu.VMEM((tokens, width), bf16) for width in (D, D, FF, FF)]
+    if len(weights) > 1:
+        scratch.append(pltpu.VMEM((2, FF, D), bf16))
     if with_output:
         ins.append(by_image(1, 16, IMG_ROWS))
         args.append(flags)
         outs.append((by_image(IMG_ROWS, D), shape_of((tokens, D), bf16)))
         outs.append((by_image(1, 1, D), shape_of((images, 1, D), f32)))
+    ins += [whole(*piece.shape) for piece in weights]
+    args += weights
     return call(
-        lambda *refs: ffn_both_kernel(layer, with_output, pieces, *refs),
+        lambda *refs: ffn_both_kernel(layer, with_output, pieces, len(weights), *refs),
         "ffn_both_out" if with_output else "ffn_both",
         images,
         ins,
         outs,
-        [pltpu.VMEM((tokens, width), bf16) for width in (D, D, FF, FF)],
+        scratch,
     )(*args)
 
 
@@ -672,6 +684,48 @@
     return jnp.sum(lax.all_to_all(parts.astype(bf16), axis, 0, 0).astype(f32), axis=0)
 
 
+def gather_early(own, size):
+    return {1 << bit: swap(own, "tensor", size, 1 << bit) for bit in range(size.bit_length() - 1)}
+
+
+def gather_late(own, early, size):
+    held = {0: own, **early}
+    for s in range(1, size):
+        if s not in held:
+            held[s] = swap(held[s & (s - 1)], "tensor", size, s & -s)
+    return [held[s] for s in range(size)]
+
+
+def joined(own, got, bit, at):
+    mine = (at // bit) % 2 == 1
+    both = jnp.stack([jnp.where(mine, got, own), jnp.where(mine, own, got)], axis=1)
+    return both.reshape((-1,) + own.shape[1:])
+
+
+def join_over(own, bit, at, size):
+    return joined(own, swap(own, "dp", size, bit), bit, at)
+
+
+def part_over(rows, bit, at, low):
+    parts = rows.reshape(2, -1, 2, low, rows.shape[2], D)
+    mine = (at // bit) % 2
+    kept = lax.dynamic_index_in_dim(parts, mine, axis=2, keepdims=False)
+    sent = lax.dynamic_index_in_dim(parts, 1 - mine, axis=2, keepdims=False)
+    shape = (2, -1, rows.shape[2], D)
+    return kept.reshape(shape), sent.astype(bf16).reshape(shape)
+
+
+def add_over(rows, bit, at, size, low):
+    kept, sent = part_over(rows, bit, at, low)
+    return kept + swap(sent, "dp", size, bit).astype(f32)
+
+
+def as_rows(parts, rows):
+    if parts.shape[2] % 16 == 0:
+        return parts
+    return parts.transpose(1, 0, 2, 3).reshape(parts.shape[1], rows, parts.shape[3])
+
+
 def fold_far(near, far, rows, size):
     kept = near.astype(f32) + swap(far, "tensor", size, 1).astype(f32)
     bit = 2
@@ -693,7 +747,7 @@
 def body(n_dp, n_tensor, tokens, cotangent, image_size, vectors, mix_weight, mix_bias, bias_table, out_weight, up_weight, up_bias, down_weight):
     local_images = tokens.shape[0] // IMG_ROWS
     devices = n_dp * n_tensor
-    stages = bits_of("dp", n_dp) + bits_of("tensor", n_tensor)[::-1]
+    stages = bits_of("dp", n_dp) + bits_of("tensor", n_tensor)
     dp_at, tensor_at = lax.axis_index("dp"), lax.axis_index("tensor")
     own = dp_at * n_tensor + tensor_at
     own_size = lax.dynamic_slice_in_dim(image_size, tensor_at * local_images, local_images, 0)
@@ -719,35 +773,37 @@
     dense_own = jnp.stack([up_weight.transpose(0, 2, 1), down_weight], axis=1)
 
     dense_part = to_all(dense_own[0], "dp", n_dp)
-    attn_w0 = [attn_own[0]] + exchange(lambda s: attn_own[0], "tensor", n_tensor)
-    attn_w1 = lax.all_gather(attn_own[1], "tensor", axis=1, tiled=True)
-    dense_w1 = lax.all_gather(dense_own[1], ("tensor", "dp"), axis=1, tiled=True)
+    attn_w = gather_late(attn_own, gather_early(attn_own, n_tensor), n_tensor)
 
     at = tensor_at.reshape(1).astype(jnp.int32)
     masks = [key_masks(own_size, l % 2 == 1) for l in range(LAYERS)]
     flags = inside_rows(own_size)
     rows = part
+    dense_next = dense_own[1][None]
+    next_bits = [1 << bit for bit in range(n_dp.bit_length() - 1)][::-1]
     for count, stage in enumerate(stages):
         rows = rows + swap(rows, *stage)
         if count == 0:
             rows, flags, masks = tied(rows, flags, masks)
+        if 0 < count < len(next_bits):
+            dense_next = join_over(dense_next, next_bits[count - 1], dp_at, n_dp)
+            rows, dense_next = tied(rows, dense_next)
         if count == len(stages) - 2:
-            rows, attn_w0 = tied(rows, attn_w0)
+            rows, attn_w, dense_part = tied(rows, attn_w, dense_part)
     rows = rows.astype(f32)
 
-    rows, dense_part = tied(rows, dense_part)
-    if ub_own % 16:
-        dense_part = dense_part.transpose(1, 0, 2, 3).reshape(2, ff_part, D)
-    dense_w0 = {0: dense_part}
-    for bit in range(n_tensor.bit_length() - 1):
-        dense_w0[1 << bit] = swap(dense_part, "tensor", n_tensor, 1 << bit)
-    h0, *kept0, attn_w0 = attn_forward(0, tokens, rows, masks[0], attn_w0, at)
-    h0, kept0, attn_w0, dense_w0 = tied(h0, kept0, attn_w0, dense_w0)
-    for s in range(1, n_tensor):
-        if s not in dense_w0:
-            dense_w0[s] = swap(dense_w0[s & (s - 1)], "tensor", n_tensor, s & -s)
-    x1, dense_w0 = ffn_forward(0, h0, rows, [dense_w0[s] for s in range(n_tensor)], at)
-    h1, *kept1 = attn_forward(1, x1, rows, masks[1], [attn_w1], at)
+    dense_part = as_rows(dense_part, ff_part)
+    early = gather_early(dense_part, n_tensor)
+    next_got = swap(dense_next, "dp", n_dp, next_bits[-1])
+    h0, *kept0, attn_w0 = attn_forward(0, tokens, rows, masks[0], attn_w, at)
+    h0, kept0, attn_w0, early, next_got = tied(h0, kept0, attn_w0, early, next_got)
+    dense_w0 = gather_late(dense_part, early, n_tensor)
+    x1, dense_w0 = ffn_forward(0, h0, rows, dense_w0, at)
+    dense_next = as_rows(joined(dense_next, next_got, next_bits[-1], dp_at), ff_part)
+    early = gather_early(dense_next, n_tensor)
+    h1, *kept1, attn_w1 = attn_forward(1, x1, rows, masks[1], attn_w, at)
+    h1, kept1, attn_w1, early = tied(h1, kept1, attn_w1, early)
+    dense_w1 = gather_late(dense_next, early, n_tensor)
 
     gh1, near, far, vf1, output, image_mean = ffn_both(1, h1, cotangent, rows, dense_w1, at, n_tensor, flags)
     gh1, near, far = tied(gh1, near, far)
@@ -757,33 +813,42 @@
     g1, *attn_g1, va1 = attn_backward(1, gh1, x1, rows, attn_w1, kept1, at, n_tensor)
     g1, attn_g1, va1, got = tied(g1, attn_g1, va1, got)
     got1 = exchange(lambda s: attn_g1[s], "tensor", n_tensor)
-    blocks1 = (kept + got.astype(f32)).astype(bf16).reshape(2, n_dp, ub_own, D).transpose(1, 0, 2, 3)
-    blocks1 = lax.all_to_all(blocks1, "dp", 0, 0)
-
-    gh0, near, far, vf0 = ffn_both(0, h0, g1, rows, dense_w0, at, n_tensor)
-    gh0, near, far, vf0, got1, blocks1 = tied(gh0, near, far, vf0, got1, blocks1)
+    dp_bits = [1 << bit for bit in range(n_dp.bit_length() - 1)]
+    kept1, sent1 = part_over((kept + got.astype(f32)).reshape(2, n_dp, ub_own, D), dp_bits[-1], dp_at, n_dp // 2)
+    dense_got1 = swap(sent1, "dp", n_dp, dp_bits[-1])
+
+    gh0, near, far, vf0 = ffn_both(0, h0, g1, rows, [dense_w0], at, n_tensor)
+    gh0, near, far, vf0, got1, dense_got1 = tied(gh0, near, far, vf0, got1, dense_got1)
     kept, far = fold_far(near, far, ff_part, n_tensor)
     gh0, far = tied(gh0, far)
     got0 = swap(far, "tensor", n_tensor, n_tensor // 2)
     dmix, *attn_g0, va0 = attn_backward_core(0, gh0, attn_w0, kept0, at, n_tensor)
-    dmix, attn_g0, va0, got0, got1 = tied(dmix, attn_g0, va0, got0, got1)
+    dmix, attn_g0, va0, got0 = tied(dmix, attn_g0, va0, got0)
     got = exchange(lambda s: attn_g0[s], "tensor", n_tensor)
-    blocks0 = (kept + got0.astype(f32)).astype(bf16).reshape(2, n_dp, ub_own, D).transpose(1, 0, 2, 3)
-    blocks0 = lax.all_to_all(blocks0, "dp", 0, 0)
+    kept0 = (kept + got0.astype(f32)).reshape(2, n_dp, ub_own, D)
+    kept0, sent0 = part_over(kept0, dp_bits[-1], dp_at, n_dp // 2)
+    dense_got0 = swap(sent0, "dp", n_dp, dp_bits[-1])
     g0, vn0 = attn_backward_norm(0, gh0, tokens, rows, attn_w0, dmix)
-    g0, vn0, got = tied(g0, vn0, got)
-    dense_sum1 = jnp.sum(blocks1.astype(f32), axis=0)
-    dense_sum0 = jnp.sum(blocks0.astype(f32), axis=0)
+    g0, vn0, got, dense_got0, dense_got1, got1 = tied(g0, vn0, got, dense_got0, dense_got1, got1)
+
+    first, *stages = bits_of("dp", n_dp)
+    stages = bits_of("tensor", n_tensor)[::-1] + stages[::-1]
+    small = vf0 + vf1 + va0 + va1 + vn0
+    small = small + swap(small, *first)
 
     attn_sums = [total(attn_g0[0], got), total(attn_g1[0], got1)]
     matrices = jnp.concatenate(attn_sums).astype(bf16).reshape(n_dp, -1, D)
+    small, matrices = tied(small, matrices)
     sums = sum_parts(matrices, "dp")
-    small = vf0 + vf1 + va0 + va1 + vn0
-    stages = bits_of("tensor", n_tensor)[::-1] + bits_of("dp", n_dp)[::-1]
-    for count, stage in enumerate(stages):
+    for stage in stages:
         small = small + swap(small, *stage)
-        if count == n_tensor.bit_length():
-            small, sums = tied(small, sums)
+    small, sums, kept0, kept1 = tied(small, sums, kept0, kept1)
+    kept0 = kept0 + dense_got0.astype(f32)
+    kept1 = kept1 + dense_got1.astype(f32)
+    for bit in dp_bits[:-1]:
+        kept0 = add_over(kept0, bit, dp_at, n_dp, 1)
+        kept1 = add_over(kept1, bit, dp_at, n_dp, 1)
+    dense_sum0, dense_sum1 = kept0[:, 0], kept1[:, 0]
     attn_all = to_all(sums.astype(bf16), "dp", n_dp).astype(f32).reshape(LAYERS, 4, own_cols, D)
     vectors_grad = lax.dynamic_slice(small, (0, own * vec_own), (LAYERS, vec_own))
     up_bias_grad = lax.dynamic_slice(small, (2, tensor_at * ff_part + dp_at * ub_own), (LAYERS, ub_own))

time: 300 us -> 286 us (0.953)
  between operations: 15.3 us -> 2.06 us
    all_to_all x2 -> x0, starting transfers between devices: 9.78 us -> none  [the longest x1 5.98 us: body(): blocks0 = lax.all_to_all(blocks0, 'dp', 0, 0)]
    ppermute x26 -> x38, starting transfers between devices: 30.7 us -> 38.3 us  [swap(): return lax.ppermute(rows, axis, [(i, i ^ bit) for i in range(size)])]
    ppermute x26 -> x38, waiting for transfers between devices: 49.1 us -> 48.7 us  [swap(): return lax.ppermute(rows, axis, [(i, i ^ bit) for i in range(size)])]
  transfers between devices with their start and end apart: 33 -> 41, of which waited for: 14 -> 16; matrix products, arithmetic and copies ran while one was open for 5% -> 5% of each run, Pallas kernels for 43% -> 45%
where the time goes in v5:
time: 286 us; the launch traced here: 283 us
  Pallas kernels  151 us (53%)
  starting transfers between devices  52.6 us (18%)
  waiting for transfers between devices  48.9 us (17%)
  local copies, waits for them, and re-layouts  14.1 us (5%)
  other arithmetic  14 us (5%)
    ppermute x38, waiting for transfers between devices, swap(): return lax.ppermute(rows, axis, [(i, i ^ bit) for i in range(size)])  48.7 us
    pallas_call x2, Pallas kernels, ffn_both(): call(lambda *refs: ffn_both_kernel(layer, with_output, pieces, len(weight...  44 us
    ppermute x38, starting transfers between devices, swap(): return lax.ppermute(rows, axis, [(i, i ^ bit) for i in range(size)])  38.3 us
    pallas_call x2, Pallas kernels, attn_forward(): call(lambda *refs: attn_fwd_kernel(layer, pieces, *refs), 'attn_fwd', ima...  36.6 us
    pallas_call x1, Pallas kernels, attn_backward(): call(lambda *refs: attn_bwd_kernel(layer, *refs), 'attn_bwd', images, [by...  28.9 us
    pallas_call x1, Pallas kernels, attn_backward_core(): call(lambda *refs: attn_core_kernel(layer, *refs), 'attn_core', images, [...  24.2 us
    all_to_all x2, starting transfers between devices, to_all(): lax.all_to_all(jnp.broadcast_to(rows[None], (size,) + rows.shape), axis,...  10.5 us
    pallas_call x1, Pallas kernels, ffn_forward(): call(lambda *refs: ffn_fwd_kernel(layer, len(weights), *refs), 'ffn_fwd',...  9.31 us
  transfers between devices with their start and end apart: 41, of which 16 were waited for; matrix products, arithmetic and copies ran while one was open for 5% of the time, Pallas kernels for 45%

profile of v5, /device:TPU:0, one launch (start us, length us, event | category | flops | bytes accessed | tf_op | source)
XLA Modules:
  0.0 282.8 jit_solution(3065772538894381425)
XLA Ops:
  2.0 3.0 %collective-permute-start.7 = (bf16[2,4,96,384]{3,2,1,0:T(8,128)(2,1)S(1)}, bf16[2,4,96,384]{3,2,1,0:T(8,128)(2,1)S(1)}, u32[]{:S(2)}, u32[]{:S(2)}) collective-permute-start(bf16[2,4,96,384]{3,2,1,0:T(8,128)(2,1)S(1)} %pad_maximum_fusion.refs_3_), channel_id=1, source_target_pairs={{0,2},{1,3},{2,0},{3,1},{4,6},{5,7},{6,4},{7,5},{8,10},{9,11},{10,... | collective-permute-start | bytes 1769480 | tf_op jit(solution)/shard_map/ppermute | solution.py:652
  5.1 2.7 collective-permute-start.2
  11.2 6.4 %all-to-all-start = ((bf16[8,2,48,384]{3,2,1,0:T(8,128)(2,1)}), bf16[8,2,48,384]{3,2,1,0:T(8,128)(2,1)S(1)}, u32[]{:S(2)}, u32[]{:S(2)}) async-start(bf16[8,2,48,384]{3,2,1,0:T(8,128)(2,1)} %broadcast_in_dim.51), calls=%async_computation | async-start | bytes 1179648 | tf_op jit(solution)/shard_map/all_to_all | solution.py:680
  23.7 4.8 %collective-permute-done.1 = bf16[8,2304]{1,0:T(8,128)(2,1)S(1)} collective-permute-done((bf16[8,2304]{1,0:T(8,128)(2,1)S(1)}, bf16[8,2304]{1,0:T(8,128)(2,1)S(1)}, u32[]{:S(2)}, u32[]{:S(2)}) %collective-permute-start.1) | collective-permute-done | bytes 36896 | tf_op jit(solution)/shard_map/ppermute | solution.py:652
  28.5 2.5 collective-permute-start.4
  36.8 3.8 %collective-permute-done.5 = bf16[8,2304]{1,0:T(8,128)(2,1)S(1)} collective-permute-done((bf16[8,2304]{1,0:T(8,128)(2,1)S(1)}, bf16[8,2304]{1,0:T(8,128)(2,1)S(1)}, u32[]{:S(2)}, u32[]{:S(2)}) %collective-permute-start.5) | collective-permute-done | bytes 36896 | tf_op jit(solution)/shard_map/ppermute | solution.py:652
  42.9 17.8 %attn_fwd.2 = (f32[1568,384]{1,0:T(8,128)}, bf16[2048,384]{1,0:T(8,128)(2,1)}, bf16[2048,1152]{1,0:T(8,128)(2,1)}, bf16[2,8,3,128,512]{4,3,2,1,0:T(8,128)(2,1)},...) custom-call(bf16[1568,384]{1,0:T(8,128)(2,1)} %refs_1_.3, f32[8,2304]{1,0:T(8,128)} %add_convert_fusion.2.refs_1_.refs_2_, ...), custom_call_target="tpu_custom_call" | custom-call | flops 100000000 | bytes 100000 | tf_op jit(solution)/shard_map/attn_fwd/pallas_call | solution.py:505
  64.3 9.3 %ffn_fwd.1 = (f32[1568,384]{1,0:T(8,128)}, bf16[2,1536,384]{2,1,0:T(8,128)(2,1)}) custom-call(f32[1568,384]{1,0:T(8,128)} %get-tuple-element.143.refs_0_, f32[8,2304]{1,0:T(8,128)} %add_convert_fusion.2.refs_1_.refs_2_, bf16[8,2,48,384]{3,2,1,0:T(8,128)(2,1)} %copy-done.6, bf16[8,2,48,384]{3,2,1,0:T(8,128)(2,1)} %copy-done.8, ...), custom_call_target="tpu_custom_call" | custom-call | flops 100000000 | bytes 100000 | tf_op jit(solution)/shard_map/ffn_fwd/pallas_call | solution.py:590
  73.6 18.8 %attn_fwd.3 = (f32[1568,384]{1,0:T(8,128)}, bf16[2048,384]{1,0:T(8,128)(2,1)}, bf16[2048,1152]{1,0:T(8,128)(2,1)}, bf16[2,8,3,128,512]{4,3,2,1,0:T(8,128)(2,1)},...) custom-call(f32[1568,384]{1,0:T(8,128)} %get-tuple-element.146.refs_0_.refs_1_, ...), custom_call_target="tpu_custom_call" | custom-call | flops 100000000 | bytes 100000 | tf_op jit(solution)/shard_map/attn_fwd/pallas_call | solution.py:505
  95.4 23.4 %ffn_both_out.1 = (f32[1568,384]{1,0:T(8,128)}, bf16[2,768,384]{2,1,0:T(8,128)(2,1)}, bf16[2,768,384]{2,1,0:T(8,128)(2,1)}, f32[8,2304]{1,0:T(8,128)}, bf16[1568,384]{1,0:T(8,128)(2,1)}, /*index=5*/f32[2,1,384]{2,1,0:T(1,128)}) custom-call(f32[1568,384]{1,0:T(8,128)} %get-tuple-element.155.refs_0_, bf16[1568,384]{1,0:T(8,128)(2,1)} %refs_1_.2, ...), custom_call_target="tpu_custom_call" | custom-call | flops 100000000 | bytes 100000 | tf_op jit(solution)/shard_map/ffn_both_out/pallas_call | solution.py:623
  119.0 2.9 %collective-permute-done.17 = bf16[2,768,384]{2,1,0:T(8,128)(2,1)S(1)} collective-permute-done((bf16[2,768,384]{2,1,0:T(8,128)(2,1)}, bf16[2,768,384]{2,1,0:T(8,128)(2,1)S(1)}, u32[]{:S(2)}, u32[]{:S(2)}) %collective-permute-start.17) | collective-permute-done | bytes 1179680 | tf_op jit(solution)/shard_map/ppermute | solution.py:652
  124.6 28.9 %attn_bwd.1 = (f32[1568,384]{1,0:T(8,128)}, bf16[4,96,384]{2,1,0:T(8,128)(2,1)}, bf16[4,96,384]{2,1,0:T(8,128)(2,1)}, bf16[4,96,384]{2,1,0:T(8,128)(2,1)}, bf16[...) custom-call(f32[1568,384]{1,0:T(8,128)} %get-tuple-element.167.refs_0_, f32[1568,384]{1,0:T(8,128)} %get-tuple-element.146.refs_0_.refs_1_, ...), custom_call_target="tpu_custom_call" | custom-call | flops 100000000 | bytes 100000 | tf_op jit(solution)/shard_map/attn_bwd/pallas_call | solution.py:530
  160.0 20.6 %ffn_both.1 = (f32[1568,384]{1,0:T(8,128)}, bf16[2,768,384]{2,1,0:T(8,128)(2,1)}, bf16[2,768,384]{2,1,0:T(8,128)(2,1)}, f32[8,2304]{1,0:T(8,128)}) custom-call(f32[1568,384]{1,0:T(8,128)} %get-tuple-element.143.refs_0_, f32[1568,384]{1,0:T(8,128)} %get-tuple-element.180.refs_1_, f32[8,2304]{1,0:T(8,128)} %add_convert_fusion.2.refs_1_.refs_2_, ...), custom_call_target="tpu_custom_call" | custom-call | flops 100000000 | bytes 100000 | tf_op jit(solution)/shard_map/ffn_both/pallas_call | solution.py:623
  186.5 24.2 %attn_core.1 = (bf16[2048,1152]{1,0:T(8,128)(2,1)}, bf16[4,96,384]{2,1,0:T(8,128)(2,1)}, bf16[4,96,384]{2,1,0:T(8,128)(2,1)}, bf16[4,96,384]{2,1,0:T(8,128)(2,1)...) custom-call(f32[1568,384]{1,0:T(8,128)} %get-tuple-element.193.refs_0_, ...), custom_call_target="tpu_custom_call" | custom-call | flops 100000000 | bytes 100000 | tf_op jit(solution)/shard_map/attn_core/pallas_call | solution.py:553
  213.6 8.1 %attn_norm.1 = (f32[1568,384]{1,0:T(8,128)}, f32[8,2304]{1,0:T(8,128)}) custom-call(f32[1568,384]{1,0:T(8,128)} %get-tuple-element.193.refs_0_, bf16[1568,384]{1,0:T(8,128)(2,1)} %refs_1_.3, f32[8,2304]{1,0:T(8,128)} %add_convert_fusion.2.refs_1_.refs_2_, bf16[4,384,384]{2,1,0:T(8,128)(2,1)} %get-tuple-element.194.refs_1_.refs_3_, ...), custom_call_target="tpu_custom_call" | custom-call | flops 100000000 | bytes 100000 | tf_op jit(solution)/shard_map/attn_norm/pallas_call | solution.py:569
  221.7 5.6 %collective-permute-done.28 = bf16[2,4,48,384]{3,2,1,0:T(8,128)(2,1)S(1)} collective-permute-done((bf16[2,4,48,384]{3,2,1,0:T(8,128)(2,1)S(1)}, bf16[2,4,48,384]{3,2,1,0:T(8,128)(2,1)S(1)}, u32[]{:S(2)}, u32[]{:S(2)}) %collective-permute-start.28) | collective-permute-done | bytes 294944 | tf_op jit(solution)/shard_map/ppermute | solution.py:652
  231.5 3.5 %collective-permute-done.29 = f32[8,2304]{1,0:T(8,128)S(1)} collective-permute-done((f32[8,2304]{1,0:T(8,128)S(1)}, f32[8,2304]{1,0:T(8,128)S(1)}, u32[]{:S(2)}, u32[]{:S(2)}) %collective-permute-start.29) | collective-permute-done | bytes 73760 | tf_op jit(solution)/shard_map/ppermute | solution.py:652
  235.1 3.8 %all-to-all-start.1 = ((bf16[8,96,384]{2,1,0:T(8,128)(2,1)}), bf16[8,96,384]{2,1,0:T(8,128)(2,1)S(1)}, u32[]{:S(2)}, u32[]{:S(2)}) async-start(bf16[8,96,384]{2,1,0:T(8,128)(2,1)} %pad_maximum_fusion.2), calls=%async_computation.1 | async-start | bytes 1179648 | tf_op jit(solution)/shard_map/all_to_all | solution.py:684
  241.8 2.8 collective-permute-done.31
  246.7 2.5 collective-permute-done.32
  249.2 2.8 collective-permute-start.33
  252.0 3.4 %collective-permute-done.33 = f32[8,2304]{1,0:T(8,128)S(1)} collective-permute-done((f32[8,2304]{1,0:T(8,128)S(1)}, f32[8,2304]{1,0:T(8,128)S(1)}, u32[]{:S(2)}, u32[]{:S(2)}) %collective-permute-start.33) | collective-permute-done | bytes 73760 | tf_op jit(solution)/shard_map/ppermute | solution.py:652
  261.9 4.1 %all-to-all-start.2 = ((bf16[8,96,384]{2,1,0:T(8,128)(2,1)}), bf16[8,96,384]{2,1,0:T(8,128)(2,1)S(1)}, u32[]{:S(2)}, u32[]{:S(2)}) async-start(bf16[8,96,384]{2,1,0:T(8,128)(2,1)} %broadcast_in_dim.52), calls=%async_computation.2 | async-start | bytes 1179648 | tf_op jit(solution)/shard_map/all_to_all | solution.py:680
  268.9 7.8 %collective-permute-done.35 = bf16[2,1,48,384]{3,2,1,0:T(8,128)(2,1)S(1)} collective-permute-done((bf16[2,1,48,384]{3,2,1,0:T(8,128)(2,1)S(1)}, bf16[2,1,48,384]{3,2,1,0:T(8,128)(2,1)S(1)}, u32[]{:S(2)}, u32[]{:S(2)}) %collective-permute-start.35) | collective-permute-done | bytes 73760 | tf_op jit(solution)/shard_map/ppermute | solution.py:652
  (235 shorter events, 67.1 us)
Async XLA Ops:
  2.0 21.6 %collective-permute-start.7 = (bf16[2,4,96,384]{3,2,1,0:T(8,128)(2,1)S(1)}, bf16[2,4,96,384]{3,2,1,0:T(8,128)(2,1)S(1)}, u32[]{:S(2)}, u32[]{:S(2)}) collective-permute-start(bf16[2,4,96,384]{3,2,1,0:T(8,128)(2,1)S(1)} %pad_maximum_fusion.refs_3_), channel_id=1, source_target_pairs={{0,2},{1,3},{2,0},{3,1},{4,6},{5,7},{6,4},{7,5},{8,10},{9,11},{10,... | collective-permute-start | bytes 1769480 | tf_op jit(solution)/shard_map/ppermute | solution.py:652
  5.0 35.7 %collective-permute-start.6 = (bf16[2,4,96,384]{3,2,1,0:T(8,128)(2,1)S(1)}, bf16[2,4,96,384]{3,2,1,0:T(8,128)(2,1)S(1)}, u32[]{:S(2)}, u32[]{:S(2)}) collective-permute-start(bf16[2,4,96,384]{3,2,1,0:T(8,128)(2,1)S(1)} %pad_maximum_fusion.refs_3_), channel_id=1, source_target_pairs={{0,1},{1,0},{2,3},{3,2},{4,5},{5,4},{6,7},{7,6},{8,9},{9,8},{10,11... | collective-permute-start | bytes 1769480 | tf_op jit(solution)/shard_map/ppermute | solution.py:652
  5.1 18.5 %collective-permute-start.2 = (bf16[1,2,48,384]{3,2,1,0:T(8,128)(2,1)S(1)}, bf16[1,2,48,384]{3,2,1,0:T(8,128)(2,1)S(1)}, u32[]{:S(2)}, u32[]{:S(2)}) collective-permute-start(bf16[1,2,48,384]{3,2,1,0:T(8,128)(2,1)S(1)} %get-tuple-element.272), channel_id=1, source_target_pairs={{0,16},{4,20},{8,24},{12,28},{16,0},{20,4},{24,8},{28,12},{1,17},{... | collective-permute-start | bytes 221192 | tf_op jit(solution)/shard_map/ppermute | solution.py:652
  11.2 29.5 %all-to-all-start = ((bf16[8,2,48,384]{3,2,1,0:T(8,128)(2,1)}), bf16[8,2,48,384]{3,2,1,0:T(8,128)(2,1)S(1)}, u32[]{:S(2)}, u32[]{:S(2)}) async-start(bf16[8,2,48,384]{3,2,1,0:T(8,128)(2,1)} %broadcast_in_dim.51), calls=%async_computation | async-start | bytes 1179648 | tf_op jit(solution)/shard_map/all_to_all | solution.py:680
  23.6 17.1 %collective-permute-start.8 = (bf16[2,4,96,384]{3,2,1,0:T(8,128)(2,1)S(1)}, bf16[2,4,96,384]{3,2,1,0:T(8,128)(2,1)S(1)}, u32[]{:S(2)}, u32[]{:S(2)}) collective-permute-start(bf16[2,4,96,384]{3,2,1,0:T(8,128)(2,1)S(1)} %collective-permute-done.7.refs_5_), channel_id=1, source_target_pairs={{0,1},{1,0},{2,3},{3,2},{4,5},{5,4},{6,7},{7,6},{8,9},{9,8},{10,11... | collective-permute-start | bytes 1769480 | tf_op jit(solution)/shard_map/ppermute | solution.py:652
  40.8 19.9 %collective-permute-start.12 = (bf16[4,2,48,384]{3,2,1,0:T(8,128)(2,1)S(1)}, bf16[4,2,48,384]{3,2,1,0:T(8,128)(2,1)S(1)}, u32[]{:S(2)}, u32[]{:S(2)}) collective-permute-start(bf16[4,2,48,384]{3,2,1,0:T(8,128)(2,1)S(1)} %bitcast.118), channel_id=1, source_target_pairs={{0,4},{4,0},{8,12},{12,8},{16,20},{20,16},{24,28},{28,24},{1,5},{5... | collective-permute-start | bytes 884744 | tf_op jit(solution)/shard_map/ppermute | solution.py:652
  41.7 19.0 %collective-permute-start.10 = (bf16[8,2,48,384]{3,2,1,0:T(8,128)(2,1)S(1)}, bf16[8,2,48,384]{3,2,1,0:T(8,128)(2,1)S(1)}, u32[]{:S(2)}, u32[]{:S(2)}) collective-permute-start(bf16[8,2,48,384]{3,2,1,0:T(8,128)(2,1)S(1)} %all-to-all-done.refs_2_), channel_id=1, source_target_pairs={{0,1},{1,0},{2,3},{3,2},{4,5},{5,4},{6,7},{7,6},{8,9},{9,8},{10,11... | collective-permute-start | bytes 1769480 | tf_op jit(solution)/shard_map/ppermute | solution.py:652
  41.9 18.9 %collective-permute-start.11 = (bf16[8,2,48,384]{3,2,1,0:T(8,128)(2,1)S(1)}, bf16[8,2,48,384]{3,2,1,0:T(8,128)(2,1)S(1)}, u32[]{:S(2)}, u32[]{:S(2)}) collective-permute-start(bf16[8,2,48,384]{3,2,1,0:T(8,128)(2,1)S(1)} %all-to-all-done.refs_2_), channel_id=1, source_target_pairs={{0,2},{1,3},{2,0},{3,1},{4,6},{5,7},{6,4},{7,5},{8,10},{9,11},{10,... | collective-permute-start | bytes 1769480 | tf_op jit(solution)/shard_map/ppermute | solution.py:652
  61.8 30.7 %collective-permute-start.14 = (bf16[8,2,48,384]{3,2,1,0:T(8,128)(2,1)S(1)}, bf16[8,2,48,384]{3,2,1,0:T(8,128)(2,1)S(1)}, u32[]{:S(2)}, u32[]{:S(2)}) collective-permute-start(bf16[8,2,48,384]{3,2,1,0:T(8,128)(2,1)S(1)} %bitcast.110), channel_id=1, source_target_pairs={{0,1},{1,0},{2,3},{3,2},{4,5},{5,4},{6,7},{7,6},{8,9},{9,8},{10,11... | collective-permute-start | bytes 1769480 | tf_op jit(solution)/shard_map/ppermute | solution.py:652
  61.8 30.6 %collective-permute-start.15 = (bf16[8,2,48,384]{3,2,1,0:T(8,128)(2,1)S(1)}, bf16[8,2,48,384]{3,2,1,0:T(8,128)(2,1)S(1)}, u32[]{:S(2)}, u32[]{:S(2)}) collective-permute-start(bf16[8,2,48,384]{3,2,1,0:T(8,128)(2,1)S(1)} %bitcast.111), channel_id=1, source_target_pairs={{0,2},{1,3},{2,0},{3,1},{4,6},{5,7},{6,4},{7,5},{8,10},{9,11},{10,... | collective-permute-start | bytes 1769480 | tf_op jit(solution)/shard_map/ppermute | solution.py:652
  123.5 30.0 %collective-permute-start.18 = (bf16[2,384,384]{2,1,0:T(8,128)(2,1)S(1)}, bf16[2,384,384]{2,1,0:T(8,128)(2,1)S(1)}, u32[]{:S(2)}, u32[]{:S(2)}) collective-permute-start(bf16[2,384,384]{2,1,0:T(8,128)(2,1)S(1)} %slice.137), channel_id=1, source_target_pairs={{0,2},{1,3},{2,0},{3,1},{4,6},{5,7},{6,4},{7,5},{8,10},{9,11},{10,... | collective-permute-start | bytes 1769480 | tf_op jit(solution)/shard_map/ppermute | solution.py:652
  155.7 24.9 %collective-permute-start.22 = (bf16[2,4,48,384]{3,2,1,0:T(8,128)(2,1)S(1)}, bf16[2,4,48,384]{3,2,1,0:T(8,128)(2,1)S(1)}, u32[]{:S(2)}, u32[]{:S(2)}) collective-permute-start(bf16[2,4,48,384]{3,2,1,0:T(8,128)(2,1)S(1)} %fusion), channel_id=1, source_target_pairs={{0,16},{4,20},{8,24},{12,28},{16,0},{20,4},{24,8},{28,12},{1,17},{... | collective-permute-start | bytes 884744 | tf_op jit(solution)/shard_map/ppermute | solution.py:652
  158.1 22.5 %collective-permute-start.19 = (bf16[4,96,384]{2,1,0:T(8,128)(2,1)S(1)}, bf16[4,96,384]{2,1,0:T(8,128)(2,1)S(1)}, u32[]{:S(2)}, u32[]{:S(2)}) collective-permute-start(bf16[4,96,384]{2,1,0:T(8,128)(2,1)S(1)} %copy-done.40), channel_id=1, source_target_pairs={{0,1},{1,0},{2,3},{3,2},{4,5},{5,4},{6,7},{7,6},{8,9},{9,8},{10,11... | collective-permute-start | bytes 884744 | tf_op jit(solution)/shard_map/ppermute | solution.py:652
  158.2 22.5 %collective-permute-start.20 = (bf16[4,96,384]{2,1,0:T(8,128)(2,1)S(1)}, bf16[4,96,384]{2,1,0:T(8,128)(2,1)S(1)}, u32[]{:S(2)}, u32[]{:S(2)}) collective-permute-start(bf16[4,96,384]{2,1,0:T(8,128)(2,1)S(1)} %copy-done.38), channel_id=1, source_target_pairs={{0,2},{1,3},{2,0},{3,1},{4,6},{5,7},{6,4},{7,5},{8,10},{9,11},{10,... | collective-permute-start | bytes 884744 | tf_op jit(solution)/shard_map/ppermute | solution.py:652
  159.2 21.4 %collective-permute-start.21 = (bf16[4,96,384]{2,1,0:T(8,128)(2,1)S(1)}, bf16[4,96,384]{2,1,0:T(8,128)(2,1)S(1)}, u32[]{:S(2)}, u32[]{:S(2)}) collective-permute-start(bf16[4,96,384]{2,1,0:T(8,128)(2,1)S(1)} %copy-done.37), channel_id=1, source_target_pairs={{0,3},{1,2},{2,1},{3,0},{4,7},{5,6},{6,5},{7,4},{8,11},{9,10},{10,... | collective-permute-start | bytes 884744 | tf_op jit(solution)/shard_map/ppermute | solution.py:652
  185.4 25.3 %collective-permute-start.24 = (bf16[2,384,384]{2,1,0:T(8,128)(2,1)S(1)}, bf16[2,384,384]{2,1,0:T(8,128)(2,1)S(1)}, u32[]{:S(2)}, u32[]{:S(2)}) collective-permute-start(bf16[2,384,384]{2,1,0:T(8,128)(2,1)S(1)} %slice.136), channel_id=1, source_target_pairs={{0,2},{1,3},{2,0},{3,1},{4,6},{5,7},{6,4},{7,5},{8,10},{9,11},{10,... | collective-permute-start | bytes 1769480 | tf_op jit(solution)/shard_map/ppermute | solution.py:652
  211.0 16.3 %collective-permute-start.28 = (bf16[2,4,48,384]{3,2,1,0:T(8,128)(2,1)S(1)}, bf16[2,4,48,384]{3,2,1,0:T(8,128)(2,1)S(1)}, u32[]{:S(2)}, u32[]{:S(2)}) collective-permute-start(bf16[2,4,48,384]{3,2,1,0:T(8,128)(2,1)S(1)} %fusion.1), channel_id=1, source_target_pairs={{0,16},{4,20},{8,24},{12,28},{16,0},{20,4},{24,8},{28,12},{1,17},{... | collective-permute-start | bytes 884744 | tf_op jit(solution)/shard_map/ppermute | solution.py:652
  211.7 15.5 %collective-permute-start.25 = (bf16[4,96,384]{2,1,0:T(8,128)(2,1)S(1)}, bf16[4,96,384]{2,1,0:T(8,128)(2,1)S(1)}, u32[]{:S(2)}, u32[]{:S(2)}) collective-permute-start(bf16[4,96,384]{2,1,0:T(8,128)(2,1)S(1)} %copy-done.42), channel_id=1, source_target_pairs={{0,1},{1,0},{2,3},{3,2},{4,5},{5,4},{6,7},{7,6},{8,9},{9,8},{10,11... | collective-permute-start | bytes 884744 | tf_op jit(solution)/shard_map/ppermute | solution.py:652
  211.8 15.5 %collective-permute-start.26 = (bf16[4,96,384]{2,1,0:T(8,128)(2,1)S(1)}, bf16[4,96,384]{2,1,0:T(8,128)(2,1)S(1)}, u32[]{:S(2)}, u32[]{:S(2)}) collective-permute-start(bf16[4,96,384]{2,1,0:T(8,128)(2,1)S(1)} %copy-done.41), channel_id=1, source_target_pairs={{0,2},{1,3},{2,0},{3,1},{4,6},{5,7},{6,4},{7,5},{8,10},{9,11},{10,... | collective-permute-start | bytes 884744 | tf_op jit(solution)/shard_map/ppermute | solution.py:652
  212.8 14.5 %collective-permute-start.27 = (bf16[4,96,384]{2,1,0:T(8,128)(2,1)S(1)}, bf16[4,96,384]{2,1,0:T(8,128)(2,1)S(1)}, u32[]{:S(2)}, u32[]{:S(2)}) collective-permute-start(bf16[4,96,384]{2,1,0:T(8,128)(2,1)S(1)} %copy-done.39), channel_id=1, source_target_pairs={{0,3},{1,2},{2,1},{3,0},{4,7},{5,6},{6,5},{7,4},{8,11},{9,10},{10,... | collective-permute-start | bytes 884744 | tf_op jit(solution)/shard_map/ppermute | solution.py:652
  235.1 20.4 %all-to-all-start.1 = ((bf16[8,96,384]{2,1,0:T(8,128)(2,1)}), bf16[8,96,384]{2,1,0:T(8,128)(2,1)S(1)}, u32[]{:S(2)}, u32[]{:S(2)}) async-start(bf16[8,96,384]{2,1,0:T(8,128)(2,1)} %pad_maximum_fusion.2), calls=%async_computation.1 | async-start | bytes 1179648 | tf_op jit(solution)/shard_map/all_to_all | solution.py:684
  261.9 18.6 %all-to-all-start.2 = ((bf16[8,96,384]{2,1,0:T(8,128)(2,1)}), bf16[8,96,384]{2,1,0:T(8,128)(2,1)S(1)}, u32[]{:S(2)}, u32[]{:S(2)}) async-start(bf16[8,96,384]{2,1,0:T(8,128)(2,1)} %broadcast_in_dim.52), calls=%async_computation.2 | async-start | bytes 1179648 | tf_op jit(solution)/shard_map/all_to_all | solution.py:680
  266.6 10.0 %collective-permute-start.35 = (bf16[2,1,48,384]{3,2,1,0:T(8,128)(2,1)S(1)}, bf16[2,1,48,384]{3,2,1,0:T(8,128)(2,1)S(1)}, u32[]{:S(2)}, u32[]{:S(2)}) collective-permute-start(bf16[2,1,48,384]{3,2,1,0:T(8,128)(2,1)S(1)} %dynamic-slice_convert_fusion.2), channel_id=1, source_target_pairs={{0,8},{4,12},{8,0},{12,4},{16,24},{20,28},{24,16},{28,20},{1,9},{5... | collective-permute-start | bytes 221192 | tf_op jit(solution)/shard_map/ppermute | solution.py:652
  268.8 10.2 %collective-permute-start.37 = (bf16[2,1,48,384]{3,2,1,0:T(8,128)(2,1)S(1)}, bf16[2,1,48,384]{3,2,1,0:T(8,128)(2,1)S(1)}, u32[]{:S(2)}, u32[]{:S(2)}) collective-permute-start(bf16[2,1,48,384]{3,2,1,0:T(8,128)(2,1)S(1)} %dynamic-slice_convert_fusion.1), channel_id=1, source_target_pairs={{0,8},{4,12},{8,0},{12,4},{16,24},{20,28},{24,16},{28,20},{1,9},{5... | collective-permute-start | bytes 221192 | tf_op jit(solution)/shard_map/ppermute | solution.py:652
  (60 other events, 422.1 us)

commit v6 on v5

--- a/solution.py
+++ b/solution.py
@@ -30,7 +30,7 @@
 never = -1e30
 bf16 = jnp.bfloat16
 f32 = jnp.float32
-VMEM_LIMIT = 56 * 1024 * 1024
+VMEM_MIB = {"attn_fwd": 56, "ffn_fwd": 32, "ffn_both_out": 56, "ffn_both": 42, "attn_bwd": 56, "attn_core": 38, "attn_norm": 28}
 
 
 def nn(a, b):
@@ -231,7 +231,7 @@
 
     def one_pair(pair, carry):
         rows = pl.ds(pl.multiple_of(pair * 128, 128), 128)
-        mask = mask_ref[0, pair]
+        mask = mask_ref[0, pair].astype(f32) * neg_fill
         for g in range(TILES):
             q = qkv_ref[rows, 128 * g : 128 * (g + 1)]
             k = qkv_ref[rows, D + 128 * g : D + 128 * (g + 1)]
@@ -480,7 +480,7 @@
         out_specs=[spec for spec, _ in outs],
         out_shape=[shape for _, shape in outs],
         scratch_shapes=scratch,
-        compiler_params=pltpu.CompilerParams(vmem_limit_bytes=VMEM_LIMIT, dimension_semantics=("arbitrary",)),
+        compiler_params=pltpu.CompilerParams(vmem_limit_bytes=VMEM_MIB[name] * 1024 * 1024, dimension_semantics=("arbitrary",)),
         cost_estimate=pl.CostEstimate(flops=10**8, bytes_accessed=10**5, transcendentals=0),
     )
 
@@ -639,7 +639,7 @@
     inside = inside.reshape(-1, PAIRS, 128, 1)
     labels = jnp.asarray(padded_labels(shifted).reshape(PAIRS, 128))
     same = labels[None, :, :, None] == labels[None, :, None, :]
-    return jnp.where(inside & same, 0.0, neg_fill).astype(f32)
+    return jnp.where(inside & same, 0.0, 1.0).astype(bf16)
 
 
 def inside_rows(own_size):

time: 286 us -> 276 us (0.965)
  Pallas kernels: 151 us -> 137 us
  waiting for transfers between devices: 48.9 us -> 52.7 us
    pallas_call x2, Pallas kernels: 44 us -> 39.8 us  [ffn_both(): call(lambda *refs: ffn_both_kernel(layer, with_output, pieces, len(weight...]
    pallas_call x1, Pallas kernels: 24.2 us -> 20.3 us  [attn_backward_core(): call(lambda *refs: attn_core_kernel(layer, *refs), 'attn_core', images, [...]
    ppermute x38, waiting for transfers between devices: 48.7 us -> 52.4 us  [swap(): return lax.ppermute(rows, axis, [(i, i ^ bit) for i in range(size)])]
    pallas_call x1, Pallas kernels: 9.31 us -> 6.33 us  [ffn_forward(): call(lambda *refs: ffn_fwd_kernel(layer, len(weights), *refs), 'ffn_fwd',...]
    unnamed x88 -> x94, local copies, waits for them, and re-layouts: 4.84 us -> 7.43 us
  transfers between devices with their start and end apart: 41 -> 41, of which waited for: 16 -> 16; matrix products, arithmetic and copies ran while one was open for 5% -> 5% of each run, Pallas kernels for 45% -> 42%
where the time goes in v6:
time: 276 us; the launch traced here: 272 us
  Pallas kernels  137 us (50%)
  waiting for transfers between devices  52.7 us (19%)
  starting transfers between devices  52.6 us (19%)
  local copies, waits for them, and re-layouts  16.5 us (6%)
  other arithmetic  11.7 us (4%)
    ppermute x38, waiting for transfers between devices, swap(): return lax.ppermute(rows, axis, [(i, i ^ bit) for i in range(size)])  52.4 us
    pallas_call x2, Pallas kernels, ffn_both(): call(lambda *refs: ffn_both_kernel(layer, with_output, pieces, len(weight...  39.8 us
    ppermute x38, starting transfers between devices, swap(): return lax.ppermute(rows, axis, [(i, i ^ bit) for i in range(size)])  38.4 us
    pallas_call x2, Pallas kernels, attn_forward(): call(lambda *refs: attn_fwd_kernel(layer, pieces, *refs), 'attn_fwd', ima...  36.3 us
    pallas_call x1, Pallas kernels, attn_backward(): call(lambda *refs: attn_bwd_kernel(layer, *refs), 'attn_bwd', images, [by...  28.7 us
    pallas_call x1, Pallas kernels, attn_backward_core(): call(lambda *refs: attn_core_kernel(layer, *refs), 'attn_core', images, [...  20.3 us
    all_to_all x2, starting transfers between devices, to_all(): lax.all_to_all(jnp.broadcast_to(rows[None], (size,) + rows.shape), axis,...  10.3 us
    unnamed x94, local copies, waits for them, and re-layouts  7.43 us
  transfers between devices with their start and end apart: 41, of which 16 were waited for; matrix products, arithmetic and copies ran while one was open for 5% of the time, Pallas kernels for 42%

profile of v6, /device:TPU:0, one launch (start us, length us, event | category | flops | bytes accessed | tf_op | source)
XLA Modules:
  0.0 272.5 jit_solution(7089797604990177871)
XLA Ops:
  2.0 3.0 %collective-permute-start.7 = (bf16[2,4,96,384]{3,2,1,0:T(8,128)(2,1)S(1)}, bf16[2,4,96,384]{3,2,1,0:T(8,128)(2,1)S(1)}, u32[]{:S(2)}, u32[]{:S(2)}) collective-permute-start(bf16[2,4,96,384]{3,2,1,0:T(8,128)(2,1)S(1)} %pad_maximum_fusion.refs_3_), channel_id=1, source_target_pairs={{0,2},{1,3},{2,0},{3,1},{4,6},{5,7},{6,4},{7,5},{8,10},{9,11},{10,... | collective-permute-start | bytes 1769480 | tf_op jit(solution)/shard_map/ppermute | solution.py:652
  5.1 2.7 collective-permute-start.2
  11.2 6.3 %all-to-all-start = ((bf16[8,2,48,384]{3,2,1,0:T(8,128)(2,1)}), bf16[8,2,48,384]{3,2,1,0:T(8,128)(2,1)S(1)}, u32[]{:S(2)}, u32[]{:S(2)}) async-start(bf16[8,2,48,384]{3,2,1,0:T(8,128)(2,1)} %broadcast_in_dim.51), calls=%async_computation | async-start | bytes 1179648 | tf_op jit(solution)/shard_map/all_to_all | solution.py:680
  23.2 5.1 %collective-permute-done.1 = bf16[8,2304]{1,0:T(8,128)(2,1)S(1)} collective-permute-done((bf16[8,2304]{1,0:T(8,128)(2,1)S(1)}, bf16[8,2304]{1,0:T(8,128)(2,1)S(1)}, u32[]{:S(2)}, u32[]{:S(2)}) %collective-permute-start.1) | collective-permute-done | bytes 36896 | tf_op jit(solution)/shard_map/ppermute | solution.py:652
  28.4 2.5 collective-permute-start.4
  36.7 3.8 %collective-permute-done.5 = bf16[8,2304]{1,0:T(8,128)(2,1)S(1)} collective-permute-done((bf16[8,2304]{1,0:T(8,128)(2,1)S(1)}, bf16[8,2304]{1,0:T(8,128)(2,1)S(1)}, u32[]{:S(2)}, u32[]{:S(2)}) %collective-permute-start.5) | collective-permute-done | bytes 36896 | tf_op jit(solution)/shard_map/ppermute | solution.py:652
  42.7 17.7 %attn_fwd.2 = (f32[1568,384]{1,0:T(8,128)}, bf16[2048,384]{1,0:T(8,128)(2,1)}, bf16[2048,1152]{1,0:T(8,128)(2,1)}, bf16[2,8,3,128,512]{4,3,2,1,0:T(8,128)(2,1)},...) custom-call(bf16[1568,384]{1,0:T(8,128)(2,1)} %refs_1_.3, f32[8,2304]{1,0:T(8,128)} %add_convert_fusion.2.refs_1_.refs_2_, ...), custom_call_target="tpu_custom_call" | custom-call | flops 100000000 | bytes 100000 | tf_op jit(solution)/shard_map/attn_fwd/pallas_call | solution.py:505
  63.0 6.3 %ffn_fwd.1 = (f32[1568,384]{1,0:T(8,128)S(1)}, bf16[2,1536,384]{2,1,0:T(8,128)(2,1)S(1)}) custom-call(f32[1568,384]{1,0:T(8,128)S(1)} %copy-done.2, f32[8,2304]{1,0:T(8,128)S(1)} %copy-done.6, bf16[8,2,48,384]{3,2,1,0:T(8,128)(2,1)S(1)} %all-to-all-done.refs_2_, bf16[8,2,48,384]{3,2,1,0:T(8,128)(2,1)S(1)} %collective-permute-done.10.refs_3_, ...), custom_call_target="tpu_custom_call" | custom-call | flops 100000000 | bytes 100000 | tf_op jit(solution)/shard_map/ffn_fwd/pallas_call | solution.py:590
  72.3 18.6 %attn_fwd.3 = (f32[1568,384]{1,0:T(8,128)}, bf16[2048,384]{1,0:T(8,128)(2,1)}, bf16[2048,1152]{1,0:T(8,128)(2,1)}, bf16[2,8,3,128,512]{4,3,2,1,0:T(8,128)(2,1)},...) custom-call(f32[1568,384]{1,0:T(8,128)} %copy-done.3, f32[8,2304]{1,0:T(8,128)} %add_convert_fusion.2.refs_1_.refs_2_, ...), custom_call_target="tpu_custom_call" | custom-call | flops 100000000 | bytes 100000 | tf_op jit(solution)/shard_map/attn_fwd/pallas_call | solution.py:505
  93.9 23.3 %ffn_both_out.1 = (f32[1568,384]{1,0:T(8,128)}, bf16[2,768,384]{2,1,0:T(8,128)(2,1)}, bf16[2,768,384]{2,1,0:T(8,128)(2,1)}, f32[8,2304]{1,0:T(8,128)}, bf16[1568,384]{1,0:T(8,128)(2,1)}, /*index=5*/f32[2,1,384]{2,1,0:T(1,128)}) custom-call(f32[1568,384]{1,0:T(8,128)} %get-tuple-element.155.refs_0_, bf16[1568,384]{1,0:T(8,128)(2,1)} %refs_1_.2, ...), custom_call_target="tpu_custom_call" | custom-call | flops 100000000 | bytes 100000 | tf_op jit(solution)/shard_map/ffn_both_out/pallas_call | solution.py:623
  117.5 2.9 %collective-permute-done.17 = bf16[2,768,384]{2,1,0:T(8,128)(2,1)S(1)} collective-permute-done((bf16[2,768,384]{2,1,0:T(8,128)(2,1)}, bf16[2,768,384]{2,1,0:T(8,128)(2,1)S(1)}, u32[]{:S(2)}, u32[]{:S(2)}) %collective-permute-start.17) | collective-permute-done | bytes 1179680 | tf_op jit(solution)/shard_map/ppermute | solution.py:652
  124.7 28.7 %attn_bwd.1 = (f32[1568,384]{1,0:T(8,128)}, bf16[4,96,384]{2,1,0:T(8,128)(2,1)}, bf16[4,96,384]{2,1,0:T(8,128)(2,1)}, bf16[4,96,384]{2,1,0:T(8,128)(2,1)}, bf16[...) custom-call(f32[1568,384]{1,0:T(8,128)} %get-tuple-element.167.refs_0_, f32[1568,384]{1,0:T(8,128)} %copy-done.3, ...), custom_call_target="tpu_custom_call" | custom-call | flops 100000000 | bytes 100000 | tf_op jit(solution)/shard_map/attn_bwd/pallas_call | solution.py:530
  159.2 16.4 %ffn_both.1 = (f32[1568,384]{1,0:T(8,128)S(1)}, bf16[2,768,384]{2,1,0:T(8,128)(2,1)S(1)}, bf16[2,768,384]{2,1,0:T(8,128)(2,1)S(1)}, f32[8,2304]{1,0:T(8,128)S(1)}) custom-call(f32[1568,384]{1,0:T(8,128)S(1)} %copy-done.2, f32[1568,384]{1,0:T(8,128)S(1)} %copy-done.8, f32[8,2304]{1,0:T(8,128)S(1)} %copy-done.7, s32[1]{0:T(128)} %bitcast.20.refs_7_.refs_6_.refs_3_.refs_8_, ...), custom_call_target="tpu_custom_call" | custom-call | flops 100000000 | bytes 100000 | tf_op jit(solution)/shard_map/ffn_both/pallas_call | solution.py:623
  176.1 2.5 collective-permute-done.23
  180.8 20.3 %attn_core.1 = (bf16[2048,1152]{1,0:T(8,128)(2,1)S(1)}, bf16[4,96,384]{2,1,0:T(8,128)(2,1)S(1)}, bf16[4,96,384]{2,1,0:T(8,128)(2,1)S(1)}, bf16[4,96,384]{2,1,0:T...) custom-call(f32[1568,384]{1,0:T(8,128)S(1)} %get-tuple-element.193.refs_0_, ...), custom_call_target="tpu_custom_call" | custom-call | flops 100000000 | bytes 100000 | tf_op jit(solution)/shard_map/attn_core/pallas_call | solution.py:553
  203.8 5.5 %attn_norm.1 = (f32[1568,384]{1,0:T(8,128)}, f32[8,2304]{1,0:T(8,128)S(1)}) custom-call(f32[1568,384]{1,0:T(8,128)S(1)} %get-tuple-element.193.refs_0_, bf16[1568,384]{1,0:T(8,128)(2,1)S(1)} %copy-done.4, f32[8,2304]{1,0:T(8,128)S(1)} %copy-done.7, bf16[4,384,384]{2,1,0:T(8,128)(2,1)S(1)} %copy-done.5, bf16[2048,1152]{1,0:T(8,128)(2,1)S(1)} %get-tuple-element.206.refs_4_), custom_call_target="tpu_custom_call" | custom-call | flops 100000000 | bytes 100000 | tf_op jit(solution)/shard_map/attn_norm/pallas_call | solution.py:569
  209.2 8.6 %collective-permute-done.28 = bf16[2,4,48,384]{3,2,1,0:T(8,128)(2,1)S(1)} collective-permute-done((bf16[2,4,48,384]{3,2,1,0:T(8,128)(2,1)S(1)}, bf16[2,4,48,384]{3,2,1,0:T(8,128)(2,1)S(1)}, u32[]{:S(2)}, u32[]{:S(2)}) %collective-permute-start.28) | collective-permute-done | bytes 294944 | tf_op jit(solution)/shard_map/ppermute | solution.py:652
  220.9 3.4 %collective-permute-done.29 = f32[8,2304]{1,0:T(8,128)S(1)} collective-permute-done((f32[8,2304]{1,0:T(8,128)S(1)}, f32[8,2304]{1,0:T(8,128)S(1)}, u32[]{:S(2)}, u32[]{:S(2)}) %collective-permute-start.29) | collective-permute-done | bytes 73760 | tf_op jit(solution)/shard_map/ppermute | solution.py:652
  224.3 3.9 %all-to-all-start.1 = ((bf16[8,96,384]{2,1,0:T(8,128)(2,1)}), bf16[8,96,384]{2,1,0:T(8,128)(2,1)S(1)}, u32[]{:S(2)}, u32[]{:S(2)}) async-start(bf16[8,96,384]{2,1,0:T(8,128)(2,1)} %pad_maximum_fusion.2), calls=%async_computation.1 | async-start | bytes 1179648 | tf_op jit(solution)/shard_map/all_to_all | solution.py:684
  231.0 2.9 %collective-permute-done.31 = f32[8,2304]{1,0:T(8,128)S(1)} collective-permute-done((f32[8,2304]{1,0:T(8,128)S(1)}, f32[8,2304]{1,0:T(8,128)S(1)}, u32[]{:S(2)}, u32[]{:S(2)}) %collective-permute-start.31) | collective-permute-done | bytes 73760 | tf_op jit(solution)/shard_map/ppermute | solution.py:652
  238.4 3.0 %collective-permute-start.33 = (f32[8,2304]{1,0:T(8,128)S(1)}, f32[8,2304]{1,0:T(8,128)S(1)}, u32[]{:S(2)}, u32[]{:S(2)}) collective-permute-start(f32[8,2304]{1,0:T(8,128)S(1)} %add.261), channel_id=1, source_target_pairs={{0,8},{4,12},{8,0},{12,4},{16,24},{20,28},{24,16},{28,20},{1,9},{5... | collective-permute-start | bytes 221192 | tf_op jit(solution)/shard_map/ppermute | solution.py:652
  241.4 3.5 %collective-permute-done.33 = f32[8,2304]{1,0:T(8,128)S(1)} collective-permute-done((f32[8,2304]{1,0:T(8,128)S(1)}, f32[8,2304]{1,0:T(8,128)S(1)}, u32[]{:S(2)}, u32[]{:S(2)}) %collective-permute-start.33) | collective-permute-done | bytes 73760 | tf_op jit(solution)/shard_map/ppermute | solution.py:652
  251.3 4.0 %all-to-all-start.2 = ((bf16[8,96,384]{2,1,0:T(8,128)(2,1)}), bf16[8,96,384]{2,1,0:T(8,128)(2,1)S(1)}, u32[]{:S(2)}, u32[]{:S(2)}) async-start(bf16[8,96,384]{2,1,0:T(8,128)(2,1)} %broadcast_in_dim.52), calls=%async_computation.2 | async-start | bytes 1179648 | tf_op jit(solution)/shard_map/all_to_all | solution.py:680
  258.2 8.4 %collective-permute-done.35 = bf16[2,1,48,384]{3,2,1,0:T(8,128)(2,1)S(1)} collective-permute-done((bf16[2,1,48,384]{3,2,1,0:T(8,128)(2,1)S(1)}, bf16[2,1,48,384]{3,2,1,0:T(8,128)(2,1)S(1)}, u32[]{:S(2)}, u32[]{:S(2)}) %collective-permute-start.35) | collective-permute-done | bytes 73760 | tf_op jit(solution)/shard_map/ppermute | solution.py:652
  (241 shorter events, 66.9 us)
Async XLA Ops:
  2.0 21.1 %collective-permute-start.7 = (bf16[2,4,96,384]{3,2,1,0:T(8,128)(2,1)S(1)}, bf16[2,4,96,384]{3,2,1,0:T(8,128)(2,1)S(1)}, u32[]{:S(2)}, u32[]{:S(2)}) collective-permute-start(bf16[2,4,96,384]{3,2,1,0:T(8,128)(2,1)S(1)} %pad_maximum_fusion.refs_3_), channel_id=1, source_target_pairs={{0,2},{1,3},{2,0},{3,1},{4,6},{5,7},{6,4},{7,5},{8,10},{9,11},{10,... | collective-permute-start | bytes 1769480 | tf_op jit(solution)/shard_map/ppermute | solution.py:652
  5.0 35.5 %collective-permute-start.6 = (bf16[2,4,96,384]{3,2,1,0:T(8,128)(2,1)S(1)}, bf16[2,4,96,384]{3,2,1,0:T(8,128)(2,1)S(1)}, u32[]{:S(2)}, u32[]{:S(2)}) collective-permute-start(bf16[2,4,96,384]{3,2,1,0:T(8,128)(2,1)S(1)} %pad_maximum_fusion.refs_3_), channel_id=1, source_target_pairs={{0,1},{1,0},{2,3},{3,2},{4,5},{5,4},{6,7},{7,6},{8,9},{9,8},{10,11... | collective-permute-start | bytes 1769480 | tf_op jit(solution)/shard_map/ppermute | solution.py:652
  5.1 18.0 %collective-permute-start.2 = (bf16[1,2,48,384]{3,2,1,0:T(8,128)(2,1)S(1)}, bf16[1,2,48,384]{3,2,1,0:T(8,128)(2,1)S(1)}, u32[]{:S(2)}, u32[]{:S(2)}) collective-permute-start(bf16[1,2,48,384]{3,2,1,0:T(8,128)(2,1)S(1)} %get-tuple-element.272), channel_id=1, source_target_pairs={{0,16},{4,20},{8,24},{12,28},{16,0},{20,4},{24,8},{28,12},{1,17},{... | collective-permute-start | bytes 221192 | tf_op jit(solution)/shard_map/ppermute | solution.py:652
  11.2 29.3 %all-to-all-start = ((bf16[8,2,48,384]{3,2,1,0:T(8,128)(2,1)}), bf16[8,2,48,384]{3,2,1,0:T(8,128)(2,1)S(1)}, u32[]{:S(2)}, u32[]{:S(2)}) async-start(bf16[8,2,48,384]{3,2,1,0:T(8,128)(2,1)} %broadcast_in_dim.51), calls=%async_computation | async-start | bytes 1179648 | tf_op jit(solution)/shard_map/all_to_all | solution.py:680
  23.1 17.4 %collective-permute-start.8 = (bf16[2,4,96,384]{3,2,1,0:T(8,128)(2,1)S(1)}, bf16[2,4,96,384]{3,2,1,0:T(8,128)(2,1)S(1)}, u32[]{:S(2)}, u32[]{:S(2)}) collective-permute-start(bf16[2,4,96,384]{3,2,1,0:T(8,128)(2,1)S(1)} %collective-permute-done.7.refs_5_), channel_id=1, source_target_pairs={{0,1},{1,0},{2,3},{3,2},{4,5},{5,4},{6,7},{7,6},{8,9},{9,8},{10,11... | collective-permute-start | bytes 1769480 | tf_op jit(solution)/shard_map/ppermute | solution.py:652
  40.6 19.8 %collective-permute-start.12 = (bf16[4,2,48,384]{3,2,1,0:T(8,128)(2,1)S(1)}, bf16[4,2,48,384]{3,2,1,0:T(8,128)(2,1)S(1)}, u32[]{:S(2)}, u32[]{:S(2)}) collective-permute-start(bf16[4,2,48,384]{3,2,1,0:T(8,128)(2,1)S(1)} %bitcast.118), channel_id=1, source_target_pairs={{0,4},{4,0},{8,12},{12,8},{16,20},{20,16},{24,28},{28,24},{1,5},{5... | collective-permute-start | bytes 884744 | tf_op jit(solution)/shard_map/ppermute | solution.py:652
  41.6 18.9 %collective-permute-start.10 = (bf16[8,2,48,384]{3,2,1,0:T(8,128)(2,1)S(1)}, bf16[8,2,48,384]{3,2,1,0:T(8,128)(2,1)S(1)}, u32[]{:S(2)}, u32[]{:S(2)}) collective-permute-start(bf16[8,2,48,384]{3,2,1,0:T(8,128)(2,1)S(1)} %all-to-all-done.refs_2_), channel_id=1, source_target_pairs={{0,1},{1,0},{2,3},{3,2},{4,5},{5,4},{6,7},{7,6},{8,9},{9,8},{10,11... | collective-permute-start | bytes 1769480 | tf_op jit(solution)/shard_map/ppermute | solution.py:652
  41.7 18.7 %collective-permute-start.11 = (bf16[8,2,48,384]{3,2,1,0:T(8,128)(2,1)S(1)}, bf16[8,2,48,384]{3,2,1,0:T(8,128)(2,1)S(1)}, u32[]{:S(2)}, u32[]{:S(2)}) collective-permute-start(bf16[8,2,48,384]{3,2,1,0:T(8,128)(2,1)S(1)} %all-to-all-done.refs_2_), channel_id=1, source_target_pairs={{0,2},{1,3},{2,0},{3,1},{4,6},{5,7},{6,4},{7,5},{8,10},{9,11},{10,... | collective-permute-start | bytes 1769480 | tf_op jit(solution)/shard_map/ppermute | solution.py:652
  60.8 30.1 %collective-permute-start.14 = (bf16[8,2,48,384]{3,2,1,0:T(8,128)(2,1)S(1)}, bf16[8,2,48,384]{3,2,1,0:T(8,128)(2,1)S(1)}, u32[]{:S(2)}, u32[]{:S(2)}) collective-permute-start(bf16[8,2,48,384]{3,2,1,0:T(8,128)(2,1)S(1)} %bitcast.110), channel_id=1, source_target_pairs={{0,1},{1,0},{2,3},{3,2},{4,5},{5,4},{6,7},{7,6},{8,9},{9,8},{10,11... | collective-permute-start | bytes 1769480 | tf_op jit(solution)/shard_map/ppermute | solution.py:652
  61.3 29.7 %collective-permute-start.15 = (bf16[8,2,48,384]{3,2,1,0:T(8,128)(2,1)S(1)}, bf16[8,2,48,384]{3,2,1,0:T(8,128)(2,1)S(1)}, u32[]{:S(2)}, u32[]{:S(2)}) collective-permute-start(bf16[8,2,48,384]{3,2,1,0:T(8,128)(2,1)S(1)} %bitcast.111), channel_id=1, source_target_pairs={{0,2},{1,3},{2,0},{3,1},{4,6},{5,7},{6,4},{7,5},{8,10},{9,11},{10,... | collective-permute-start | bytes 1769480 | tf_op jit(solution)/shard_map/ppermute | solution.py:652
  123.4 30.0 %collective-permute-start.18 = (bf16[2,384,384]{2,1,0:T(8,128)(2,1)S(1)}, bf16[2,384,384]{2,1,0:T(8,128)(2,1)}, u32[]{:S(2)}, u32[]{:S(2)}) collective-permute-start(bf16[2,384,384]{2,1,0:T(8,128)(2,1)S(1)} %slice.137), channel_id=1, source_target_pairs={{0,2},{1,3},{2,0},{3,1},{4,6},{5,7},{6,4},{7,5},{8,10},{9,11},{10,... | collective-permute-start | bytes 1769480 | tf_op jit(solution)/shard_map/ppermute | solution.py:652
  154.9 20.8 %collective-permute-start.22 = (bf16[2,4,48,384]{3,2,1,0:T(8,128)(2,1)S(1)}, bf16[2,4,48,384]{3,2,1,0:T(8,128)(2,1)}, u32[]{:S(2)}, u32[]{:S(2)}) collective-permute-start(bf16[2,4,48,384]{3,2,1,0:T(8,128)(2,1)S(1)} %fusion), channel_id=1, source_target_pairs={{0,16},{4,20},{8,24},{12,28},{16,0},{20,4},{24,8},{28,12},{1,17},{... | collective-permute-start | bytes 884744 | tf_op jit(solution)/shard_map/ppermute | solution.py:652
  157.3 18.3 %collective-permute-start.19 = (bf16[4,96,384]{2,1,0:T(8,128)(2,1)S(1)}, bf16[4,96,384]{2,1,0:T(8,128)(2,1)S(1)}, u32[]{:S(2)}, u32[]{:S(2)}) collective-permute-start(bf16[4,96,384]{2,1,0:T(8,128)(2,1)S(1)} %copy-done.45), channel_id=1, source_target_pairs={{0,1},{1,0},{2,3},{3,2},{4,5},{5,4},{6,7},{7,6},{8,9},{9,8},{10,11... | collective-permute-start | bytes 884744 | tf_op jit(solution)/shard_map/ppermute | solution.py:652
  157.3 18.3 %collective-permute-start.20 = (bf16[4,96,384]{2,1,0:T(8,128)(2,1)S(1)}, bf16[4,96,384]{2,1,0:T(8,128)(2,1)S(1)}, u32[]{:S(2)}, u32[]{:S(2)}) collective-permute-start(bf16[4,96,384]{2,1,0:T(8,128)(2,1)S(1)} %copy-done.44), channel_id=1, source_target_pairs={{0,2},{1,3},{2,0},{3,1},{4,6},{5,7},{6,4},{7,5},{8,10},{9,11},{10,... | collective-permute-start | bytes 884744 | tf_op jit(solution)/shard_map/ppermute | solution.py:652
  158.2 17.4 %collective-permute-start.21 = (bf16[4,96,384]{2,1,0:T(8,128)(2,1)S(1)}, bf16[4,96,384]{2,1,0:T(8,128)(2,1)S(1)}, u32[]{:S(2)}, u32[]{:S(2)}) collective-permute-start(bf16[4,96,384]{2,1,0:T(8,128)(2,1)S(1)} %copy-done.43), channel_id=1, source_target_pairs={{0,3},{1,2},{2,1},{3,0},{4,7},{5,6},{6,5},{7,4},{8,11},{9,10},{10,... | collective-permute-start | bytes 884744 | tf_op jit(solution)/shard_map/ppermute | solution.py:652
  179.0 22.1 %collective-permute-start.24 = (bf16[2,384,384]{2,1,0:T(8,128)(2,1)S(1)}, bf16[2,384,384]{2,1,0:T(8,128)(2,1)S(1)}, u32[]{:S(2)}, u32[]{:S(2)}) collective-permute-start(bf16[2,384,384]{2,1,0:T(8,128)(2,1)S(1)} %slice.136), channel_id=1, source_target_pairs={{0,2},{1,3},{2,0},{3,1},{4,6},{5,7},{6,4},{7,5},{8,10},{9,11},{10,... | collective-permute-start | bytes 1769480 | tf_op jit(solution)/shard_map/ppermute | solution.py:652
  201.3 16.5 %collective-permute-start.28 = (bf16[2,4,48,384]{3,2,1,0:T(8,128)(2,1)S(1)}, bf16[2,4,48,384]{3,2,1,0:T(8,128)(2,1)S(1)}, u32[]{:S(2)}, u32[]{:S(2)}) collective-permute-start(bf16[2,4,48,384]{3,2,1,0:T(8,128)(2,1)S(1)} %fusion.1), channel_id=1, source_target_pairs={{0,16},{4,20},{8,24},{12,28},{16,0},{20,4},{24,8},{28,12},{1,17},{... | collective-permute-start | bytes 884744 | tf_op jit(solution)/shard_map/ppermute | solution.py:652
  201.9 15.9 %collective-permute-start.25 = (bf16[4,96,384]{2,1,0:T(8,128)(2,1)S(1)}, bf16[4,96,384]{2,1,0:T(8,128)(2,1)S(1)}, u32[]{:S(2)}, u32[]{:S(2)}) collective-permute-start(bf16[4,96,384]{2,1,0:T(8,128)(2,1)S(1)} %get-tuple-element.209), channel_id=1, source_target_pairs={{0,1},{1,0},{2,3},{3,2},{4,5},{5,4},{6,7},{7,6},{8,9},{9,8},{10,11... | collective-permute-start | bytes 884744 | tf_op jit(solution)/shard_map/ppermute | solution.py:652
  202.0 15.9 %collective-permute-start.26 = (bf16[4,96,384]{2,1,0:T(8,128)(2,1)S(1)}, bf16[4,96,384]{2,1,0:T(8,128)(2,1)S(1)}, u32[]{:S(2)}, u32[]{:S(2)}) collective-permute-start(bf16[4,96,384]{2,1,0:T(8,128)(2,1)S(1)} %get-tuple-element.210), channel_id=1, source_target_pairs={{0,2},{1,3},{2,0},{3,1},{4,6},{5,7},{6,4},{7,5},{8,10},{9,11},{10,... | collective-permute-start | bytes 884744 | tf_op jit(solution)/shard_map/ppermute | solution.py:652
  202.8 15.1 %collective-permute-start.27 = (bf16[4,96,384]{2,1,0:T(8,128)(2,1)S(1)}, bf16[4,96,384]{2,1,0:T(8,128)(2,1)S(1)}, u32[]{:S(2)}, u32[]{:S(2)}) collective-permute-start(bf16[4,96,384]{2,1,0:T(8,128)(2,1)S(1)} %get-tuple-element.211), channel_id=1, source_target_pairs={{0,3},{1,2},{2,1},{3,0},{4,7},{5,6},{6,5},{7,4},{8,11},{9,10},{10,... | collective-permute-start | bytes 884744 | tf_op jit(solution)/shard_map/ppermute | solution.py:652
  224.3 20.6 %all-to-all-start.1 = ((bf16[8,96,384]{2,1,0:T(8,128)(2,1)}), bf16[8,96,384]{2,1,0:T(8,128)(2,1)S(1)}, u32[]{:S(2)}, u32[]{:S(2)}) async-start(bf16[8,96,384]{2,1,0:T(8,128)(2,1)} %pad_maximum_fusion.2), calls=%async_computation.1 | async-start | bytes 1179648 | tf_op jit(solution)/shard_map/all_to_all | solution.py:684
  251.3 18.9 %all-to-all-start.2 = ((bf16[8,96,384]{2,1,0:T(8,128)(2,1)}), bf16[8,96,384]{2,1,0:T(8,128)(2,1)S(1)}, u32[]{:S(2)}, u32[]{:S(2)}) async-start(bf16[8,96,384]{2,1,0:T(8,128)(2,1)} %broadcast_in_dim.52), calls=%async_computation.2 | async-start | bytes 1179648 | tf_op jit(solution)/shard_map/all_to_all | solution.py:680
  256.0 10.6 %collective-permute-start.35 = (bf16[2,1,48,384]{3,2,1,0:T(8,128)(2,1)S(1)}, bf16[2,1,48,384]{3,2,1,0:T(8,128)(2,1)S(1)}, u32[]{:S(2)}, u32[]{:S(2)}) collective-permute-start(bf16[2,1,48,384]{3,2,1,0:T(8,128)(2,1)S(1)} %dynamic-slice_convert_fusion.2), channel_id=1, source_target_pairs={{0,8},{4,12},{8,0},{12,4},{16,24},{20,28},{24,16},{28,20},{1,9},{5... | collective-permute-start | bytes 221192 | tf_op jit(solution)/shard_map/ppermute | solution.py:652
  258.1 10.4 %collective-permute-start.37 = (bf16[2,1,48,384]{3,2,1,0:T(8,128)(2,1)S(1)}, bf16[2,1,48,384]{3,2,1,0:T(8,128)(2,1)S(1)}, u32[]{:S(2)}, u32[]{:S(2)}) collective-permute-start(bf16[2,1,48,384]{3,2,1,0:T(8,128)(2,1)S(1)} %dynamic-slice_convert_fusion.1), channel_id=1, source_target_pairs={{0,8},{4,12},{8,0},{12,4},{16,24},{20,28},{24,16},{28,20},{1,9},{5... | collective-permute-start | bytes 221192 | tf_op jit(solution)/shard_map/ppermute | solution.py:652
  (63 other events, 467.5 us)

commit v7 on v6

--- a/solution.py
+++ b/solution.py
@@ -727,13 +727,15 @@
 
 
 def fold_far(near, far, rows, size):
-    kept = near.astype(f32) + swap(far, "tensor", size, 1).astype(f32)
+    got = swap(far, "tensor", size, 1)
     bit = 2
     while bit < size // 2:
-        parts = kept.reshape(2, -1, 2, rows, D)
-        kept = (parts[:, :, 0] + swap(parts[:, :, 1].astype(bf16), "tensor", size, bit).astype(f32)).reshape(2, -1, D)
+        parts = (near.astype(f32) + got.astype(f32)).reshape(2, -1, 2, rows, D)
+        near, got = parts[:, :, 0].reshape(2, -1, D), swap(parts[:, :, 1].astype(bf16), "tensor", size, bit).reshape(2, -1, D)
         bit *= 2
-    return kept[:, :rows], kept[:, rows:].astype(bf16)
+    kept = near[:, :rows].astype(f32) + got[:, :rows].astype(f32)
+    sent = near[:, rows:].astype(f32) + got[:, rows:].astype(f32)
+    return kept, sent.astype(bf16)
 
 
 def own_block(rows, at, size, axis):

time: 276 us -> 273 us (0.989)
  no operation moved by 1% of the time
where the time goes in v7:
time: 273 us; the launch traced here: 270 us
  Pallas kernels  137 us (50%)
  starting transfers between devices  53.4 us (20%)
  waiting for transfers between devices  52.1 us (19%)
  local copies, waits for them, and re-layouts  14.1 us (5%)
  other arithmetic  11.7 us (4%)
    ppermute x38, waiting for transfers between devices, swap(): return lax.ppermute(rows, axis, [(i, i ^ bit) for i in range(size)])  51.8 us
    pallas_call x2, Pallas kernels, ffn_both(): call(lambda *refs: ffn_both_kernel(layer, with_output, pieces, len(weight...  39.8 us
    ppermute x38, starting transfers between devices, swap(): return lax.ppermute(rows, axis, [(i, i ^ bit) for i in range(size)])  39.1 us
    pallas_call x2, Pallas kernels, attn_forward(): call(lambda *refs: attn_fwd_kernel(layer, pieces, *refs), 'attn_fwd', ima...  36.3 us
    pallas_call x1, Pallas kernels, attn_backward(): call(lambda *refs: attn_bwd_kernel(layer, *refs), 'attn_bwd', images, [by...  28.7 us
    pallas_call x1, Pallas kernels, attn_backward_core(): call(lambda *refs: attn_core_kernel(layer, *refs), 'attn_core', images, [...  20.3 us
    all_to_all x2, starting transfers between devices, to_all(): lax.all_to_all(jnp.broadcast_to(rows[None], (size,) + rows.shape), axis,...  10.3 us
    pallas_call x1, Pallas kernels, ffn_forward(): call(lambda *refs: ffn_fwd_kernel(layer, len(weights), *refs), 'ffn_fwd',...  6.33 us
  transfers between devices with their start and end apart: 41, of which 16 were waited for; matrix products, arithmetic and copies ran while one was open for 5% of the time, Pallas kernels for 42%

profile of v7, /device:TPU:0, one launch (start us, length us, event | category | flops | bytes accessed | tf_op | source)
XLA Modules:
  0.0 270.2 jit_solution(11501919889101190715)
XLA Ops:
  2.0 3.0 %collective-permute-start.7 = (bf16[2,4,96,384]{3,2,1,0:T(8,128)(2,1)S(1)}, bf16[2,4,96,384]{3,2,1,0:T(8,128)(2,1)S(1)}, u32[]{:S(2)}, u32[]{:S(2)}) collective-permute-start(bf16[2,4,96,384]{3,2,1,0:T(8,128)(2,1)S(1)} %pad_maximum_fusion.refs_3_), channel_id=1, source_target_pairs={{0,2},{1,3},{2,0},{3,1},{4,6},{5,7},{6,4},{7,5},{8,10},{9,11},{10,... | collective-permute-start | bytes 1769480 | tf_op jit(solution)/shard_map/ppermute | solution.py:652
  5.1 2.7 collective-permute-start.2
  11.2 6.3 %all-to-all-start = ((bf16[8,2,48,384]{3,2,1,0:T(8,128)(2,1)}), bf16[8,2,48,384]{3,2,1,0:T(8,128)(2,1)S(1)}, u32[]{:S(2)}, u32[]{:S(2)}) async-start(bf16[8,2,48,384]{3,2,1,0:T(8,128)(2,1)} %broadcast_in_dim.51), calls=%async_computation | async-start | bytes 1179648 | tf_op jit(solution)/shard_map/all_to_all | solution.py:680
  23.2 5.2 %collective-permute-done.1 = bf16[8,2304]{1,0:T(8,128)(2,1)S(1)} collective-permute-done((bf16[8,2304]{1,0:T(8,128)(2,1)S(1)}, bf16[8,2304]{1,0:T(8,128)(2,1)S(1)}, u32[]{:S(2)}, u32[]{:S(2)}) %collective-permute-start.1) | collective-permute-done | bytes 36896 | tf_op jit(solution)/shard_map/ppermute | solution.py:652
  28.4 2.5 collective-permute-start.4
  36.7 3.8 %collective-permute-done.5 = bf16[8,2304]{1,0:T(8,128)(2,1)S(1)} collective-permute-done((bf16[8,2304]{1,0:T(8,128)(2,1)S(1)}, bf16[8,2304]{1,0:T(8,128)(2,1)S(1)}, u32[]{:S(2)}, u32[]{:S(2)}) %collective-permute-start.5) | collective-permute-done | bytes 36896 | tf_op jit(solution)/shard_map/ppermute | solution.py:652
  42.7 17.7 %attn_fwd.2 = (f32[1568,384]{1,0:T(8,128)}, bf16[2048,384]{1,0:T(8,128)(2,1)}, bf16[2048,1152]{1,0:T(8,128)(2,1)}, bf16[2,8,3,128,512]{4,3,2,1,0:T(8,128)(2,1)},...) custom-call(bf16[1568,384]{1,0:T(8,128)(2,1)} %refs_1_.3, f32[8,2304]{1,0:T(8,128)} %add_convert_fusion.4.refs_1_.refs_2_, ...), custom_call_target="tpu_custom_call" | custom-call | flops 100000000 | bytes 100000 | tf_op jit(solution)/shard_map/attn_fwd/pallas_call | solution.py:505
  63.0 6.3 %ffn_fwd.1 = (f32[1568,384]{1,0:T(8,128)S(1)}, bf16[2,1536,384]{2,1,0:T(8,128)(2,1)S(1)}) custom-call(f32[1568,384]{1,0:T(8,128)S(1)} %copy-done.2, f32[8,2304]{1,0:T(8,128)S(1)} %copy-done.6, bf16[8,2,48,384]{3,2,1,0:T(8,128)(2,1)S(1)} %all-to-all-done.refs_2_, bf16[8,2,48,384]{3,2,1,0:T(8,128)(2,1)S(1)} %collective-permute-done.10.refs_3_, ...), custom_call_target="tpu_custom_call" | custom-call | flops 100000000 | bytes 100000 | tf_op jit(solution)/shard_map/ffn_fwd/pallas_call | solution.py:590
  72.3 18.6 %attn_fwd.3 = (f32[1568,384]{1,0:T(8,128)}, bf16[2048,384]{1,0:T(8,128)(2,1)}, bf16[2048,1152]{1,0:T(8,128)(2,1)}, bf16[2,8,3,128,512]{4,3,2,1,0:T(8,128)(2,1)},...) custom-call(f32[1568,384]{1,0:T(8,128)} %copy-done.3, f32[8,2304]{1,0:T(8,128)} %add_convert_fusion.4.refs_1_.refs_2_, ...), custom_call_target="tpu_custom_call" | custom-call | flops 100000000 | bytes 100000 | tf_op jit(solution)/shard_map/attn_fwd/pallas_call | solution.py:505
  93.9 23.3 %ffn_both_out.1 = (f32[1568,384]{1,0:T(8,128)}, bf16[2,768,384]{2,1,0:T(8,128)(2,1)}, bf16[2,768,384]{2,1,0:T(8,128)(2,1)}, f32[8,2304]{1,0:T(8,128)}, bf16[1568,384]{1,0:T(8,128)(2,1)}, /*index=5*/f32[2,1,384]{2,1,0:T(1,128)}) custom-call(f32[1568,384]{1,0:T(8,128)} %get-tuple-element.155.refs_0_, bf16[1568,384]{1,0:T(8,128)(2,1)} %refs_1_.2, ...), custom_call_target="tpu_custom_call" | custom-call | flops 100000000 | bytes 100000 | tf_op jit(solution)/shard_map/ffn_both_out/pallas_call | solution.py:623
  117.4 3.1 %collective-permute-done.17 = bf16[2,768,384]{2,1,0:T(8,128)(2,1)} collective-permute-done((bf16[2,768,384]{2,1,0:T(8,128)(2,1)}, bf16[2,768,384]{2,1,0:T(8,128)(2,1)}, u32[]{:S(2)}, u32[]{:S(2)}) %collective-permute-start.17) | collective-permute-done | bytes 1179680 | tf_op jit(solution)/shard_map/ppermute | solution.py:652
  123.1 28.7 %attn_bwd.1 = (f32[1568,384]{1,0:T(8,128)}, bf16[4,96,384]{2,1,0:T(8,128)(2,1)}, bf16[4,96,384]{2,1,0:T(8,128)(2,1)}, bf16[4,96,384]{2,1,0:T(8,128)(2,1)}, bf16[...) custom-call(f32[1568,384]{1,0:T(8,128)} %get-tuple-element.167.refs_0_, f32[1568,384]{1,0:T(8,128)} %copy-done.3, ...), custom_call_target="tpu_custom_call" | custom-call | flops 100000000 | bytes 100000 | tf_op jit(solution)/shard_map/attn_bwd/pallas_call | solution.py:530
  157.9 16.4 %ffn_both.1 = (f32[1568,384]{1,0:T(8,128)S(1)}, bf16[2,768,384]{2,1,0:T(8,128)(2,1)S(1)}, bf16[2,768,384]{2,1,0:T(8,128)(2,1)S(1)}, f32[8,2304]{1,0:T(8,128)S(1)}) custom-call(f32[1568,384]{1,0:T(8,128)S(1)} %copy-done.2, f32[1568,384]{1,0:T(8,128)S(1)} %copy-done.8, f32[8,2304]{1,0:T(8,128)S(1)} %copy-done.7, s32[1]{0:T(128)} %bitcast.20.refs_7_.refs_6_.refs_3_.refs_8_, ...), custom_call_target="tpu_custom_call" | custom-call | flops 100000000 | bytes 100000 | tf_op jit(solution)/shard_map/ffn_both/pallas_call | solution.py:623
  174.9 2.5 collective-permute-done.23
  178.4 20.3 %attn_core.1 = (bf16[2048,1152]{1,0:T(8,128)(2,1)S(1)}, bf16[4,96,384]{2,1,0:T(8,128)(2,1)S(1)}, bf16[4,96,384]{2,1,0:T(8,128)(2,1)S(1)}, bf16[4,96,384]{2,1,0:T...) custom-call(f32[1568,384]{1,0:T(8,128)S(1)} %get-tuple-element.193.refs_0_, ...), custom_call_target="tpu_custom_call" | custom-call | flops 100000000 | bytes 100000 | tf_op jit(solution)/shard_map/attn_core/pallas_call | solution.py:553
  201.4 5.5 %attn_norm.1 = (f32[1568,384]{1,0:T(8,128)}, f32[8,2304]{1,0:T(8,128)S(1)}) custom-call(f32[1568,384]{1,0:T(8,128)S(1)} %get-tuple-element.193.refs_0_, bf16[1568,384]{1,0:T(8,128)(2,1)S(1)} %copy-done.4, f32[8,2304]{1,0:T(8,128)S(1)} %copy-done.7, bf16[4,384,384]{2,1,0:T(8,128)(2,1)S(1)} %copy-done.5, bf16[2048,1152]{1,0:T(8,128)(2,1)S(1)} %get-tuple-element.206.refs_4_), custom_call_target="tpu_custom_call" | custom-call | flops 100000000 | bytes 100000 | tf_op jit(solution)/shard_map/attn_norm/pallas_call | solution.py:569
  206.9 8.3 %collective-permute-done.28 = bf16[2,4,48,384]{3,2,1,0:T(8,128)(2,1)S(1)} collective-permute-done((bf16[2,4,48,384]{3,2,1,0:T(8,128)(2,1)S(1)}, bf16[2,4,48,384]{3,2,1,0:T(8,128)(2,1)S(1)}, u32[]{:S(2)}, u32[]{:S(2)}) %collective-permute-start.28) | collective-permute-done | bytes 294944 | tf_op jit(solution)/shard_map/ppermute | solution.py:652
  218.7 3.3 %collective-permute-done.29 = f32[8,2304]{1,0:T(8,128)S(1)} collective-permute-done((f32[8,2304]{1,0:T(8,128)S(1)}, f32[8,2304]{1,0:T(8,128)S(1)}, u32[]{:S(2)}, u32[]{:S(2)}) %collective-permute-start.29) | collective-permute-done | bytes 73760 | tf_op jit(solution)/shard_map/ppermute | solution.py:652
  222.0 3.9 %all-to-all-start.1 = ((bf16[8,96,384]{2,1,0:T(8,128)(2,1)}), bf16[8,96,384]{2,1,0:T(8,128)(2,1)S(1)}, u32[]{:S(2)}, u32[]{:S(2)}) async-start(bf16[8,96,384]{2,1,0:T(8,128)(2,1)} %pad_maximum_fusion.2), calls=%async_computation.1 | async-start | bytes 1179648 | tf_op jit(solution)/shard_map/all_to_all | solution.py:684
  229.0 2.6 collective-permute-done.31
  236.1 3.0 %collective-permute-start.33 = (f32[8,2304]{1,0:T(8,128)S(1)}, f32[8,2304]{1,0:T(8,128)S(1)}, u32[]{:S(2)}, u32[]{:S(2)}) collective-permute-start(f32[8,2304]{1,0:T(8,128)S(1)} %add.269), channel_id=1, source_target_pairs={{0,8},{4,12},{8,0},{12,4},{16,24},{20,28},{24,16},{28,20},{1,9},{5... | collective-permute-start | bytes 221192 | tf_op jit(solution)/shard_map/ppermute | solution.py:652
  239.1 3.5 %collective-permute-done.33 = f32[8,2304]{1,0:T(8,128)S(1)} collective-permute-done((f32[8,2304]{1,0:T(8,128)S(1)}, f32[8,2304]{1,0:T(8,128)S(1)}, u32[]{:S(2)}, u32[]{:S(2)}) %collective-permute-start.33) | collective-permute-done | bytes 73760 | tf_op jit(solution)/shard_map/ppermute | solution.py:652
  249.0 4.0 %all-to-all-start.2 = ((bf16[8,96,384]{2,1,0:T(8,128)(2,1)}), bf16[8,96,384]{2,1,0:T(8,128)(2,1)S(1)}, u32[]{:S(2)}, u32[]{:S(2)}) async-start(bf16[8,96,384]{2,1,0:T(8,128)(2,1)} %broadcast_in_dim.52), calls=%async_computation.2 | async-start | bytes 1179648 | tf_op jit(solution)/shard_map/all_to_all | solution.py:680
  255.9 8.4 %collective-permute-done.35 = bf16[2,1,48,384]{3,2,1,0:T(8,128)(2,1)S(1)} collective-permute-done((bf16[2,1,48,384]{3,2,1,0:T(8,128)(2,1)S(1)}, bf16[2,1,48,384]{3,2,1,0:T(8,128)(2,1)S(1)}, u32[]{:S(2)}, u32[]{:S(2)}) %collective-permute-start.35) | collective-permute-done | bytes 73760 | tf_op jit(solution)/shard_map/ppermute | solution.py:652
  (239 shorter events, 65.2 us)
Async XLA Ops:
  2.0 21.1 %collective-permute-start.7 = (bf16[2,4,96,384]{3,2,1,0:T(8,128)(2,1)S(1)}, bf16[2,4,96,384]{3,2,1,0:T(8,128)(2,1)S(1)}, u32[]{:S(2)}, u32[]{:S(2)}) collective-permute-start(bf16[2,4,96,384]{3,2,1,0:T(8,128)(2,1)S(1)} %pad_maximum_fusion.refs_3_), channel_id=1, source_target_pairs={{0,2},{1,3},{2,0},{3,1},{4,6},{5,7},{6,4},{7,5},{8,10},{9,11},{10,... | collective-permute-start | bytes 1769480 | tf_op jit(solution)/shard_map/ppermute | solution.py:652
  5.0 35.5 %collective-permute-start.6 = (bf16[2,4,96,384]{3,2,1,0:T(8,128)(2,1)S(1)}, bf16[2,4,96,384]{3,2,1,0:T(8,128)(2,1)S(1)}, u32[]{:S(2)}, u32[]{:S(2)}) collective-permute-start(bf16[2,4,96,384]{3,2,1,0:T(8,128)(2,1)S(1)} %pad_maximum_fusion.refs_3_), channel_id=1, source_target_pairs={{0,1},{1,0},{2,3},{3,2},{4,5},{5,4},{6,7},{7,6},{8,9},{9,8},{10,11... | collective-permute-start | bytes 1769480 | tf_op jit(solution)/shard_map/ppermute | solution.py:652
  5.1 18.0 %collective-permute-start.2 = (bf16[1,2,48,384]{3,2,1,0:T(8,128)(2,1)S(1)}, bf16[1,2,48,384]{3,2,1,0:T(8,128)(2,1)S(1)}, u32[]{:S(2)}, u32[]{:S(2)}) collective-permute-start(bf16[1,2,48,384]{3,2,1,0:T(8,128)(2,1)S(1)} %get-tuple-element.272), channel_id=1, source_target_pairs={{0,16},{4,20},{8,24},{12,28},{16,0},{20,4},{24,8},{28,12},{1,17},{... | collective-permute-start | bytes 221192 | tf_op jit(solution)/shard_map/ppermute | solution.py:652
  11.2 29.3 %all-to-all-start = ((bf16[8,2,48,384]{3,2,1,0:T(8,128)(2,1)}), bf16[8,2,48,384]{3,2,1,0:T(8,128)(2,1)S(1)}, u32[]{:S(2)}, u32[]{:S(2)}) async-start(bf16[8,2,48,384]{3,2,1,0:T(8,128)(2,1)} %broadcast_in_dim.51), calls=%async_computation | async-start | bytes 1179648 | tf_op jit(solution)/shard_map/all_to_all | solution.py:680
  23.1 17.5 %collective-permute-start.8 = (bf16[2,4,96,384]{3,2,1,0:T(8,128)(2,1)S(1)}, bf16[2,4,96,384]{3,2,1,0:T(8,128)(2,1)S(1)}, u32[]{:S(2)}, u32[]{:S(2)}) collective-permute-start(bf16[2,4,96,384]{3,2,1,0:T(8,128)(2,1)S(1)} %collective-permute-done.7.refs_5_), channel_id=1, source_target_pairs={{0,1},{1,0},{2,3},{3,2},{4,5},{5,4},{6,7},{7,6},{8,9},{9,8},{10,11... | collective-permute-start | bytes 1769480 | tf_op jit(solution)/shard_map/ppermute | solution.py:652
  40.6 19.8 %collective-permute-start.12 = (bf16[4,2,48,384]{3,2,1,0:T(8,128)(2,1)S(1)}, bf16[4,2,48,384]{3,2,1,0:T(8,128)(2,1)S(1)}, u32[]{:S(2)}, u32[]{:S(2)}) collective-permute-start(bf16[4,2,48,384]{3,2,1,0:T(8,128)(2,1)S(1)} %bitcast.118), channel_id=1, source_target_pairs={{0,4},{4,0},{8,12},{12,8},{16,20},{20,16},{24,28},{28,24},{1,5},{5... | collective-permute-start | bytes 884744 | tf_op jit(solution)/shard_map/ppermute | solution.py:652
  41.6 18.9 %collective-permute-start.10 = (bf16[8,2,48,384]{3,2,1,0:T(8,128)(2,1)S(1)}, bf16[8,2,48,384]{3,2,1,0:T(8,128)(2,1)S(1)}, u32[]{:S(2)}, u32[]{:S(2)}) collective-permute-start(bf16[8,2,48,384]{3,2,1,0:T(8,128)(2,1)S(1)} %all-to-all-done.refs_2_), channel_id=1, source_target_pairs={{0,1},{1,0},{2,3},{3,2},{4,5},{5,4},{6,7},{7,6},{8,9},{9,8},{10,11... | collective-permute-start | bytes 1769480 | tf_op jit(solution)/shard_map/ppermute | solution.py:652
  41.7 18.7 %collective-permute-start.11 = (bf16[8,2,48,384]{3,2,1,0:T(8,128)(2,1)S(1)}, bf16[8,2,48,384]{3,2,1,0:T(8,128)(2,1)S(1)}, u32[]{:S(2)}, u32[]{:S(2)}) collective-permute-start(bf16[8,2,48,384]{3,2,1,0:T(8,128)(2,1)S(1)} %all-to-all-done.refs_2_), channel_id=1, source_target_pairs={{0,2},{1,3},{2,0},{3,1},{4,6},{5,7},{6,4},{7,5},{8,10},{9,11},{10,... | collective-permute-start | bytes 1769480 | tf_op jit(solution)/shard_map/ppermute | solution.py:652
  60.8 30.1 %collective-permute-start.14 = (bf16[8,2,48,384]{3,2,1,0:T(8,128)(2,1)S(1)}, bf16[8,2,48,384]{3,2,1,0:T(8,128)(2,1)S(1)}, u32[]{:S(2)}, u32[]{:S(2)}) collective-permute-start(bf16[8,2,48,384]{3,2,1,0:T(8,128)(2,1)S(1)} %bitcast.110), channel_id=1, source_target_pairs={{0,1},{1,0},{2,3},{3,2},{4,5},{5,4},{6,7},{7,6},{8,9},{9,8},{10,11... | collective-permute-start | bytes 1769480 | tf_op jit(solution)/shard_map/ppermute | solution.py:652
  61.3 29.6 %collective-permute-start.15 = (bf16[8,2,48,384]{3,2,1,0:T(8,128)(2,1)S(1)}, bf16[8,2,48,384]{3,2,1,0:T(8,128)(2,1)S(1)}, u32[]{:S(2)}, u32[]{:S(2)}) collective-permute-start(bf16[8,2,48,384]{3,2,1,0:T(8,128)(2,1)S(1)} %bitcast.111), channel_id=1, source_target_pairs={{0,2},{1,3},{2,0},{3,1},{4,6},{5,7},{6,4},{7,5},{8,10},{9,11},{10,... | collective-permute-start | bytes 1769480 | tf_op jit(solution)/shard_map/ppermute | solution.py:652
  121.8 30.0 %collective-permute-start.18 = (bf16[2,384,384]{2,1,0:T(8,128)(2,1)S(1)}, bf16[2,384,384]{2,1,0:T(8,128)(2,1)}, u32[]{:S(2)}, u32[]{:S(2)}) collective-permute-start(bf16[2,384,384]{2,1,0:T(8,128)(2,1)S(1)} %add_convert_fusion.1), channel_id=1, source_target_pairs={{0,2},{1,3},{2,0},{3,1},{4,6},{5,7},{6,4},{7,5},{8,10},{9,11},{10,... | collective-permute-start | bytes 1769480 | tf_op jit(solution)/shard_map/ppermute | solution.py:652
  153.6 20.8 %collective-permute-start.22 = (bf16[2,4,48,384]{3,2,1,0:T(8,128)(2,1)S(1)}, bf16[2,4,48,384]{3,2,1,0:T(8,128)(2,1)S(1)}, u32[]{:S(2)}, u32[]{:S(2)}) collective-permute-start(bf16[2,4,48,384]{3,2,1,0:T(8,128)(2,1)S(1)} %fusion), channel_id=1, source_target_pairs={{0,16},{4,20},{8,24},{12,28},{16,0},{20,4},{24,8},{28,12},{1,17},{... | collective-permute-start | bytes 884744 | tf_op jit(solution)/shard_map/ppermute | solution.py:652
  156.0 18.4 %collective-permute-start.19 = (bf16[4,96,384]{2,1,0:T(8,128)(2,1)S(1)}, bf16[4,96,384]{2,1,0:T(8,128)(2,1)S(1)}, u32[]{:S(2)}, u32[]{:S(2)}) collective-permute-start(bf16[4,96,384]{2,1,0:T(8,128)(2,1)S(1)} %copy-done.45), channel_id=1, source_target_pairs={{0,1},{1,0},{2,3},{3,2},{4,5},{5,4},{6,7},{7,6},{8,9},{9,8},{10,11... | collective-permute-start | bytes 884744 | tf_op jit(solution)/shard_map/ppermute | solution.py:652
  156.0 18.4 %collective-permute-start.20 = (bf16[4,96,384]{2,1,0:T(8,128)(2,1)S(1)}, bf16[4,96,384]{2,1,0:T(8,128)(2,1)S(1)}, u32[]{:S(2)}, u32[]{:S(2)}) collective-permute-start(bf16[4,96,384]{2,1,0:T(8,128)(2,1)S(1)} %copy-done.44), channel_id=1, source_target_pairs={{0,2},{1,3},{2,0},{3,1},{4,6},{5,7},{6,4},{7,5},{8,10},{9,11},{10,... | collective-permute-start | bytes 884744 | tf_op jit(solution)/shard_map/ppermute | solution.py:652
  156.9 17.5 %collective-permute-start.21 = (bf16[4,96,384]{2,1,0:T(8,128)(2,1)S(1)}, bf16[4,96,384]{2,1,0:T(8,128)(2,1)S(1)}, u32[]{:S(2)}, u32[]{:S(2)}) collective-permute-start(bf16[4,96,384]{2,1,0:T(8,128)(2,1)S(1)} %copy-done.43), channel_id=1, source_target_pairs={{0,3},{1,2},{2,1},{3,0},{4,7},{5,6},{6,5},{7,4},{8,11},{9,10},{10,... | collective-permute-start | bytes 884744 | tf_op jit(solution)/shard_map/ppermute | solution.py:652
  177.5 21.2 %collective-permute-start.24 = (bf16[2,384,384]{2,1,0:T(8,128)(2,1)S(1)}, bf16[2,384,384]{2,1,0:T(8,128)(2,1)S(1)}, u32[]{:S(2)}, u32[]{:S(2)}) collective-permute-start(bf16[2,384,384]{2,1,0:T(8,128)(2,1)S(1)} %add_convert_fusion), channel_id=1, source_target_pairs={{0,2},{1,3},{2,0},{3,1},{4,6},{5,7},{6,4},{7,5},{8,10},{9,11},{10,... | collective-permute-start | bytes 1769480 | tf_op jit(solution)/shard_map/ppermute | solution.py:652
  199.0 16.3 %collective-permute-start.28 = (bf16[2,4,48,384]{3,2,1,0:T(8,128)(2,1)S(1)}, bf16[2,4,48,384]{3,2,1,0:T(8,128)(2,1)S(1)}, u32[]{:S(2)}, u32[]{:S(2)}) collective-permute-start(bf16[2,4,48,384]{3,2,1,0:T(8,128)(2,1)S(1)} %fusion.1), channel_id=1, source_target_pairs={{0,16},{4,20},{8,24},{12,28},{16,0},{20,4},{24,8},{28,12},{1,17},{... | collective-permute-start | bytes 884744 | tf_op jit(solution)/shard_map/ppermute | solution.py:652
  199.6 15.7 %collective-permute-start.25 = (bf16[4,96,384]{2,1,0:T(8,128)(2,1)S(1)}, bf16[4,96,384]{2,1,0:T(8,128)(2,1)S(1)}, u32[]{:S(2)}, u32[]{:S(2)}) collective-permute-start(bf16[4,96,384]{2,1,0:T(8,128)(2,1)S(1)} %get-tuple-element.209), channel_id=1, source_target_pairs={{0,1},{1,0},{2,3},{3,2},{4,5},{5,4},{6,7},{7,6},{8,9},{9,8},{10,11... | collective-permute-start | bytes 884744 | tf_op jit(solution)/shard_map/ppermute | solution.py:652
  199.6 15.7 %collective-permute-start.26 = (bf16[4,96,384]{2,1,0:T(8,128)(2,1)S(1)}, bf16[4,96,384]{2,1,0:T(8,128)(2,1)S(1)}, u32[]{:S(2)}, u32[]{:S(2)}) collective-permute-start(bf16[4,96,384]{2,1,0:T(8,128)(2,1)S(1)} %get-tuple-element.210), channel_id=1, source_target_pairs={{0,2},{1,3},{2,0},{3,1},{4,6},{5,7},{6,4},{7,5},{8,10},{9,11},{10,... | collective-permute-start | bytes 884744 | tf_op jit(solution)/shard_map/ppermute | solution.py:652
  200.8 14.5 %collective-permute-start.27 = (bf16[4,96,384]{2,1,0:T(8,128)(2,1)S(1)}, bf16[4,96,384]{2,1,0:T(8,128)(2,1)S(1)}, u32[]{:S(2)}, u32[]{:S(2)}) collective-permute-start(bf16[4,96,384]{2,1,0:T(8,128)(2,1)S(1)} %get-tuple-element.211), channel_id=1, source_target_pairs={{0,3},{1,2},{2,1},{3,0},{4,7},{5,6},{6,5},{7,4},{8,11},{9,10},{10,... | collective-permute-start | bytes 884744 | tf_op jit(solution)/shard_map/ppermute | solution.py:652
  222.0 20.6 %all-to-all-start.1 = ((bf16[8,96,384]{2,1,0:T(8,128)(2,1)}), bf16[8,96,384]{2,1,0:T(8,128)(2,1)S(1)}, u32[]{:S(2)}, u32[]{:S(2)}) async-start(bf16[8,96,384]{2,1,0:T(8,128)(2,1)} %pad_maximum_fusion.2), calls=%async_computation.1 | async-start | bytes 1179648 | tf_op jit(solution)/shard_map/all_to_all | solution.py:684
  249.0 18.9 %all-to-all-start.2 = ((bf16[8,96,384]{2,1,0:T(8,128)(2,1)}), bf16[8,96,384]{2,1,0:T(8,128)(2,1)S(1)}, u32[]{:S(2)}, u32[]{:S(2)}) async-start(bf16[8,96,384]{2,1,0:T(8,128)(2,1)} %broadcast_in_dim.52), calls=%async_computation.2 | async-start | bytes 1179648 | tf_op jit(solution)/shard_map/all_to_all | solution.py:680
  253.7 10.6 %collective-permute-start.35 = (bf16[2,1,48,384]{3,2,1,0:T(8,128)(2,1)S(1)}, bf16[2,1,48,384]{3,2,1,0:T(8,128)(2,1)S(1)}, u32[]{:S(2)}, u32[]{:S(2)}) collective-permute-start(bf16[2,1,48,384]{3,2,1,0:T(8,128)(2,1)S(1)} %dynamic-slice_convert_fusion.2), channel_id=1, source_target_pairs={{0,8},{4,12},{8,0},{12,4},{16,24},{20,28},{24,16},{28,20},{1,9},{5... | collective-permute-start | bytes 221192 | tf_op jit(solution)/shard_map/ppermute | solution.py:652
  255.8 10.4 %collective-permute-start.37 = (bf16[2,1,48,384]{3,2,1,0:T(8,128)(2,1)S(1)}, bf16[2,1,48,384]{3,2,1,0:T(8,128)(2,1)S(1)}, u32[]{:S(2)}, u32[]{:S(2)}) collective-permute-start(bf16[2,1,48,384]{3,2,1,0:T(8,128)(2,1)S(1)} %dynamic-slice_convert_fusion.1), channel_id=1, source_target_pairs={{0,8},{4,12},{8,0},{12,4},{16,24},{20,28},{24,16},{28,20},{1,9},{5... | collective-permute-start | bytes 221192 | tf_op jit(solution)/shard_map/ppermute | solution.py:652
  (63 other events, 522.8 us)
